TPU v7x, 32 devices: a whole 2x2x4 slice. The times are simulated.
32 devices in a mesh: dp: 2 (over core), cp: 8 (over z, x), hd: 2 (over y).
Axes of the slice: x: 2, y: 2, z: 4, core: 2. Of those that a mesh axis runs over, the one named last changes fastest.
Arguments:
- tokens: bfloat16 [2, 5120, 1024], P('dp', ('cp', 'hd')), may hold values from -6 to 6
- doc_ids: int32 [2, 5120], P('dp'), may hold values from 0 to 2, as said below
- cotangent: bfloat16 [2, 5120, 1024], P('dp', ('cp', 'hd')), may hold values from -6 to 6
- w_in: bfloat16 [1024, 4096], P(('dp', 'cp')), may hold values from -0.1875 to 0.1875
- w_dt: bfloat16 [1024, 24], P(('dp', 'cp')), may hold values from -0.1875 to 0.1875
- w_mo: bfloat16 [1536, 1024], P(('dp', 'cp')), may hold values from -0.15625 to 0.15625
- w_ao: bfloat16 [512, 1024], P(('dp', 'cp')), may hold values from -4 to 4
- w_gu: bfloat16 [1024, 4096], P(('dp', 'cp')), may hold values from -0.1875 to 0.1875
- w_down: bfloat16 [2048, 1024], P(('dp', 'cp')), may hold values from -0.125 to 0.125
- norm1: float32 [1024], replicated, may hold values from 0.5 to 1.5
- norm2: float32 [1024], replicated, may hold values from 0.5 to 1.5
- gate_norm: float32 [1536], replicated, may hold values from 0.5 to 1.5
- conv_w: float32 [4, 1792], replicated, may hold values from -3 to 3
- conv_b: float32 [1792], replicated, may hold values from -2 to 2
- dt_bias: float32 [24], replicated, may hold values from -3 to -1
- a_log: float32 [24], replicated
- d_skip: float32 [24], replicated, may hold values from 0.5 to 1.5
Outputs:
- out: bfloat16 [2, 5120, 1024], P('dp', ('cp', 'hd'))
- d_tokens: bfloat16 [2, 5120, 1024], P('dp', ('cp', 'hd'))
- g_w_in: float32 [1024, 4096], P(('dp', 'cp', 'hd'))
- g_w_dt: float32 [1024, 24], P(('dp', 'cp', 'hd'))
- g_w_mo: float32 [1536, 1024], P(('dp', 'cp', 'hd'))
- g_w_ao: float32 [512, 1024], P(('dp', 'cp', 'hd'))
- g_w_gu: float32 [1024, 4096], P(('dp', 'cp', 'hd'))
- g_w_down: float32 [2048, 1024], P(('dp', 'cp', 'hd'))
- g_norm1: float32 [1024], replicated
- g_norm2: float32 [1024], replicated
- g_gate_norm: float32 [1536], replicated
- g_conv_w: float32 [4, 1792], replicated
- g_conv_b: float32 [1792], replicated
- g_dt_bias: float32 [24], replicated
- g_a_log: float32 [24], replicated
- g_d_skip: float32 [24], replicated
Inputs may be any that keep to these rules, and one draw needn't show every extreme that they name: `doc_ids`: in each sequence the document numbers are 0, 1, 2 in order and never fall; document 0 ends within the first 640 positions and document 2 begins within the last 640 positions.
All inputs are finite; a program needn't handle non-finite values.
Results may differ from a plain program's by a relative error of at most 0.015.
Values may be sent and summed in bfloat16 or wider, within the bound.
No kernel may reach another device: no remote copies, remote signals or barrier semaphores. Data moves between devices by JAX's collectives and lax.ppermute only.
A program may use at most 256 MiB of HBM per device.

v0:
```python
import math

import jax
import jax.numpy as jnp
from jax import lax
from jax.sharding import PartitionSpec as P

HM = 24
HDIM = 64
NST = 128
QH = 8
KVH = 2
FF = 2048


eps_norm = 1e-05
rope_base = 100000000000.0
masked = -1e30
highest = lax.Precision.HIGHEST


def shifted(value, axis, steps):
    count = lax.axis_size(axis)
    initial, last = (max(0, -steps), min(count, count - steps))
    return lax.ppermute(value, axis, [(source, source + steps) for source in range(initial, last)])


def prefix(x, axis, join, neutral):
    place = lax.axis_index(axis)
    gathered = jax.tree.map(
        lambda a, kind: lax.all_gather(a.astype(kind), axis), x, (jnp.bfloat16, jnp.bfloat16)
    )
    state = jax.tree.map(lambda a, e: jnp.zeros_like(a) + jnp.asarray(e, a.dtype), x, neutral)

    def prefix_one(turn, state):
        return join(
            state,
            jax.tree.map(
                lambda a, own: lax.dynamic_index_in_dim(a, turn, 0, False).astype(own.dtype),
                gathered,
                x,
            ),
        )

    return lax.fori_loop(0, place, prefix_one, state)


def entering_2(x, axis, join, neutral):
    count = lax.axis_size(axis)
    place = lax.axis_index(axis)
    ahead = count - 1 - place
    gathered = jax.tree.map(
        lambda a, kind: lax.all_gather(a.astype(kind), axis),
        x,
        jax.tree.map(lambda a: jnp.bfloat16 if a.dtype == jnp.float32 else a.dtype, x),
    )
    state = jax.tree.map(lambda a, e: jnp.zeros_like(a) + jnp.asarray(e, a.dtype), x, neutral)

    def entering_one(turn, state):
        source = count - 1 - turn
        return join(
            state,
            jax.tree.map(
                lambda a, own: lax.dynamic_index_in_dim(a, source, 0, False).astype(own.dtype),
                gathered,
                x,
            ),
        )

    return lax.fori_loop(0, ahead, entering_one, state)


def rms_norm(values, gain_vec):
    return (
        values * lax.rsqrt(jnp.mean(values * values, axis=-1, keepdims=True) + eps_norm) * gain_vec
    )


def rotate(values, positions):
    half_width = values.shape[-1] // 2
    frequency = rope_base ** (-2.0 * jnp.arange(half_width, dtype=jnp.float32) / values.shape[-1])
    angles = positions.astype(jnp.float32)[:, None] * frequency[None, :]
    cosines = jnp.cos(angles)[:, None, :]
    sines = jnp.sin(angles)[:, None, :]
    first_half = values[..., :half_width]
    second_half = values[..., half_width:]
    return jnp.concatenate(
        [first_half * cosines - second_half * sines, second_half * cosines + first_half * sines],
        axis=-1,
    )


def causal_conv(padded, conv_taps, conv_shift):
    tap_count = conv_taps.shape[0]
    out_rows = padded.shape[0] - tap_count + 1
    summed = conv_shift[None, :]
    for tap_index in range(tap_count):
        summed = summed + conv_taps[tap_index][None, :] * padded[tap_index : tap_index + out_rows]
    return summed


def chain_states(earlier, later):
    return (earlier[0] * later[0], later[0][:, None, None] * earlier[1] + later[1])


def ssd_state(x_conv, b_conv, dt_value, decay_rate):
    cum_decay = jnp.cumsum(dt_value * decay_rate[None, :], axis=0)
    weights = jnp.exp(cum_decay[-1:, :] - cum_decay) * dt_value
    return (jnp.einsum("lh,lhp,ln->hpn", weights, x_conv, b_conv, precision=highest), cum_decay[-1])


def ssd_out(x_conv, b_conv, c_conv, dt_value, decay_rate, skip_gain, entering):
    length, head_count, head_width = x_conv.shape
    block_len = math.gcd(256, length)
    blocks = length // block_len
    lower_mask = (jnp.arange(block_len)[:, None] >= jnp.arange(block_len)[None, :])[
        None, :, :, None
    ]
    x_block = x_conv.reshape(blocks, block_len, head_count, head_width)
    b_block = b_conv.reshape(blocks, block_len, -1)
    c_block = c_conv.reshape(blocks, block_len, -1)
    dt_block = dt_value.reshape(blocks, block_len, head_count)
    cum_decay = jnp.cumsum(dt_block * decay_rate[None, None, :], axis=1)
    spread = jnp.where(lower_mask, cum_decay[:, :, None, :] - cum_decay[:, None, :, :], 0.0)
    decays = jnp.where(lower_mask, jnp.exp(spread), 0.0)
    inner_prod = jnp.einsum("btn,bsn->bts", c_block, b_block, precision=highest)
    mixing = decays * inner_prod[..., None] * dt_block[:, None, :, :]
    within = jnp.einsum("btsh,bshp->bthp", mixing, x_block, precision=highest)
    end_weight = jnp.exp(cum_decay[:, -1:, :] - cum_decay) * dt_block
    local_states = jnp.einsum("bsh,bshp,bsn->bhpn", end_weight, x_block, b_block, precision=highest)
    block_fall = jnp.exp(cum_decay[:, -1, :])

    def advance(carried, block_item):
        return (block_item[1][:, None, None] * carried + block_item[0], carried)

    _, before = lax.scan(advance, entering, (local_states, block_fall))
    from_state = jnp.exp(cum_decay)[..., None] * jnp.einsum(
        "btn,bhpn->bthp", c_block, before, precision=highest
    )
    result = within + from_state + skip_gain[None, None, :, None] * x_block
    return result.reshape(length, head_count, head_width)


def t_dot(left, right):
    return lax.dot_general(
        left, right, (((0,), (0,)), ((), ())), preferred_element_type=jnp.float32
    )


def dot_t(left, right):
    return lax.dot_general(
        left, right, (((1,), (1,)), ((), ())), preferred_element_type=jnp.float32
    )


def per_device(
    tokens,
    doc_ids,
    cotangent,
    w_in,
    w_dt,
    w_mo,
    w_ao,
    w_gu,
    w_down,
    norm1,
    norm2,
    gate_norm,
    conv_w,
    conv_b,
    dt_bias,
    a_log,
    d_skip,
):
    n_hd = lax.axis_size("hd")
    n_cp = lax.axis_size("cp")
    hd_index = lax.axis_index("hd")
    cp_index = lax.axis_index("cp")
    x_in = tokens[0].astype(jnp.float32)
    tok_count = x_in.shape[0]
    head_span = tok_count * n_hd
    d_ssm = HM * HDIM
    q_width = QH * HDIM
    k_width = KVH * HDIM
    x_part = d_ssm // n_hd
    heads_part = HM // n_hd
    q_part = q_width // n_hd
    q_heads = QH // n_hd
    bc_width = 2 * NST
    tap_count = conv_w.shape[0]
    score_scale = 1.0 / math.sqrt(HDIM)
    documents = doc_ids[0]
    w_inner, w_delta, w_mamba, w_attn, w_gate_up, w_back = (
        lax.all_gather(w_in, ("dp", "cp"), axis=0, tiled=True),
        lax.all_gather(w_dt, ("dp", "cp"), axis=0, tiled=True),
        lax.all_gather(w_mo, ("dp", "cp"), axis=0, tiled=True),
        lax.all_gather(w_ao, ("dp", "cp"), axis=0, tiled=True),
        lax.all_gather(w_gu, ("dp", "cp"), axis=0, tiled=True),
        lax.all_gather(w_down, ("dp", "cp"), axis=0, tiled=True),
    )
    normed1, norm1_pull = jax.vjp(rms_norm, x_in, norm1)
    normed1_low = normed1.astype(jnp.bfloat16)
    projected = jnp.dot(normed1_low, w_inner, preferred_element_type=jnp.float32)
    dt_proj = jnp.dot(normed1_low, w_delta, preferred_element_type=jnp.float32)
    gate_z = projected[:, :d_ssm]
    x_stream = projected[:, d_ssm : 2 * d_ssm]
    bc_stream = projected[:, 2 * d_ssm : 2 * d_ssm + bc_width]
    q_start = 2 * d_ssm + bc_width
    k_start = q_start + q_width
    v_start = k_start + k_width
    positions = (cp_index * n_hd + hd_index) * tok_count + jnp.arange(tok_count, dtype=jnp.int32)

    def rotate_both(query_in, key_in):
        return (
            rotate(query_in.reshape(tok_count, QH, HDIM), positions),
            rotate(key_in.reshape(tok_count, KVH, HDIM), positions),
        )

    (q_rot, k_rot), rope_pull = jax.vjp(
        rotate_both, projected[:, q_start:k_start], projected[:, k_start:v_start]
    )
    send_pack = jnp.concatenate(
        [
            x_stream.reshape(tok_count, n_hd, x_part),
            jnp.broadcast_to(bc_stream[:, None, :], (tok_count, n_hd, bc_width)),
            q_rot.reshape(tok_count, n_hd, q_part),
            k_rot,
            projected[:, v_start:].reshape(tok_count, n_hd, HDIM),
        ],
        axis=-1,
    ).astype(jnp.bfloat16)
    dt_pack = dt_proj.reshape(tok_count, n_hd, heads_part).astype(jnp.bfloat16)
    heads_in, dt_heads_in = (
        lax.all_to_all(send_pack, "hd", split_axis=1, concat_axis=0, tiled=True),
        lax.all_to_all(dt_pack, "hd", split_axis=1, concat_axis=0, tiled=True),
    )
    heads_in = heads_in[:, 0]
    dt_heads = dt_heads_in[:, 0].astype(jnp.float32)
    conv_in = heads_in[:, : x_part + bc_width]
    q_heads_in = heads_in[:, x_part + bc_width : x_part + bc_width + q_part]
    kv_local = heads_in[:, x_part + bc_width + q_part :]
    rim_rows = shifted(conv_in[head_span - (tap_count - 1) :], "cp", 1)
    padded = jnp.concatenate([rim_rows, conv_in], axis=0).astype(jnp.float32)
    conv_taps = jnp.concatenate(
        [lax.dynamic_slice_in_dim(conv_w, hd_index * x_part, x_part, 1), conv_w[:, d_ssm:]], axis=1
    )
    conv_shift = jnp.concatenate(
        [lax.dynamic_slice_in_dim(conv_b, hd_index * x_part, x_part, 0), conv_b[d_ssm:]], axis=0
    )
    dt_shift = lax.dynamic_slice_in_dim(dt_bias, hd_index * heads_part, heads_part, 0)
    log_scale = lax.dynamic_slice_in_dim(a_log, hd_index * heads_part, heads_part, 0)
    skip_gain = lax.dynamic_slice_in_dim(d_skip, hd_index * heads_part, heads_part, 0)

    def prepare(padded_in, taps_in, shift_in, dt_in, dt_shift_in, log_in):
        activated = jax.nn.silu(causal_conv(padded_in, taps_in, shift_in))
        return (
            activated[:, :x_part].reshape(head_span, heads_part, HDIM),
            activated[:, x_part : x_part + NST],
            activated[:, x_part + NST :],
            jax.nn.softplus(dt_in + dt_shift_in),
            -jnp.exp(log_in),
        )

    (x_conv, b_conv, c_conv, dt_value, decay_rate), prep_pull = jax.vjp(
        prepare, padded, conv_taps, conv_shift, dt_heads, dt_shift, log_scale
    )
    (state_local, total_decay), state_pull = jax.vjp(
        ssd_state, x_conv, b_conv, dt_value, decay_rate
    )
    decay_dev = jnp.exp(total_decay)
    state_in = prefix(
        (decay_dev, state_local),
        "cp",
        chain_states,
        (jnp.ones_like(decay_dev), jnp.zeros_like(state_local)),
    )[1]
    y_heads, ssd_pull = jax.vjp(
        ssd_out, x_conv, b_conv, c_conv, dt_value, decay_rate, skip_gain, state_in
    )
    kv_all = lax.all_gather(kv_local, "cp", axis=0, tiled=True)
    seq_len = n_cp * head_span
    key_tile = math.gcd(512, seq_len)
    row_count = head_span * q_heads
    q_rows = q_heads_in.reshape(row_count, HDIM)
    row_token = jnp.arange(row_count, dtype=jnp.int32) // q_heads
    query_pos = cp_index * head_span + row_token
    query_docs = jnp.repeat(
        lax.dynamic_slice_in_dim(documents, cp_index * head_span, head_span, 0), q_heads
    )
    key_token = jnp.arange(key_tile, dtype=jnp.int32)
    key_limit = ((cp_index + 1) * head_span + key_tile - 1) // key_tile

    def block_scores(kv_source, key_block):
        key_pos = key_block * key_tile + key_token
        key_piece = lax.dynamic_slice_in_dim(kv_source, key_block * key_tile, key_tile, 0)
        raw_scores = dot_t(q_rows, key_piece[:, :HDIM]) * score_scale
        key_docs = lax.dynamic_slice_in_dim(documents, key_block * key_tile, key_tile, 0)
        allowed = (key_pos[None, :] <= query_pos[:, None]) & (
            key_docs[None, :] == query_docs[:, None]
        )
        return (jnp.where(allowed, raw_scores, masked), allowed, key_piece)

    def first_pass(key_block, carried):
        row_top, row_total = carried
        scores, allowed, key_piece = block_scores(kv_all, key_block)
        new_top = jnp.maximum(row_top, jnp.max(scores, axis=1))
        weights = jnp.where(allowed, jnp.exp(scores - new_top[:, None]), 0.0)
        return (new_top, row_total * jnp.exp(row_top - new_top) + jnp.sum(weights, axis=1))

    start_state = (
        jnp.full((row_count,), masked, jnp.float32),
        jnp.zeros((row_count,), jnp.float32),
    )
    row_top, row_total = lax.fori_loop(0, key_limit, first_pass, start_state)
    log_sums = row_top + jnp.log(row_total)

    def second_pass(key_block, accum):
        scores, allowed, key_piece = block_scores(kv_all, key_block)
        probs = jnp.where(allowed, jnp.exp(scores - log_sums[:, None]), 0.0).astype(jnp.bfloat16)
        return accum + jnp.dot(probs, key_piece[:, HDIM:], preferred_element_type=jnp.float32)

    att_out = lax.fori_loop(0, key_limit, second_pass, jnp.zeros((row_count, HDIM), jnp.float32))
    out_pack = jnp.concatenate(
        [y_heads.reshape(head_span, x_part), att_out.reshape(head_span, q_part)], axis=-1
    ).astype(jnp.bfloat16)
    back_pack = lax.all_to_all(out_pack[:, None, :], "hd", split_axis=0, concat_axis=1, tiled=True)
    y_seq = back_pack[:, :, :x_part].reshape(tok_count, d_ssm).astype(jnp.float32)
    att_seq = back_pack[:, :, x_part:].reshape(tok_count, q_width)

    def gate_branch(y_input, z_input, gain_vec):
        return rms_norm(y_input * jax.nn.silu(z_input), gain_vec)

    gated, gated_pull = jax.vjp(gate_branch, y_seq, gate_z, gate_norm)
    gated_low = gated.astype(jnp.bfloat16)
    mixed = jnp.dot(gated_low, w_mamba, preferred_element_type=jnp.float32) + jnp.dot(
        att_seq, w_attn, preferred_element_type=jnp.float32
    )
    x_mid = x_in + mixed
    normed2, norm2_pull = jax.vjp(rms_norm, x_mid, norm2)
    normed2_low = normed2.astype(jnp.bfloat16)
    gate_up = jnp.dot(normed2_low, w_gate_up, preferred_element_type=jnp.float32)

    def swiglu(both_halves):
        return jax.nn.silu(both_halves[:, :FF]) * both_halves[:, FF:]

    hidden, swiglu_pull = jax.vjp(swiglu, gate_up)
    hidden_low = hidden.astype(jnp.bfloat16)
    result_seq = x_mid + jnp.dot(hidden_low, w_back, preferred_element_type=jnp.float32)
    grad_out = cotangent[0].astype(jnp.float32)
    grad_ffn_low = cotangent[0]
    g_down = t_dot(hidden_low, grad_ffn_low)
    grad_hidden = dot_t(grad_ffn_low, w_back)
    grad_gate_up = swiglu_pull(grad_hidden)[0].astype(jnp.bfloat16)
    g_gate_up = t_dot(normed2_low, grad_gate_up)
    grad_normed2 = dot_t(grad_gate_up, w_gate_up)
    grad_mid_part, g_norm2 = norm2_pull(grad_normed2)
    grad_mid = grad_out + grad_mid_part
    grad_mid_low = grad_mid.astype(jnp.bfloat16)
    g_mamba = t_dot(gated_low, grad_mid_low)
    g_attn = t_dot(att_seq, grad_mid_low)
    grad_gated = dot_t(grad_mid_low, w_mamba)
    grad_att_seq = dot_t(grad_mid_low, w_attn)
    grad_y, grad_z, g_gate_norm = gated_pull(grad_gated)
    grad_pack = jnp.concatenate(
        [grad_y.reshape(tok_count, n_hd, x_part), grad_att_seq.reshape(tok_count, n_hd, q_part)],
        axis=-1,
    ).astype(jnp.bfloat16)
    grad_heads = lax.all_to_all(grad_pack, "hd", split_axis=1, concat_axis=0, tiled=True)[:, 0]
    grad_y_heads = grad_heads[:, :x_part].astype(jnp.float32).reshape(head_span, heads_part, HDIM)
    grad_rows = grad_heads[:, x_part:].reshape(row_count, HDIM)
    keys_back = lax.all_gather(kv_local, "cp", axis=0, tiled=True)
    row_delta = jnp.sum(grad_rows.astype(jnp.float32) * att_out, axis=-1)

    def back_step(key_block, carried):
        grad_query, kv_buffer = carried
        scores, allowed, key_piece = block_scores(keys_back, key_block)
        probs = jnp.where(allowed, jnp.exp(scores - log_sums[:, None]), 0.0)
        grad_probs = dot_t(grad_rows, key_piece[:, HDIM:])
        grad_scores = (probs * (grad_probs - row_delta[:, None])).astype(jnp.bfloat16)
        grad_query = (
            grad_query
            + jnp.dot(grad_scores, key_piece[:, :HDIM], preferred_element_type=jnp.float32)
            * score_scale
        )
        grad_key = t_dot(grad_scores, q_rows) * score_scale
        grad_value = t_dot(probs.astype(jnp.bfloat16), grad_rows)
        previous = lax.dynamic_slice_in_dim(kv_buffer, key_block * key_tile, key_tile, 0)
        kv_buffer = lax.dynamic_update_slice_in_dim(
            kv_buffer,
            previous + jnp.concatenate([grad_key, grad_value], axis=1),
            key_block * key_tile,
            0,
        )
        return (grad_query, kv_buffer)

    grad_queries, kv_grads = lax.fori_loop(
        0,
        key_limit,
        back_step,
        (jnp.zeros((row_count, HDIM), jnp.float32), jnp.zeros((seq_len, 2 * HDIM), jnp.float32)),
    )
    own_kv_grads = lax.psum_scatter(
        kv_grads.astype(jnp.bfloat16), "cp", scatter_dimension=0, tiled=True
    ).astype(jnp.float32)
    grads_out = ssd_pull(grad_y_heads)
    future = entering_2(
        (decay_dev, grads_out[6]),
        "cp",
        chain_states,
        (jnp.ones_like(decay_dev), jnp.zeros_like(state_local)),
    )[1]
    grads_state = state_pull((future, decay_dev * jnp.sum(future * state_in, axis=(1, 2))))
    grad_prep = prep_pull(
        (
            grads_out[0] + grads_state[0],
            grads_out[1] + grads_state[1],
            grads_out[2],
            grads_out[3] + grads_state[2],
            grads_out[4] + grads_state[3],
        )
    )
    grad_padded, grad_taps, grad_shift, grad_dt_heads, grad_dt_shift, grad_log = grad_prep
    rim_back = shifted(grad_padded[: tap_count - 1], "cp", -1)
    grad_conv_in = grad_padded[tap_count - 1 :] + jnp.concatenate(
        [jnp.zeros((head_span - tap_count + 1, grad_padded.shape[1]), jnp.float32), rim_back],
        axis=0,
    )
    back_send = jnp.concatenate(
        [grad_conv_in, grad_queries.reshape(head_span, q_part), own_kv_grads], axis=-1
    ).astype(jnp.bfloat16)
    back_dt = grad_dt_heads.astype(jnp.bfloat16)
    grad_back, grad_dt_back = (
        lax.all_to_all(back_send[:, None, :], "hd", split_axis=0, concat_axis=1, tiled=True),
        lax.all_to_all(back_dt[:, None, :], "hd", split_axis=0, concat_axis=1, tiled=True),
    )
    grad_x_stream = grad_back[:, :, :x_part].reshape(tok_count, d_ssm)
    grad_bc = jnp.sum(
        grad_back[:, :, x_part : x_part + bc_width].astype(jnp.float32), axis=1
    ).astype(jnp.bfloat16)
    q_lo = x_part + bc_width
    grad_q_rot = (
        grad_back[:, :, q_lo : q_lo + q_part].astype(jnp.float32).reshape(tok_count, QH, HDIM)
    )
    grad_k_rot = grad_back[:, :, q_lo + q_part : q_lo + q_part + HDIM].astype(jnp.float32)
    grad_v = grad_back[:, :, q_lo + q_part + HDIM :].reshape(tok_count, k_width)
    grad_q_pre, grad_k_pre = rope_pull((grad_q_rot, grad_k_rot))
    grad_dt_seq = grad_dt_back.reshape(tok_count, HM)
    grad_proj = jnp.concatenate(
        [
            grad_z.astype(jnp.bfloat16),
            grad_x_stream,
            grad_bc,
            grad_q_pre.astype(jnp.bfloat16),
            grad_k_pre.astype(jnp.bfloat16),
            grad_v,
        ],
        axis=1,
    )
    g_inner = t_dot(normed1_low, grad_proj)
    g_delta = t_dot(normed1_low, grad_dt_seq)
    grad_normed1 = dot_t(grad_proj, w_inner) + dot_t(grad_dt_seq, w_delta)
    grad_x_part, g_norm1 = norm1_pull(grad_normed1)
    grad_tokens_out = (grad_mid + grad_x_part).astype(jnp.bfloat16)
    conv_x_full = lax.dynamic_update_slice_in_dim(
        jnp.zeros((tap_count, d_ssm), jnp.float32), grad_taps[:, :x_part], hd_index * x_part, 1
    )
    g_conv_w = jnp.concatenate([conv_x_full, grad_taps[:, x_part:]], axis=1)
    shift_x_full = lax.dynamic_update_slice_in_dim(
        jnp.zeros((d_ssm,), jnp.float32), grad_shift[:x_part], hd_index * x_part, 0
    )
    g_conv_b = jnp.concatenate([shift_x_full, grad_shift[x_part:]], axis=0)
    g_dt_bias = lax.dynamic_update_slice_in_dim(
        jnp.zeros((HM,), jnp.float32), grad_dt_shift, hd_index * heads_part, 0
    )
    g_a_log = lax.dynamic_update_slice_in_dim(
        jnp.zeros((HM,), jnp.float32), grad_log, hd_index * heads_part, 0
    )
    g_d_skip = lax.dynamic_update_slice_in_dim(
        jnp.zeros((HM,), jnp.float32), grads_out[5], hd_index * heads_part, 0
    )
    s_in, s_dt, s_mo, s_ao, s_gu, s_down = (
        lax.psum_scatter(g_inner, ("dp", "cp", "hd"), scatter_dimension=0, tiled=True),
        lax.psum_scatter(g_delta, ("dp", "cp", "hd"), scatter_dimension=0, tiled=True),
        lax.psum_scatter(g_mamba, ("dp", "cp", "hd"), scatter_dimension=0, tiled=True),
        lax.psum_scatter(g_attn, ("dp", "cp", "hd"), scatter_dimension=0, tiled=True),
        lax.psum_scatter(g_gate_up, ("dp", "cp", "hd"), scatter_dimension=0, tiled=True),
        lax.psum_scatter(g_down, ("dp", "cp", "hd"), scatter_dimension=0, tiled=True),
    )
    small_sums = lax.psum(
        (g_norm1, g_norm2, g_gate_norm, g_conv_w, g_conv_b, g_dt_bias, g_a_log, g_d_skip),
        ("dp", "cp", "hd"),
    )
    return (
        result_seq.astype(jnp.bfloat16)[None],
        grad_tokens_out[None],
        s_in,
        s_dt,
        s_mo,
        s_ao,
        s_gu,
        s_down,
        small_sums[0],
        small_sums[1],
        small_sums[2],
        small_sums[3],
        small_sums[4],
        small_sums[5],
        small_sums[6],
        small_sums[7],
    )


def solution(mesh):
    in_specs = (
        P("dp", ("cp", "hd"), None),
        P("dp", None),
        P("dp", ("cp", "hd"), None),
        P(("dp", "cp"), None),
        P(("dp", "cp"), None),
        P(("dp", "cp"), None),
        P(("dp", "cp"), None),
        P(("dp", "cp"), None),
        P(("dp", "cp"), None),
        P(),
        P(),
        P(),
        P(),
        P(),
        P(),
        P(),
        P(),
    )
    out_specs = (
        P("dp", ("cp", "hd"), None),
        P("dp", ("cp", "hd"), None),
        P(("dp", "cp", "hd"), None),
        P(("dp", "cp", "hd"), None),
        P(("dp", "cp", "hd"), None),
        P(("dp", "cp", "hd"), None),
        P(("dp", "cp", "hd"), None),
        P(("dp", "cp", "hd"), None),
        P(),
        P(),
        P(),
        P(),
        P(),
        P(),
        P(),
        P(),
    )
    return jax.shard_map(
        per_device, mesh=mesh, in_specs=in_specs, out_specs=out_specs, check_vma=False
    )
```

profile of v0, /device:TPU:0, one launch (start us, length us, event | category | flops | bytes accessed | tf_op | source)
XLA Modules:
  0.0 2164.0 jit_solution(11549934525176982024)
XLA Ops:
  10.1 77.7 %all-gather.13.cloned.1.call-done = bf16[1024,4096]{1,0:T(8,128)(2,1)} async-done(((bf16[64,4096]{1,0:T(8,128)(2,1)}), bf16[1024,4096]{1,0:T(8,128)(2,1)}) %all-gather.13.cloned.1.call-update) | async-done | bytes 8388624 | tf_op jit(solution)/shard_map/all_gather | solution.py:194
  103.6 30.4 %all-gather.2 = bf16[16,64,24]{1,2,0:T(8,128)(2,1)S(1)} all-gather(bf16[1,64,24]{1,2,0:T(8,128)(2,1)S(1)} %bitcast.530), channel_id=1, replica_groups=mesh['dp'=2,'cp'=8,'hd'=2] {'dp','cp'}, dimensions={0}, use_global_device_ids=true | all-gather | bytes 52224 | tf_op jit(solution)/shard_map/all_gather | solution.py:195
  165.7 19.1 all-gather.3
  196.9 11.1 while.99
  208.1 9.4 while.100
  218.5 9.9 all-gather.25.cloned.1.call-done
  252.9 19.5 all_to_all.90
  283.6 30.0 %all-gather.19.cloned.1.call-done = bf16[512,1024]{1,0:T(8,128)(2,1)} async-done(((bf16[32,1024]{1,0:T(8,128)(2,1)}), bf16[512,1024]{1,0:T(8,128)(2,1)}) %all-gather.19.cloned.1.call-update) | async-done | bytes 1048592 | tf_op jit(solution)/shard_map/all_gather | solution.py:197
  316.2 73.3 %all-gather.21.cloned.1.call-done = bf16[1024,4096]{1,0:T(8,128)(2,1)} async-done(((bf16[64,4096]{1,0:T(8,128)(2,1)}), bf16[1024,4096]{1,0:T(8,128)(2,1)}) %all-gather.21.cloned.1.call-update) | async-done | bytes 8388624 | tf_op jit(solution)/shard_map/all_gather | solution.py:198
  397.6 42.9 %all-gather.23.cloned.1.call-done = bf16[2048,1024]{1,0:T(8,128)(2,1)} async-done(((bf16[128,1024]{1,0:T(8,128)(2,1)}), bf16[2048,1024]{1,0:T(8,128)(2,1)}) %all-gather.23.cloned.1.call-update) | async-done | bytes 4194320 | tf_op jit(solution)/shard_map/all_gather | solution.py:199
  473.1 15.5 all-to-all-done.3
  516.4 46.4 %while.101 = (s32[]{:T(128)}, f32[2560,64]{0,1:T(8,128)}, f32[5120,128]{1,0:T(8,128)}, s32[]{:T(128)}, s32[5120]{0:T(1024)}, /*index=5*/bf16[5120,128]{1,0:T(8,1...) while((s32[]{:T(128)}, f32[2560,64]{0,1:T(8,128)}, ...), condition=%wide.region_26.27_spmd.clone, body=%wide.region_25.26_spmd.clone.sunk | while | flops 853793792 | bytes 51229516 | solution.py:396
  604.9 12.2 while.98
  668.3 13.4 fusion.163
  713.3 22.8 %collective-permute-done.1 = f32[3,1024]{1,0:T(4,128)S(1)} collective-permute-done((f32[3,1024]{1,0:T(4,128)S(1)}, f32[3,1024]{1,0:T(4,128)S(1)}, u32[]{:S(2)}, u32[]{:S(2)}) %collective-permute-start.1) | collective-permute-done | bytes 12320 | tf_op jit(solution)/shard_map/ppermute | solution.py:25
  736.4 116.0 %reduce-scatter.10.cloned.1.call-done = bf16[640,128]{1,0:T(8,128)(2,1)} async-done(((bf16[5120,128]{1,0:T(8,128)(2,1)}), bf16[640,128]{1,0:T(8,128)(2,1)}) %reduce-scatter.10.cloned.1.call-update) | async-done | bytes 163856 | tf_op jit(solution)/shard_map/reduce_scatter | solution.py:402
  868.9 17.1 all-to-all-done.4
  924.3 66.8 %reduce-scatter.22.cloned.1.call-done = f32[32,24]{1,0:T(8,128)} async-done(((f32[1024,24]{1,0:T(8,128)}), f32[32,24]{1,0:T(8,128)}) %reduce-scatter.22.cloned.1.call-update) | async-done | bytes 3088
  1000.4 38.9 %all-reduce.22 = (f32[1024]{0:T(1024)}, f32[1024]{0:T(1024)}, f32[1536]{0:T(1024)}, f32[4,1792]{1,0:T(4,128)}, f32[1792]{0:T(1024)}, /*index=5*/f32[24]{0:T(128)}, f32[24]{0:T(128)}, f32[24]{0:T(128)}) all-reduce(f32[1024]{0:T(1024)S(1)} %get-tuple-element.626, ...), channel_id=1, replica_groups=mesh['dp'=2,'cp'=8,'hd'=2] {'dp','cp','hd'}, use_global_device_ids=true, to_apply=%region_47.48 | all-reduce | flops 12616 | bytes 100928 | tf_op jit(solution)/shard_map/psum | solution.py:489
  1042.6 90.9 %reduce-scatter.16.cloned.1.call-done = f32[16,1024]{1,0:T(8,128)} async-done(((f32[512,1024]{1,0:T(8,128)}), f32[16,1024]{1,0:T(8,128)}) %reduce-scatter.16.cloned.1.call-update) | async-done | bytes 65552 | tf_op jit(solution)/shard_map/reduce_scatter | solution.py:485
  1133.5 117.0 %reduce-scatter.14.cloned.1.call-done = f32[48,1024]{1,0:T(8,128)} async-done(((f32[1536,1024]{1,0:T(8,128)}), f32[48,1024]{1,0:T(8,128)}) %reduce-scatter.14.cloned.1.call-update) | async-done | bytes 196624 | tf_op jit(solution)/shard_map/reduce_scatter | solution.py:484
  1250.4 187.3 %reduce-scatter.20.cloned.1.call-done = f32[64,1024]{1,0:T(8,128)} async-done(((f32[2048,1024]{1,0:T(8,128)}), f32[64,1024]{1,0:T(8,128)}) %reduce-scatter.20.cloned.1.call-update) | async-done | bytes 262160 | tf_op jit(solution)/shard_map/reduce_scatter | solution.py:487
  1437.7 359.9 %reduce-scatter.18.cloned.1.call-done = f32[32,4096]{1,0:T(8,128)} async-done(((f32[1024,4096]{1,0:T(8,128)}), f32[32,4096]{1,0:T(8,128)}) %reduce-scatter.18.cloned.1.call-update) | async-done | bytes 524304 | tf_op jit(solution)/shard_map/reduce_scatter | solution.py:486
  1797.7 359.6 %reduce-scatter.12.cloned.1.call-done = f32[32,4096]{1,0:T(8,128)} async-done(((f32[1024,4096]{1,0:T(8,128)}), f32[32,4096]{1,0:T(8,128)}) %reduce-scatter.12.cloned.1.call-update) | async-done | bytes 524304 | tf_op jit(solution)/shard_map/reduce_scatter | solution.py:482
  (734 shorter events, 451.5 us)
Async XLA Ops:
  7.2 80.7 %all-gather.13.cloned.1.call-start = ((), (), s32[]{:S(2)}) async-start(), calls=%async_computation.13 | async-start | bytes 8912896 | tf_op jit(solution)/shard_map/all_gather | solution.py:194
  99.6 35.7 %all-to-all-start = ((bf16[320,2,1408]{2,0,1:T(8,128)(2,1)}), bf16[320,2,1408]{2,0,1:T(8,128)(2,1)S(1)}, u32[]{:S(2)}, u32[]{:S(2)}) async-start(bf16[320,2,1408]{2,0,1:T(8,128)(2,1)} %concatenate.71), calls=%async_computation | async-start | bytes 3604480 | tf_op jit(solution)/shard_map/all_to_all | solution.py:234
  135.3 7.1 all-to-all-start.1
  138.5 58.3 %all-gather.15.cloned.1.call-start = ((), (), s32[]{:S(2)}) async-start(), calls=%async_computation.14 | async-start | bytes 1474560 | tf_op jit(solution)/shard_map/all_gather | solution.py:280
  139.5 88.9 %all-gather.25.cloned.1.call-start = ((), (), s32[]{:S(2)}) async-start(), calls=%async_computation.25 | async-start | bytes 1769472 | tf_op jit(solution)/shard_map/all_gather | solution.py:31
  145.3 4.1 collective-permute-start
  161.3 117.5 %all-gather.17.cloned.1.call-start = ((), (), s32[]{:S(2)}) async-start(), calls=%async_computation.15 | async-start | bytes 3342336 | tf_op jit(solution)/shard_map/all_gather | solution.py:196
  161.8 151.8 %all-gather.19.cloned.1.call-start = ((), (), s32[]{:S(2)}) async-start(), calls=%async_computation.16 | async-start | bytes 1114112 | tf_op jit(solution)/shard_map/all_gather | solution.py:197
  162.4 227.1 %all-gather.21.cloned.1.call-start = ((), (), s32[]{:S(2)}) async-start(), calls=%async_computation.17 | async-start | bytes 8912896 | tf_op jit(solution)/shard_map/all_gather | solution.py:198
  163.0 277.6 %all-gather.23.cloned.1.call-start = ((), (), s32[]{:S(2)}) async-start(), calls=%async_computation.18 | async-start | bytes 4456448 | tf_op jit(solution)/shard_map/all_gather | solution.py:199
  184.9 315.0 %copy-start.77 = (f32[5,128,12]{1,2,0:T(8,128)}, f32[5,128,12]{1,2,0:T(8,128)S(1)}, u32[]{:S(2)}) copy-start(f32[5,128,12]{1,2,0:T(8,128)S(1)} %get-tuple-element.785) | copy-start | bytes 92164
  278.7 183.0 %copy-start.9 = (f32[320,1536]{1,0:T(8,128)}, f32[320,1536]{1,0:T(8,128)S(1)}, u32[]{:S(2)}) copy-start(f32[320,1536]{1,0:T(8,128)S(1)} %get-tuple-element.750) | copy-start | bytes 5898244
  278.7 182.9 %copy-start.104 = (f32[320]{0:T(512)}, f32[320]{0:T(512)S(1)}, u32[]{:S(2)}) copy-start(f32[320]{0:T(512)S(1)} %fusion.200) | copy-start | bytes 3844
  467.8 20.8 all-to-all-start.3
  471.5 133.3 %all-gather.27.cloned.1.call-start = ((), (), s32[]{:S(2)}) async-start(), calls=%async_computation.26 | async-start | bytes 1769472 | tf_op jit(solution)/shard_map/all_gather | solution.py:53
  511.8 340.6 %reduce-scatter.10.cloned.1.call-start = ((), (), s32[]{:S(2)}) async-start(), calls=%async_computation.19 | async-start | bytes 1474560 | tf_op jit(solution)/shard_map/reduce_scatter | solution.py:402
  604.7 386.4 %reduce-scatter.22.cloned.1.call-start = ((), (), s32[]{:S(2)}) async-start(), calls=%async_computation.27 | async-start | bytes 540672
  650.1 483.4 %reduce-scatter.16.cloned.1.call-start = ((), (), s32[]{:S(2)}) async-start(), calls=%async_computation.22 | async-start | bytes 2162688 | tf_op jit(solution)/shard_map/reduce_scatter | solution.py:485
  653.4 597.1 %reduce-scatter.14.cloned.1.call-start = ((), (), s32[]{:S(2)}) async-start(), calls=%async_computation.21 | async-start | bytes 6488064 | tf_op jit(solution)/shard_map/reduce_scatter | solution.py:484
  659.5 778.2 %reduce-scatter.20.cloned.1.call-start = ((), (), s32[]{:S(2)}) async-start(), calls=%async_computation.24 | async-start | bytes 8650752 | tf_op jit(solution)/shard_map/reduce_scatter | solution.py:487
  667.6 1130.1 %reduce-scatter.18.cloned.1.call-start = ((), (), s32[]{:S(2)}) async-start(), calls=%async_computation.23 | async-start | bytes 17301504 | tf_op jit(solution)/shard_map/reduce_scatter | solution.py:486
  710.4 25.7 %collective-permute-start.1 = (f32[3,1024]{1,0:T(4,128)S(1)}, f32[3,1024]{1,0:T(4,128)S(1)}, u32[]{:S(2)}, u32[]{:S(2)}) collective-permute-start(f32[3,1024]{1,0:T(4,128)S(1)} %pad_add_fusion.1), channel_id=1, source_target_pairs={{2,0},{4,2},{6,4},{8,6},{10,8},{12,10},{14,12},{3,1},{5,3},{7,5},{... | collective-permute-start | bytes 36872 | tf_op jit(solution)/shard_map/ppermute | solution.py:25
  858.9 27.1 %all-to-all-start.4 = ((bf16[2,2,225280]{2,1,0:T(2,128)(2,1)}), bf16[2,2,225280]{2,1,0:T(2,128)(2,1)}, u32[]{:S(2)}, u32[]{:S(2)}) async-start(bf16[2,2,225280]{2,1,0:T(2,128)(2,1)} %reshape.626), calls=%async_computation.5 | async-start | bytes 3604480 | tf_op jit(solution)/shard_map/all_to_all | solution.py:433
  863.7 1293.5 %reduce-scatter.12.cloned.1.call-start = ((), (), s32[]{:S(2)}) async-start(), calls=%async_computation.20 | async-start | bytes 17301504 | tf_op jit(solution)/shard_map/reduce_scatter | solution.py:482
  (156 other events, 2435.1 us)
Sparse Core Ops, SparseCore 0:
  10.2 77.5 all-gather.12
  142.1 40.5 all-gather.14
  185.5 42.8 all-gather.24
  230.5 44.2 all-gather.16
  276.8 36.7 all-gather.18
  315.7 73.8 all-gather.20
  391.7 48.8 all-gather.22
  511.5 41.7 all-gather.26
  604.9 247.5 reduce-scatter.9
  854.6 136.5 reduce-scatter.21
  994.1 139.3 reduce-scatter.15
  1139.5 110.8 reduce-scatter.13
  1253.4 184.3 reduce-scatter.19
  1440.6 357.0 reduce-scatter.17
  1800.5 356.6 reduce-scatter.11
where the time goes:
time: 2180 us; the launch traced here: 2160 us
  waiting for transfers between devices  1590 us (73%)
  matrix products  198 us (9%)
  blocking collectives  115 us (5%)
  local copies, waits for them, and re-layouts  114 us (5%)
  other arithmetic  104 us (5%)
    reduce_scatter x1, waiting for transfers between devices, per_device(): lax.psum_scatter(g_gate_up, ('dp', 'cp', 'hd'), scatter_dimension=0, tile...  360 us
    reduce_scatter x1, waiting for transfers between devices, per_device(): lax.psum_scatter(g_inner, ('dp', 'cp', 'hd'), scatter_dimension=0, tiled=...  360 us
    reduce_scatter x1, waiting for transfers between devices, per_device(): lax.psum_scatter(g_down, ('dp', 'cp', 'hd'), scatter_dimension=0, tiled=T...  187 us
    reduce_scatter x1, waiting for transfers between devices, per_device(): lax.psum_scatter(g_mamba, ('dp', 'cp', 'hd'), scatter_dimension=0, tiled=...  117 us
    reduce_scatter x1, waiting for transfers between devices, per_device(): lax.psum_scatter(kv_grads.astype(jnp.bfloat16), 'cp', scatter_dimension=0...  116 us
    reduce_scatter x1, waiting for transfers between devices, per_device(): lax.psum_scatter(g_attn, ('dp', 'cp', 'hd'), scatter_dimension=0, tiled=T...  90.9 us
    all_gather x1, waiting for transfers between devices, per_device(): lax.all_gather(w_in, ('dp', 'cp'), axis=0, tiled=True)  77.7 us
    all_gather x1, waiting for transfers between devices, per_device(): lax.all_gather(w_gu, ('dp', 'cp'), axis=0, tiled=True)  73.3 us
  transfers between devices with their start and end apart: 21, of which 17 were waited for; matrix products, arithmetic and copies ran while one was open for 16% of the time, Pallas kernels for 0%

commit v1 on v0

v1 whole, which is shorter than its diff:
```python
import math

import jax
import jax.numpy as jnp
from jax import lax
from jax.experimental import pallas as pl
from jax.experimental.pallas import tpu as pltpu
from jax.sharding import PartitionSpec as P

HM = 24
HDIM = 64
NST = 128
QH = 8
KVH = 2
FF = 2048

eps_norm = 1e-05
rope_base = 100000000000.0
masked = -1e30
highest = lax.Precision.HIGHEST
low_type = jnp.bfloat16
f32 = jnp.float32
chunk_len = 128
vmem_bytes = 56 * 1024 * 1024


def swap(value, axis, bit):
    count = lax.axis_size(axis)
    return lax.ppermute(value, axis, [(i, i ^ bit) for i in range(count)])


def shifted(value, axis, steps):
    count = lax.axis_size(axis)
    initial, last = (max(0, -steps), min(count, count - steps))
    return lax.ppermute(value, axis, [(source, source + steps) for source in range(initial, last)])


def has_bit(axis, bit):
    return (lax.axis_index(axis) & bit) != 0


def in_order(mine, other, high, dim, join):
    return join([jnp.where(high, other, mine), jnp.where(high, mine, other)], dim)


def gather_cp(value):
    rows, cols = value.shape
    held = value[None]
    bit = lax.axis_size("cp") // 2
    while bit:
        other = swap(held, "cp", bit)
        held = in_order(held, other, has_bit("cp", bit), 1, jnp.stack).reshape(-1, rows, cols)
        bit //= 2
    return held.reshape(-1, cols)


def gather_pair(value, axis, dim):
    return in_order(value, swap(value, axis, 1), has_bit(axis, 1), dim, jnp.concatenate)


def fold(value, axis, bit, dim):
    high = has_bit(axis, bit)
    first = lax.index_in_dim(value, 0, dim, False)
    second = lax.index_in_dim(value, 1, dim, False)
    got = swap(jnp.where(high, first, second).astype(low_type), axis, bit)
    return jnp.where(high, second, first).astype(f32) + got.astype(f32)


def fold_cp(value, order):
    count = lax.axis_size("cp")
    bits = count.bit_length() - 1
    held = value.reshape((2,) * bits + value.shape[1:])
    left = [1 << (bits - 1 - d) for d in range(bits)]
    for bit in order:
        dim = left.index(bit)
        held = fold(held, "cp", bit, dim)
        left.pop(dim)
        if left:
            held = held.astype(low_type)
    return held


def low_first():
    return [1 << d for d in range(lax.axis_size("cp").bit_length() - 1)]


def low_last():
    bits = low_first()
    return bits[1:] + bits[:1]


def after(value, earlier):
    return value + (earlier.reshape(-1)[0].astype(f32) * 0.0).astype(value.dtype)


def state_scan(log_decay, state, forward):
    heads = log_decay.shape[0]
    width = state.shape[1] // heads
    pre_log, pre_state = jnp.zeros_like(log_decay), jnp.zeros_like(state)
    count = lax.axis_size("cp")
    bit = 1

    def spread(values):
        return jnp.repeat(jnp.exp(values), width)[None, :]

    while bit < count:
        top = log_decay.astype(low_type)
        rest = (log_decay - top.astype(f32)).astype(low_type)
        tail = jnp.concatenate([top, rest, jnp.zeros((state.shape[1] - 2 * heads,), low_type)])
        tail = jnp.concatenate([tail[None], jnp.zeros((15, state.shape[1]), low_type)], axis=0)
        got = swap(jnp.concatenate([state.astype(low_type), tail], axis=0), "cp", bit)
        got_state = got[:-16].astype(f32)
        got_log = got[-16, :heads].astype(f32) + got[-16, heads : 2 * heads].astype(f32)
        joins = has_bit("cp", bit) if forward else jnp.logical_not(has_bit("cp", bit))
        pre_state = jnp.where(joins, spread(pre_log) * got_state + pre_state, pre_state)
        pre_log = jnp.where(joins, pre_log + got_log, pre_log)
        state = jnp.where(
            joins, spread(log_decay) * got_state + state, spread(got_log) * state + got_state
        )
        log_decay = log_decay + got_log
        bit *= 2
    return pre_state


def rms_norm(values, gain_vec):
    return (
        values * lax.rsqrt(jnp.mean(values * values, axis=-1, keepdims=True) + eps_norm) * gain_vec
    )


def turn(values, cosines, sines):
    half_width = values.shape[-1] // 2
    first_half = values[..., :half_width]
    second_half = values[..., half_width:]
    return jnp.concatenate(
        [first_half * cosines - second_half * sines, second_half * cosines + first_half * sines],
        axis=-1,
    )


def causal_conv(padded, conv_taps, conv_shift):
    tap_count = conv_taps.shape[0]
    out_rows = padded.shape[0] - tap_count + 1
    summed = conv_shift[None, :]
    for tap_index in range(tap_count):
        summed = summed + conv_taps[tap_index][None, :] * padded[tap_index : tap_index + out_rows]
    return summed


def t_dot(left, right, precision=None):
    return lax.dot_general(
        left,
        right,
        (((0,), (0,)), ((), ())),
        preferred_element_type=f32,
        precision=precision,
    )


def dot_t(left, right, precision=None):
    return lax.dot_general(
        left,
        right,
        (((1,), (1,)), ((), ())),
        preferred_element_type=f32,
        precision=precision,
    )


def dot(left, right, precision=None):
    return jnp.dot(left, right, preferred_element_type=f32, precision=precision)


def att_fwd_kernel(where_ref, q_ref, kv_ref, start_ref, out_ref, lse_ref, top_s, sum_s, acc_s):
    span = q_ref.shape[0]
    place = where_ref[0]
    latest = where_ref[1]
    queries = q_ref[...]
    top_s[...] = jnp.full(top_s.shape, masked, f32)
    sum_s[...] = jnp.zeros(sum_s.shape, f32)
    acc_s[...] = jnp.zeros(acc_s.shape, f32)

    def block(turn_index, _):
        j = place - turn_index
        base = pl.multiple_of(j * span, span)
        keys = kv_ref[pl.ds(base, span), :]
        raw = dot_t(queries, keys)

        def hide(scores):
            key_pos = base + lax.broadcasted_iota(jnp.int32, scores.shape, 1)
            row_pos = place * span + lax.broadcasted_iota(jnp.int32, scores.shape, 0)
            return jnp.where((key_pos <= row_pos) & (key_pos >= start_ref[...]), scores, masked)

        def work(scores):
            old_top = top_s[...]
            new_top = jnp.maximum(old_top, jnp.max(scores, axis=1, keepdims=True))
            weights = jnp.exp(scores - new_top)
            fall = jnp.exp(old_top - new_top)
            sum_s[...] = sum_s[...] * fall + jnp.sum(weights, axis=1, keepdims=True)
            acc_s[...] = acc_s[...] * fall + dot(weights.astype(low_type), keys)
            top_s[...] = new_top

        needs = (j == place) | (latest > base)

        @pl.when(needs)
        def _():
            work(hide(raw))

        @pl.when(jnp.logical_not(needs))
        def _():
            work(raw)

        return 0

    lax.fori_loop(0, place + 1, block, 0)
    out_ref[...] = acc_s[...] / sum_s[...]
    lse_ref[...] = top_s[...] + jnp.log(sum_s[...])


def att_bwd_kernel(
    where_ref, q_ref, do_ref, kv_ref, start_ref, lse_ref, delta_ref, dq_ref, dkv_ref
):
    span = q_ref.shape[0]
    place = where_ref[0]
    latest = where_ref[1]
    queries = q_ref[...]
    grads = do_ref[...]
    dq_ref[...] = jnp.zeros(dq_ref.shape, f32)

    @pl.when(pl.program_id(0) == 0)
    def _():
        dkv_ref[...] = jnp.zeros(dkv_ref.shape, f32)

    def block(j, _):
        base = pl.multiple_of(j * span, span)
        keys = kv_ref[pl.ds(base, span), :]
        raw = dot_t(keys, queries)
        grad_probs = dot_t(keys, grads)

        def hide(scores):
            key_pos = base + lax.broadcasted_iota(jnp.int32, scores.shape, 0)
            row_pos = place * span + lax.broadcasted_iota(jnp.int32, scores.shape, 1)
            return jnp.where((key_pos <= row_pos) & (key_pos >= start_ref[...]), scores, masked)

        def work(scores):
            probs = jnp.exp(scores - lse_ref[...])
            grad_scores = (probs * (grad_probs - delta_ref[...])).astype(low_type)
            dq_ref[...] += t_dot(grad_scores, keys)
            dkv_ref[pl.ds(base, span), :] += dot(grad_scores, queries) + dot(
                probs.astype(low_type), grads
            )

        needs = (j == place) | (latest > base)

        @pl.when(needs)
        def _():
            work(hide(raw))

        @pl.when(jnp.logical_not(needs))
        def _():
            work(raw)

        return 0

    lax.fori_loop(0, place + 1, block, 0)


def whole_spec(shape):
    return pl.BlockSpec(shape, lambda *_: (0,) * len(shape))


def head_spec(*shape):
    return pl.BlockSpec((None,) + shape, lambda i: (i,) + (0,) * len(shape))


def att_cost(span, heads, keys, matmuls):
    return pl.CostEstimate(
        flops=2 * matmuls * span * heads * keys * 256,
        bytes_accessed=4 * keys * 128,
        transcendentals=span * heads * keys,
    )


def attention_forward(where, queries, kv_all, starts):
    heads, span, width = queries.shape
    return pl.pallas_call(
        att_fwd_kernel,
        grid=(heads,),
        in_specs=[
            pl.BlockSpec(memory_space=pltpu.SMEM),
            head_spec(span, width),
            whole_spec(kv_all.shape),
            whole_spec((span, 1)),
        ],
        out_specs=[head_spec(span, width), head_spec(span, 1)],
        out_shape=[
            jax.ShapeDtypeStruct((heads, span, width), f32),
            jax.ShapeDtypeStruct((heads, span, 1), f32),
        ],
        scratch_shapes=[
            pltpu.VMEM((span, 1), f32),
            pltpu.VMEM((span, 1), f32),
            pltpu.VMEM((span, width), f32),
        ],
        compiler_params=pltpu.CompilerParams(vmem_limit_bytes=vmem_bytes),
        cost_estimate=att_cost(span, heads, kv_all.shape[0], 4),
        name="attention_forward",
    )(where, queries, kv_all, starts.reshape(span, 1))


def attention_backward(where, queries, grads, kv_all, starts, lse, delta):
    heads, span, width = queries.shape
    return pl.pallas_call(
        att_bwd_kernel,
        grid=(heads,),
        in_specs=[
            pl.BlockSpec(memory_space=pltpu.SMEM),
            head_spec(span, width),
            head_spec(span, width),
            whole_spec(kv_all.shape),
            whole_spec((1, span)),
            head_spec(1, span),
            head_spec(1, span),
        ],
        out_specs=[head_spec(span, width), whole_spec(kv_all.shape)],
        out_shape=[
            jax.ShapeDtypeStruct((heads, span, width), f32),
            jax.ShapeDtypeStruct(kv_all.shape, f32),
        ],
        compiler_params=pltpu.CompilerParams(vmem_limit_bytes=vmem_bytes),
        cost_estimate=att_cost(span, heads, kv_all.shape[0], 10),
        name="attention_backward",
    )(
        where,
        queries,
        grads,
        kv_all,
        starts.reshape(1, span),
        lse.reshape(heads, 1, span),
        delta.reshape(heads, 1, span),
    )


def pair_blocks(pair):
    left = lax.broadcasted_iota(jnp.int32, pair.shape, 1) < HDIM
    return jnp.where(left, pair, 0.0), jnp.where(left, 0.0, pair)


def ssd_fwd_kernel(xd_ref, b_ref, c_ref, cs_ref, cst_ref, csx_ref, in_ref, y_ref, before_ref, s_s):
    @pl.when(pl.program_id(0) == 0)
    def _():
        s_s[...] = in_ref[...]

    rows = xd_ref.shape[0]
    b, c = b_ref[...], c_ref[...]
    inner = dot_t(c, b, highest)
    lower = lax.broadcasted_iota(jnp.int32, (rows, rows), 0) >= lax.broadcasted_iota(
        jnp.int32, (rows, rows), 1
    )
    state = s_s[...]
    before_ref[...] = state
    csx = csx_ref[...]
    last = csx[rows - 1 :, :]
    carried = jnp.exp(csx) * dot(c, state, highest)

    def mixing(h):
        spread = jnp.where(lower, cs_ref[:, h : h + 1] - cst_ref[h : h + 1, :], masked)
        return jnp.exp(spread) * inner

    for pair in range(xd_ref.shape[1] // (2 * HDIM)):
        cols = slice(pair * 2 * HDIM, (pair + 1) * 2 * HDIM)
        mix = jnp.concatenate([mixing(2 * pair), mixing(2 * pair + 1)], axis=1)
        blocks = jnp.concatenate(pair_blocks(xd_ref[:, cols]), axis=0)
        y_ref[:, cols] = carried[:, cols] + dot(mix, blocks, highest)
    s_s[...] = jnp.exp(last) * state + t_dot(b, jnp.exp(last - csx) * xd_ref[...], highest)


def ssd_bwd_kernel(
    xd_ref,
    dy_ref,
    b_ref,
    c_ref,
    cs_ref,
    cst_ref,
    csx_ref,
    before_ref,
    future_ref,
    dxd_ref,
    db_ref,
    dc_ref,
    ds_s,
):
    @pl.when(pl.program_id(0) == 0)
    def _():
        ds_s[...] = future_ref[...]

    rows = xd_ref.shape[0]
    b, c = b_ref[...], c_ref[...]
    inner_t = dot_t(b, c, highest)
    row_id = lax.broadcasted_iota(jnp.int32, (rows, rows), 0)
    col_id = lax.broadcasted_iota(jnp.int32, (rows, rows), 1)
    csx = csx_ref[...]
    last = csx[rows - 1 :, :]
    grad_state = ds_s[...]
    end_fall = jnp.exp(last - csx)
    from_state = end_fall * dot(b, grad_state, highest)
    scaled_dy = jnp.exp(csx) * dy_ref[...]
    grad_inner = jnp.zeros((rows, rows), f32)

    def falls(h):
        spread = cs_ref[:, h : h + 1] - cst_ref[h : h + 1, :]
        return jnp.exp(jnp.where(row_id >= col_id, spread, masked))

    def falls_t(h):
        spread = cst_ref[h : h + 1, :] - cs_ref[:, h : h + 1]
        return jnp.exp(jnp.where(row_id <= col_id, spread, masked))

    for pair in range(xd_ref.shape[1] // (2 * HDIM)):
        cols = slice(pair * 2 * HDIM, (pair + 1) * 2 * HDIM)
        dy_left, dy_right = pair_blocks(dy_ref[:, cols])
        mix_t = jnp.concatenate(
            [falls_t(2 * pair) * inner_t, falls_t(2 * pair + 1) * inner_t], axis=1
        )
        blocks = jnp.concatenate([dy_left, dy_right], axis=0)
        dxd_ref[:, cols] = from_state[:, cols] + dot(mix_t, blocks, highest)
        xd = xd_ref[:, cols]
        grad_inner = grad_inner + falls(2 * pair) * dot_t(dy_left, xd, highest)
        grad_inner = grad_inner + falls(2 * pair + 1) * dot_t(dy_right, xd, highest)
    dc_ref[...] = dot(grad_inner, b, highest) + dot_t(scaled_dy, before_ref[...], highest)
    db_ref[...] = t_dot(grad_inner, c, highest) + dot_t(
        end_fall * xd_ref[...], grad_state, highest
    )
    ds_s[...] = jnp.exp(last) * grad_state + t_dot(c, scaled_dy, highest)


def ssd_forward(xd, b, c, cs, cst, csx, entering):
    length, width = xd.shape
    blocks = length // chunk_len
    heads = cs.shape[1]

    def rows(w):
        return pl.BlockSpec((chunk_len, w), lambda i: (i, 0))

    return pl.pallas_call(
        ssd_fwd_kernel,
        grid=(blocks,),
        in_specs=[
            rows(width),
            rows(NST),
            rows(NST),
            rows(heads),
            pl.BlockSpec((None, heads, chunk_len), lambda i: (i, 0, 0)),
            rows(width),
            whole_spec((NST, width)),
        ],
        out_specs=[rows(width), pl.BlockSpec((None, NST, width), lambda i: (i, 0, 0))],
        out_shape=[
            jax.ShapeDtypeStruct((length, width), f32),
            jax.ShapeDtypeStruct((blocks, NST, width), f32),
        ],
        scratch_shapes=[pltpu.VMEM((NST, width), f32)],
        compiler_params=pltpu.CompilerParams(vmem_limit_bytes=vmem_bytes),
        cost_estimate=pl.CostEstimate(
            flops=12 * 3 * length * width * NST, bytes_accessed=20 * length * width, transcendentals=0
        ),
        name="ssd_forward",
    )(xd, b, c, cs, cst, csx, entering)


def ssd_backward(xd, dy, b, c, cs, cst, csx, before, future):
    length, width = xd.shape
    blocks = length // chunk_len
    heads = cs.shape[1]

    def rows(w):
        return pl.BlockSpec((chunk_len, w), lambda i: (blocks - 1 - i, 0))

    def slabs(*shape):
        return pl.BlockSpec((None,) + shape, lambda i: (blocks - 1 - i, 0, 0))

    return pl.pallas_call(
        ssd_bwd_kernel,
        grid=(blocks,),
        in_specs=[
            rows(width),
            rows(width),
            rows(NST),
            rows(NST),
            rows(heads),
            slabs(heads, chunk_len),
            rows(width),
            slabs(NST, width),
            whole_spec((NST, width)),
        ],
        out_specs=[rows(width), rows(NST), rows(NST)],
        out_shape=[
            jax.ShapeDtypeStruct((length, width), f32),
            jax.ShapeDtypeStruct((length, NST), f32),
            jax.ShapeDtypeStruct((length, NST), f32),
        ],
        scratch_shapes=[pltpu.VMEM((NST, width), f32)],
        compiler_params=pltpu.CompilerParams(vmem_limit_bytes=vmem_bytes),
        cost_estimate=pl.CostEstimate(
            flops=12 * 8 * length * width * NST, bytes_accessed=24 * length * width, transcendentals=0
        ),
        name="ssd_backward",
    )(xd, dy, b, c, cs, cst, csx, before, future)


def per_device(
    tokens,
    doc_ids,
    cotangent,
    w_in,
    w_dt,
    w_mo,
    w_ao,
    w_gu,
    w_down,
    norm1,
    norm2,
    gate_norm,
    conv_w,
    conv_b,
    dt_bias,
    a_log,
    d_skip,
):
    n_hd = lax.axis_size("hd")
    n_cp = lax.axis_size("cp")
    hd_index = lax.axis_index("hd")
    cp_index = lax.axis_index("cp")
    dp_index = lax.axis_index("dp")
    hd_high = has_bit("hd", 1)
    x_in = tokens[0].astype(f32)
    tok_count, d_model = x_in.shape
    span = tok_count * n_hd
    d_ssm = HM * HDIM
    q_width = QH * HDIM
    k_width = KVH * HDIM
    x_part = d_ssm // n_hd
    heads = HM // n_hd
    q_part = q_width // n_hd
    k_part = k_width // n_hd
    q_heads = QH // n_hd
    bc_width = 2 * NST
    tap_count = conv_w.shape[0]
    score_scale = 1.0 / math.sqrt(HDIM)
    documents = doc_ids[0]

    def group(array, begin, width, dim=1):
        part = width // n_hd
        return lax.dynamic_slice_in_dim(array, begin + hd_index * part, part, dim)

    q_start = 2 * d_ssm + bc_width
    k_start = q_start + q_width
    v_start = k_start + k_width
    dt_pad = 128 - heads
    early = jnp.concatenate(
        [
            group(w_in, d_ssm, d_ssm),
            w_in[:, 2 * d_ssm : q_start],
            group(w_in, q_start, q_width),
            group(w_in, k_start, k_width),
            group(w_in, v_start, k_width),
            group(w_dt, 0, HM),
            jnp.zeros((w_dt.shape[0], dt_pad), low_type),
        ],
        axis=1,
    )
    early_cp = gather_cp(early)
    w_early = gather_pair(early_cp, "dp", 0)
    w_z = gather_pair(gather_cp(after(group(w_in, 0, d_ssm), early_cp)), "dp", 0)

    out_rows = jnp.concatenate([after(w_mo, early_cp), w_ao], axis=0)
    half_cols = d_model // 2
    handed = swap(out_rows[:, half_cols:], "dp", 1)
    holds = dp_index == hd_index
    out_half = jnp.where(holds, out_rows[:, :half_cols], handed)
    out_gathered = gather_cp(out_half)
    out_other = swap(out_gathered, "dp", 1)
    w_out = in_order(out_gathered, out_other, jnp.logical_not(holds), 1, jnp.concatenate)
    mo_rows, ao_rows = w_mo.shape[0], w_ao.shape[0]
    w_out = w_out.reshape(n_cp, mo_rows + ao_rows, d_model)
    w_out = jnp.concatenate(
        [
            w_out[:, :mo_rows].reshape(n_cp * mo_rows, d_model),
            w_out[:, mo_rows:].reshape(n_cp * ao_rows, d_model),
        ],
        axis=0,
    )

    gu_half = gather_cp(after(group(w_gu, 0, 2 * FF), out_gathered))
    w_gate_up = gather_pair(gather_pair(gu_half, "hd", 1), "dp", 0)
    down_half = gather_cp(after(group(w_down, 0, d_model), gu_half))
    w_back = gather_pair(gather_pair(down_half, "hd", 1), "dp", 0)

    tokens_all = gather_pair(tokens[0], "hd", 0)
    normed1_all = rms_norm(tokens_all.astype(f32), norm1).astype(low_type)
    proj = dot(normed1_all, w_early)
    x_bc = proj[:, : x_part + bc_width].astype(low_type)
    at = x_part + bc_width
    qk = proj[:, at : at + q_part + k_part].reshape(span, q_heads + 1, HDIM)
    v_low = proj[:, at + q_part + k_part : at + q_part + 2 * k_part].astype(low_type)
    at = at + q_part + 2 * k_part
    dt_raw = proj[:, at : at + heads].astype(low_type).astype(f32)
    positions = cp_index * span + jnp.arange(span, dtype=jnp.int32)
    half_width = HDIM // 2
    frequency = rope_base ** (-2.0 * jnp.arange(half_width, dtype=f32) / HDIM)
    angles = positions.astype(f32)[:, None] * frequency[None, :]
    cosines = jnp.cos(angles)[:, None, :]
    sines = jnp.sin(angles)[:, None, :]
    qk_rot = turn(qk, cosines, sines).astype(low_type)
    kv_local = jnp.concatenate([qk_rot[:, q_heads], v_low], axis=1)
    kv_all = gather_cp(kv_local)

    rim_rows = shifted(x_bc[span - (tap_count - 1) :], "cp", 1)
    padded = jnp.concatenate([rim_rows, x_bc], axis=0).astype(f32)
    conv_taps = jnp.concatenate([group(conv_w, 0, d_ssm), conv_w[:, d_ssm:]], axis=1)
    conv_shift = jnp.concatenate([group(conv_b, 0, d_ssm, 0), conv_b[d_ssm:]], axis=0)
    dt_shift = group(dt_bias, 0, HM, 0)
    log_scale = group(a_log, 0, HM, 0)
    skip_gain = group(d_skip, 0, HM, 0)
    skip_x = jnp.repeat(skip_gain, HDIM)[None, :]

    def prepare(padded_in, taps_in, shift_in, dt_in, dt_shift_in, log_in):
        activated = jax.nn.silu(causal_conv(padded_in, taps_in, shift_in))
        return (
            activated[:, :x_part],
            activated[:, x_part : x_part + NST],
            activated[:, x_part + NST :],
            jax.nn.softplus(dt_in + dt_shift_in),
            -jnp.exp(log_in),
        )

    (x_conv, b_conv, c_conv, dt_value, decay_rate), prep_pull = jax.vjp(
        prepare, padded, conv_taps, conv_shift, dt_raw, dt_shift, log_scale
    )
    blocks = span // chunk_len
    ones_low = jnp.tril(jnp.ones((chunk_len, chunk_len), f32))
    cs_block = jnp.einsum(
        "ts,bsh->bth",
        ones_low,
        (dt_value * decay_rate[None, :]).reshape(blocks, chunk_len, heads),
        precision=highest,
    )
    block_total = cs_block[:, -1]
    block_base = jnp.concatenate(
        [jnp.zeros((1, heads), f32), jnp.cumsum(block_total, axis=0)], axis=0
    )
    cs_dev = (cs_block + block_base[:-1, None, :]).reshape(span, heads)
    cs = cs_block.reshape(span, heads)
    cst = jnp.swapaxes(cs_block, 1, 2)
    log_dev = block_base[-1]

    def wide(values):
        return jnp.repeat(values, HDIM, axis=1)

    csx = wide(cs)
    csx_dev = wide(cs_dev)
    dtx = wide(dt_value)
    xd = dtx * x_conv
    state_local = t_dot(b_conv, jnp.exp(csx_dev[-1:] - csx_dev) * xd, highest)
    state_in = state_scan(log_dev, state_local, True)

    own_docs = lax.dynamic_slice_in_dim(documents, cp_index * span, span, 0)
    doc_begin = jnp.sum(documents[None, :] < own_docs[:, None], axis=1).astype(jnp.int32)
    where = jnp.stack([cp_index, jnp.max(doc_begin)]).astype(jnp.int32)
    q_scaled = (qk_rot[:, :q_heads] * jnp.asarray(score_scale, low_type)).swapaxes(0, 1)
    q_wide = jnp.concatenate([q_scaled, jnp.zeros_like(q_scaled)], axis=-1)
    att_wide, lse = attention_forward(where, q_wide, kv_all, doc_begin)
    att_f32 = att_wide[:, :, HDIM:]
    att_low = att_f32.swapaxes(0, 1).reshape(span, q_part).astype(low_type)

    y_core, before = ssd_forward(xd, b_conv, c_conv, cs, cst, csx, state_in)
    y_low = (y_core + skip_x * x_conv).astype(low_type).astype(f32)

    gate_z = dot(normed1_all, w_z)
    gain = group(gate_norm, 0, d_ssm, 0)[None, :]
    sig_z = jax.nn.sigmoid(gate_z)
    silu_z = gate_z * sig_z
    mixed_y = y_low * silu_z
    squares = jnp.sum(mixed_y * mixed_y, axis=-1)
    squares = squares + swap(squares, "hd", 1)
    inv = lax.rsqrt(squares / d_ssm + eps_norm)[:, None]
    gated_low = (mixed_y * inv * gain).astype(low_type)
    branches = jnp.concatenate([gated_low, att_low], axis=1)
    partial = dot(branches, w_out).reshape(n_hd, tok_count, d_model)
    x_mid = x_in + fold(partial, "hd", 1, 0)

    normed2, norm2_pull = jax.vjp(rms_norm, x_mid, norm2)
    normed2_low = normed2.astype(low_type)
    gate_up = dot(normed2_low, w_gate_up)

    def swiglu(both_halves):
        return jax.nn.silu(both_halves[:, :FF]) * both_halves[:, FF:]

    hidden, swiglu_pull = jax.vjp(swiglu, gate_up)
    hidden_low = hidden.astype(low_type)
    result_seq = x_mid + dot(hidden_low, w_back)

    grad_out_low = cotangent[0]
    grad_hidden = dot_t(grad_out_low, w_back)
    grad_gate_up = swiglu_pull(grad_hidden)[0].astype(low_type)
    grad_normed2 = dot_t(grad_gate_up, w_gate_up)
    grad_mid_part, g_norm2 = norm2_pull(grad_normed2)
    grad_mid = grad_out_low.astype(f32) + grad_mid_part
    grad_mid_all = gather_pair(grad_mid.astype(low_type), "hd", 0)

    def rows_by_owner(grad):
        rows, cols = grad.shape
        return grad.reshape(2, n_cp, n_hd, rows // (2 * n_cp * n_hd), cols)

    g_down = t_dot(hidden_low, grad_out_low).astype(low_type)
    g_down = fold(rows_by_owner(g_down), "dp", 1, 0).astype(low_type)
    g_down = fold_cp(g_down, low_first()).astype(low_type)
    s_down = fold(g_down, "hd", 1, 0)
    g_gate_up = t_dot(normed2_low, grad_gate_up).astype(low_type)
    g_gate_up = fold(rows_by_owner(g_gate_up), "dp", 1, 0).astype(low_type)
    g_gate_up = fold(g_gate_up, "hd", 1, 1).astype(low_type)
    s_gu = fold_cp(g_gate_up, low_first())

    grad_branches = dot_t(grad_mid_all, w_out)
    grad_gated = grad_branches[:, :x_part]
    grad_att = grad_branches[:, x_part:].reshape(span, q_heads, HDIM).swapaxes(0, 1)
    grad_att = grad_att.astype(low_type)
    delta = jnp.sum(grad_att.astype(f32) * att_f32, axis=-1)
    grad_att_wide = jnp.concatenate([jnp.zeros_like(grad_att), grad_att], axis=-1)

    g_out = t_dot(branches, grad_mid_all).astype(low_type)
    g_out = jnp.concatenate(
        [
            g_out[:x_part].reshape(n_cp, n_hd, mo_rows // n_hd, d_model),
            g_out[x_part:].reshape(n_cp, n_hd, ao_rows // n_hd, d_model),
        ],
        axis=2,
    )
    g_out = fold_cp(fold(g_out, "dp", 1, 1).astype(low_type), low_first())
    s_out = lax.ppermute(g_out, ("dp", "hd"), [(0, 0), (1, 2), (2, 1), (3, 3)])
    s_mo, s_ao = s_out[: mo_rows // n_hd], s_out[mo_rows // n_hd :]

    gain_grad = grad_gated * gain
    along = jnp.sum(gain_grad * mixed_y, axis=-1)
    along = along + swap(along, "hd", 1)
    grad_mixed = inv * gain_grad - mixed_y * (inv * inv * inv * (along / d_ssm)[:, None])
    g_gain = jnp.sum(grad_gated * mixed_y * inv, axis=0)
    grad_y = (grad_mixed * silu_z).astype(low_type).astype(f32)
    grad_z = (grad_mixed * y_low * sig_z * (1.0 + gate_z * (1.0 - sig_z))).astype(low_type)

    scaled_dy = jnp.exp(csx_dev) * grad_y
    future = state_scan(log_dev, t_dot(c_conv, scaled_dy, highest), False)

    dq_wide, dkv = attention_backward(
        where, q_wide, grad_att_wide, kv_all, doc_begin, lse, delta
    )
    dkv = fold_cp(dkv.astype(low_type).reshape(n_cp, span, 2 * HDIM), low_first())
    dq = dq_wide[:, :, :HDIM].swapaxes(0, 1) * score_scale
    dqk = turn(jnp.concatenate([dq, dkv[:, None, :HDIM]], axis=1), cosines, -sines)
    grad_late = jnp.concatenate(
        [grad_z, dqk.reshape(span, q_part + k_part).astype(low_type), dkv[:, HDIM:].astype(low_type)],
        axis=1,
    )

    def reduced(grad):
        grad = t_dot(normed1_all, grad).astype(low_type)
        grad = grad.reshape(2, n_cp, d_model // (2 * n_cp), grad.shape[1])
        grad = fold(grad, "dp", 1, 0).astype(low_type)
        split = (grad.shape[-1] // 256) * 128
        return jnp.concatenate(
            [
                fold_cp(grad[..., :split], low_first()),
                fold_cp(grad[..., split:], low_last()),
            ],
            axis=-1,
        ).astype(low_type)

    r_late = reduced(grad_late)

    dxd, db, dc = ssd_backward(xd, grad_y, b_conv, c_conv, cs, cst, csx, before, future)

    def per_head(values):
        return jnp.sum(values.reshape(span, heads, HDIM), axis=-1)

    ddt_direct = per_head(x_conv * dxd)
    dcs = per_head(grad_y * y_core) - dt_value * ddt_direct
    state_end = jnp.exp(csx_dev[-1:]) * state_in + state_local
    end_term = jnp.sum((future * state_end).sum(axis=0).reshape(heads, HDIM), axis=-1)
    ones_up = jnp.triu(jnp.ones((span, span), f32))
    da = dot(ones_up, dcs, highest) + end_term[None, :]
    g_skip = jnp.sum(per_head(grad_y * x_conv), axis=0)
    grad_padded, grad_taps, grad_shift, grad_dt, grad_dt_shift, grad_log = prep_pull(
        (
            dtx * dxd + skip_x * grad_y,
            db,
            dc,
            ddt_direct + decay_rate[None, :] * da,
            jnp.sum(da * dt_value, axis=0),
        )
    )
    rim_back = shifted(grad_padded[: tap_count - 1], "cp", -1)
    grad_conv_in = jnp.concatenate(
        [
            grad_padded[tap_count - 1 : span],
            grad_padded[span:] + rim_back,
        ],
        axis=0,
    )
    grad_early = jnp.concatenate(
        [
            grad_conv_in.astype(low_type),
            grad_dt.astype(low_type),
            jnp.zeros((span, dt_pad), low_type),
        ],
        axis=1,
    )
    r_early = reduced(grad_early)

    conv_cols = x_part + bc_width
    qkv_cols = q_part + 2 * k_part
    grad_normed1 = (
        dot_t(grad_late[:, :x_part], w_z)
        + dot_t(grad_late[:, x_part:], w_early[:, conv_cols : conv_cols + qkv_cols])
        + dot_t(grad_early[:, :conv_cols], w_early[:, :conv_cols])
        + dot_t(grad_early[:, conv_cols:], w_early[:, conv_cols + qkv_cols :])
    )
    grad_normed1 = fold(grad_normed1.reshape(n_hd, tok_count, d_model), "hd", 1, 0)
    _, norm1_pull = jax.vjp(rms_norm, x_in, norm1)
    grad_x_part, g_norm1 = norm1_pull(grad_normed1)
    grad_tokens_out = (grad_mid + grad_x_part).astype(low_type)

    reduced_in = jnp.concatenate([r_late, r_early], axis=1)
    own_rows = reduced_in.shape[0] // n_hd
    halves = reduced_in.reshape(n_hd, own_rows, reduced_in.shape[1])
    got = swap(jnp.where(hd_high, halves[0], halves[1]), "hd", 1)
    mine = jnp.where(hd_high, halves[1], halves[0])
    group0 = jnp.where(hd_high, got, mine).astype(f32)
    group1 = jnp.where(hd_high, mine, got).astype(f32)

    def both(begin, width):
        return [group0[:, begin : begin + width], group1[:, begin : begin + width]]

    late_cols = x_part + qkv_cols
    bc0, bc1 = both(late_cols + x_part, bc_width)
    s_in = jnp.concatenate(
        both(0, x_part)
        + both(late_cols, x_part)
        + [bc0 + bc1]
        + both(x_part, q_part)
        + both(x_part + q_part, k_part)
        + both(x_part + q_part + k_part, k_part),
        axis=1,
    )
    s_dt = jnp.concatenate(both(late_cols + conv_cols, heads), axis=1)

    def placed(values, width):
        full = jnp.zeros(values.shape[:-1] + (width,), f32)
        return lax.dynamic_update_slice_in_dim(
            full, values, hd_index * values.shape[-1], values.ndim - 1
        )

    g_conv_w = jnp.concatenate([placed(grad_taps[:, :x_part], d_ssm), grad_taps[:, x_part:]], axis=1)
    g_conv_b = jnp.concatenate([placed(grad_shift[:x_part], d_ssm), grad_shift[x_part:]], axis=0)
    small = [
        g_norm1,
        g_norm2,
        placed(g_gain, d_ssm),
        g_conv_w,
        g_conv_b,
        placed(grad_dt_shift, HM),
        placed(grad_log, HM),
        placed(g_skip, HM),
    ]
    flat = jnp.concatenate([s.reshape(-1) for s in small])
    length = flat.shape[0]
    flat = jnp.pad(flat, (0, -length % 1024)).reshape(-1, 128)
    flat = flat + swap(flat, "dp", 1)
    flat = flat + swap(flat, "hd", 1)
    for bit in low_first():
        flat = flat + swap(flat, "cp", bit)
    flat = flat.reshape(-1)
    sums = []
    begin = 0
    for s in small:
        sums.append(flat[begin : begin + s.size].reshape(s.shape))
        begin += s.size
    return (
        result_seq.astype(low_type)[None],
        grad_tokens_out[None],
        s_in,
        s_dt,
        s_mo,
        s_ao,
        s_gu,
        s_down,
        *sums,
    )


def solution(mesh):
    weight = P(("dp", "cp"), None)
    grad = P(("dp", "cp", "hd"), None)
    seq = P("dp", ("cp", "hd"), None)
    in_specs = (seq, P("dp", None), seq) + (weight,) * 6 + (P(),) * 8
    out_specs = (seq, seq) + (grad,) * 6 + (P(),) * 8
    return jax.shard_map(
        per_device, mesh=mesh, in_specs=in_specs, out_specs=out_specs, check_vma=False
    )
```

time: 2180 us -> 830 us (0.38)
  waiting for transfers between devices: 1590 us -> 282 us
  starting transfers between devices: 20.9 us -> 160 us
  matrix products: 198 us -> 67.6 us
  blocking collectives: 115 us -> 0 us
  Pallas kernels: 0 us -> 51.6 us
  other arithmetic: 104 us -> 148 us
    reduce_scatter x6 -> x0, waiting for transfers between devices: 1230 us -> none  [the longest x1 360 us: per_device(): lax.psum_scatter(g_gate_up, ('dp', 'cp', 'hd'), scatter_dimension=0, tile...]
    ppermute x0 -> x76, waiting for transfers between devices: none -> 282 us  [the longest x75 282 us: swap(): return lax.ppermute(value, axis, [(i, i ^ bit) for i in range(count)])]
    all_gather x8 -> x0, waiting for transfers between devices: 234 us -> none  [the longest x1 77.7 us: per_device(): lax.all_gather(w_in, ('dp', 'cp'), axis=0, tiled=True)]
    ppermute x0 -> x76, starting transfers between devices: none -> 155 us  [the longest x75 154 us: swap(): return lax.ppermute(value, axis, [(i, i ^ bit) for i in range(count)])]
    dot_general x25 -> x7, matrix products: 101 us -> 18.5 us  [the longest x6 17.9 us: dot(): return jnp.dot(left, right, preferred_element_type=f32, precision=precision)]
    unnamed x16 -> x0, waiting for transfers between devices: 69.9 us -> none
    pallas_call x0 -> x4, Pallas kernels: none -> 51.6 us  [the longest x1 21.1 us: ssd_backward(): pl.pallas_call(ssd_bwd_kernel, grid=(blocks,), in_specs=[rows(width), row...]
    all_gather x2 -> x0, blocking collectives: 49.5 us -> none  [the longest x1 30.4 us: per_device(): lax.all_gather(w_dt, ('dp', 'cp'), axis=0, tiled=True)]
  transfers between devices with their start and end apart: 21 -> 78, of which waited for: 17 -> 38; matrix products, arithmetic and copies ran while one was open for 16% -> 33% of each run, Pallas kernels for 0% -> 6%
where the time goes in v1:
time: 830 us; the launch traced here: 824 us
  waiting for transfers between devices  282 us (34%)
  starting transfers between devices  160 us (19%)
  other arithmetic  148 us (18%)
  local copies, waits for them, and re-layouts  108 us (13%)
  matrix products  67.6 us (8%)
  Pallas kernels  51.6 us (6%)
    ppermute x75, waiting for transfers between devices, swap(): return lax.ppermute(value, axis, [(i, i ^ bit) for i in range(count)])  282 us
    ppermute x75, starting transfers between devices, swap(): return lax.ppermute(value, axis, [(i, i ^ bit) for i in range(count)])  154 us
    unnamed x364, local copies, waits for them, and re-layouts  26 us
    dot_general x7, matrix products, t_dot(): lax.dot_general(left, right, (((0,), (0,)), ((), ())), preferred_element_...  25 us
    dot_general x7, matrix products, dot_t(): lax.dot_general(left, right, (((1,), (1,)), ((), ())), preferred_element_...  24.1 us
    pallas_call x1, Pallas kernels, ssd_backward(): pl.pallas_call(ssd_bwd_kernel, grid=(blocks,), in_specs=[rows(width), row...  21.1 us
    dot_general x6, matrix products, dot(): return jnp.dot(left, right, preferred_element_type=f32, precision=precision)  17.9 us
  transfers between devices with their start and end apart: 78, of which 38 were waited for; matrix products, arithmetic and copies ran while one was open for 33% of the time, Pallas kernels for 6%

profile of v1, /device:TPU:0, one launch (start us, length us, event | category | flops | bytes accessed | tf_op | source)
XLA Modules:
  0.0 824.3 jit_solution(18087476489334600314)
XLA Ops:
  8.2 9.1 %collective-permute-done.1 = bf16[1,64,1536]{2,1,0:T(8,128)(2,1)S(1)} collective-permute-done((bf16[1,64,1536]{2,1,0:T(8,128)(2,1)S(1)}, bf16[1,64,1536]{2,1,0:T(8,128)(2,1)S(1)}, u32[]{:S(2)}, u32[]{:S(2)}) %collective-permute-start.1) | collective-permute-done | bytes 196640 | tf_op jit(solution)/shard_map/ppermute | solution.py:29
  33.4 12.5 %collective-permute-done.3 = bf16[4,64,1536]{2,1,0:T(8,128)(2,1)S(1)} collective-permute-done((bf16[4,64,1536]{2,1,0:T(8,128)(2,1)S(1)}, bf16[4,64,1536]{2,1,0:T(8,128)(2,1)S(1)}, u32[]{:S(2)}, u32[]{:S(2)}) %collective-permute-start.3) | collective-permute-done | bytes 786464 | tf_op jit(solution)/shard_map/ppermute | solution.py:29
  60.9 8.4 %collective-permute-done.9 = bf16[1,64,768]{2,1,0:T(8,128)(2,1)S(1)} collective-permute-done((bf16[1,64,768]{2,1,0:T(8,128)(2,1)S(1)}, bf16[1,64,768]{2,1,0:T(8,128)(2,1)S(1)}, u32[]{:S(2)}, u32[]{:S(2)}) %collective-permute-start.9) | collective-permute-done | bytes 98336 | tf_op jit(solution)/shard_map/ppermute | solution.py:29
  89.7 8.4 %collective-permute-done.20 = bf16[4,128,512]{2,1,0:T(8,128)(2,1)S(1)} collective-permute-done((bf16[4,128,512]{2,1,0:T(8,128)(2,1)S(1)}, bf16[4,128,512]{2,1,0:T(8,128)(2,1)S(1)}, u32[]{:S(2)}, u32[]{:S(2)}) %collective-permute-start.20) | collective-permute-done | bytes 524320 | tf_op jit(solution)/shard_map/ppermute | solution.py:29
  106.0 8.9 %collective-permute-done.23 = bf16[1,64,2048]{2,1,0:T(8,128)(2,1)S(1)} collective-permute-done((bf16[1,64,2048]{2,1,0:T(8,128)(2,1)S(1)}, bf16[1,64,2048]{2,1,0:T(8,128)(2,1)S(1)}, u32[]{:S(2)}, u32[]{:S(2)}) %collective-permute-start.23) | collective-permute-done | bytes 262176 | tf_op jit(solution)/shard_map/ppermute | solution.py:29
  203.9 11.0 %ssd_forward.1 = (f32[640,768]{1,0:T(8,128)}, f32[5,128,768]{2,1,0:T(8,128)}) custom-call(f32[640,768]{1,0:T(8,128)} %copy-done.40, f32[640,128]{1,0:T(8,128)} %get-tuple-element.190.b_ref, f32[640,128]{1,0:T(8,128)} %get-tuple-element.189.c_ref, f32[640,12]{1,0:T(8,128)} %bitcast.665, f32[5,12,128]{2,1,0:T(8,128)} %copy-done.100, ...), custom_call_target="tpu_custom_call" | custom-call | flops 2264924160 | bytes 9830400 | tf_op jit(solution)/shard_map/ssd_forward/pallas_call | solution.py:444
  244.2 27.1 %collective-permute-done.26 = bf16[512,2048]{1,0:T(8,128)(2,1)S(1)} collective-permute-done((bf16[512,2048]{1,0:T(8,128)(2,1)S(1)}, bf16[512,2048]{1,0:T(8,128)(2,1)S(1)}, u32[]{:S(2)}, u32[]{:S(2)}) %collective-permute-start.26) | collective-permute-done | bytes 2097184 | tf_op jit(solution)/shard_map/ppermute | solution.py:29
  274.6 8.6 %attention_forward.1 = (f32[4,640,128]{2,1,0:T(8,128)}, f32[4,640,1]{2,1,0:T(8,128)}) custom-call(s32[2]{0:T(128)} %pad_add_fusion.4.where_ref, bf16[4,640,128]{2,1,0:T(8,128)(2,1)} %concatenate.159.q_ref, bf16[5120,128]{1,0:T(8,128)(2,1)} %bitcast.662, s32[640,1]{1,0:T(8,128)} %reshape.693.start_ref), custom_call_target="tpu_custom_call" | custom-call | flops 26843545600 | bytes 2621440 | tf_op jit(solution)/shard_map/attention_forward/pallas_call | solution.py:286
  283.1 7.2 collective-permute-done.31
  306.3 13.1 %collective-permute-done.22 = bf16[320,1024]{1,0:T(8,128)(2,1)} collective-permute-done((bf16[320,1024]{1,0:T(8,128)(2,1)}, bf16[320,1024]{1,0:T(8,128)(2,1)}, u32[]{:S(2)}, u32[]{:S(2)}) %collective-permute-start.22) | collective-permute-done | bytes 655392 | tf_op jit(solution)/shard_map/ppermute | solution.py:29
  333.2 7.1 fusion.116
  340.3 6.4 multiply_reduce_fusion.8
  346.7 8.2 convolution_convert_fusion
  383.8 10.9 %attention_backward.1 = (f32[4,640,128]{2,1,0:T(8,128)}, f32[5120,128]{1,0:T(8,128)}) custom-call(s32[2]{0:T(128)} %pad_add_fusion.4.where_ref, bf16[4,640,128]{2,1,0:T(8,128)(2,1)} %concatenate.159.q_ref, bf16[4,640,128]{2,1,0:T(8,128)(2,1)} %concatenate.170.do_ref, bf16[5120,128]{1,0:T(8,128)(2,1)} %bitcast.663, s32[1,640]{1,0:T(1,128)} %reshape.637.start_ref, ...), custom_call_target="tpu_custom_call" | custom-call | flops 67108864000 | bytes 2621440 | tf_op jit(solution)/shard_map/attention_backward/pallas_call | solution.py:313
  398.5 7.5 collective-permute-start.35
  416.7 9.4 %collective-permute-done.38 = bf16[144,768]{1,0:T(8,128)(2,1)S(1)} collective-permute-done((bf16[144,768]{1,0:T(8,128)(2,1)}, bf16[144,768]{1,0:T(8,128)(2,1)S(1)}, u32[]{:S(2)}, u32[]{:S(2)}) %collective-permute-start.38) | collective-permute-done | bytes 221216 | tf_op jit(solution)/shard_map/ppermute | solution.py:29
  429.5 21.0 %collective-permute-start.39 = (bf16[144,768]{1,0:T(8,128)(2,1)}, bf16[144,768]{1,0:T(8,128)(2,1)}, u32[]{:S(2)}, u32[]{:S(2)}) collective-permute-start(bf16[144,768]{1,0:T(8,128)(2,1)} %maximum_maximum_fusion.2), channel_id=1, source_target_pairs={{0,4},{2,6},{4,0},{6,2},{8,12},{10,14},{12,8},{14,10},{1,5},{3,7},... | collective-permute-start | bytes 663560 | tf_op jit(solution)/shard_map/ppermute | solution.py:29
  458.9 51.1 %collective-permute-start.40 = (bf16[144,768]{1,0:T(8,128)(2,1)S(1)}, bf16[144,768]{1,0:T(8,128)(2,1)S(1)}, u32[]{:S(2)}, u32[]{:S(2)}) collective-permute-start(bf16[144,768]{1,0:T(8,128)(2,1)S(1)} %maximum_maximum_fusion.3), channel_id=1, source_target_pairs={{0,8},{2,10},{4,12},{6,14},{8,0},{10,2},{12,4},{14,6},{1,9},{3,11}... | collective-permute-start | bytes 663560 | tf_op jit(solution)/shard_map/ppermute | solution.py:29
  521.7 21.1 %ssd_backward.1 = (f32[640,768]{1,0:T(8,128)}, f32[640,128]{1,0:T(8,128)}, f32[640,128]{1,0:T(8,128)}) custom-call(f32[640,768]{1,0:T(8,128)} %copy-done.40, f32[640,768]{1,0:T(8,128)} %convert_element_type.699.dy_ref, f32[640,128]{1,0:T(8,128)} %get-tuple-element.190.b_ref, f32[640,128]{1,0:T(8,128)} %get-tuple-element.189.c_ref, f32[640,12]{1,0:T(8,128)} %bitcast.666, ...), custom_call_target="tpu_custom_call" | custom-call | flops 6039797760 | bytes 11796480 | tf_op jit(solution)/shard_map/ssd_backward/pallas_call | solution.py:481
  698.3 6.6 collective-permute-done.56
  709.4 17.4 %collective-permute-done.45 = bf16[2,64,512]{2,1,0:T(8,128)(2,1)S(1)} collective-permute-done((bf16[2,64,512]{2,1,0:T(8,128)(2,1)S(1)}, bf16[2,64,512]{2,1,0:T(8,128)(2,1)S(1)}, u32[]{:S(2)}, u32[]{:S(2)}) %collective-permute-start.45) | collective-permute-done | bytes 131104 | tf_op jit(solution)/shard_map/ppermute | solution.py:29
  740.9 38.0 %collective-permute-done.64 = bf16[8,32,4096]{2,1,0:T(8,128)(2,1)S(1)} collective-permute-done((bf16[8,32,4096]{2,1,0:T(8,128)(2,1)S(1)}, bf16[8,32,4096]{2,1,0:T(8,128)(2,1)S(1)}, u32[]{:S(2)}, u32[]{:S(2)}) %collective-permute-start.64) | collective-permute-done | bytes 2097184 | tf_op jit(solution)/shard_map/ppermute | solution.py:29
  781.3 20.3 %collective-permute-done.65 = bf16[2,2,32,4096]{3,2,1,0:T(8,128)(2,1)S(1)} collective-permute-done((bf16[2,2,32,4096]{3,2,1,0:T(8,128)(2,1)S(1)}, bf16[2,2,32,4096]{3,2,1,0:T(8,128)(2,1)S(1)}, u32[]{:S(2)}, u32[]{:S(2)}) %collective-permute-start.65) | collective-permute-done | bytes 1048608 | tf_op jit(solution)/shard_map/ppermute | solution.py:29
  803.1 10.1 %collective-permute-done.66 = bf16[2,32,4096]{2,1,0:T(8,128)(2,1)S(1)} collective-permute-done((bf16[2,32,4096]{2,1,0:T(8,128)(2,1)S(1)}, bf16[2,32,4096]{2,1,0:T(8,128)(2,1)S(1)}, u32[]{:S(2)}, u32[]{:S(2)}) %collective-permute-start.66) | collective-permute-done | bytes 524320 | tf_op jit(solution)/shard_map/ppermute | solution.py:29
  (884 shorter events, 468.5 us)
Async XLA Ops:
  18.2 65.9 %collective-permute-start = (bf16[320,1024]{1,0:T(8,128)(2,1)S(1)}, bf16[320,1024]{1,0:T(8,128)(2,1)}, u32[]{:S(2)}, u32[]{:S(2)}) collective-permute-start(bf16[320,1024]{1,0:T(8,128)(2,1)S(1)} %bitcast.626), channel_id=1, source_target_pairs={{0,1},{1,0},{2,3},{3,2},{4,5},{5,4},{6,7},{7,6},{8,9},{9,8},{10,11... | collective-permute-start | bytes 1966088 | tf_op jit(solution)/shard_map/ppermute | solution.py:29
  85.7 32.0 %collective-permute-start.4 = (bf16[512,1536]{1,0:T(8,128)(2,1)S(1)}, bf16[512,1536]{1,0:T(8,128)(2,1)S(1)}, u32[]{:S(2)}, u32[]{:S(2)}) collective-permute-start(bf16[512,1536]{1,0:T(8,128)(2,1)S(1)} %bitcast.625), channel_id=1, source_target_pairs={{0,16},{16,0},{1,17},{17,1},{2,18},{18,2},{3,19},{19,3},{4,20},{20... | collective-permute-start | bytes 4718600 | tf_op jit(solution)/shard_map/ppermute | solution.py:29
  105.5 91.9 %collective-permute-start.21 = (bf16[1024,512]{1,0:T(8,128)(2,1)}, bf16[1024,512]{1,0:T(8,128)(2,1)}, u32[]{:S(2)}, u32[]{:S(2)}) collective-permute-start(bf16[1024,512]{1,0:T(8,128)(2,1)} %bitcast.66), channel_id=1, source_target_pairs={{0,16},{16,0},{1,17},{17,1},{2,18},{18,2},{3,19},{19,3},{4,20},{20... | collective-permute-start | bytes 3145736 | tf_op jit(solution)/shard_map/ppermute | solution.py:29
  115.9 67.9 %collective-permute-start.24 = (bf16[2,64,2048]{2,1,0:T(8,128)(2,1)}, bf16[2,64,2048]{2,1,0:T(8,128)(2,1)}, u32[]{:S(2)}, u32[]{:S(2)}) collective-permute-start(bf16[2,64,2048]{2,1,0:T(8,128)(2,1)} %maximum_bitcast_fusion), channel_id=1, source_target_pairs={{0,4},{2,6},{4,0},{6,2},{8,12},{10,14},{12,8},{14,10},{1,5},{3,7},... | collective-permute-start | bytes 1572872 | tf_op jit(solution)/shard_map/ppermute | solution.py:29
  196.3 38.3 %collective-permute-start.16 = (bf16[4,640,128]{2,1,0:T(8,128)(2,1)}, bf16[4,640,128]{2,1,0:T(8,128)(2,1)}, u32[]{:S(2)}, u32[]{:S(2)}) collective-permute-start(bf16[4,640,128]{2,1,0:T(8,128)(2,1)} %bitcast.50), channel_id=1, source_target_pairs={{0,2},{2,0},{4,6},{6,4},{8,10},{10,8},{12,14},{14,12},{1,3},{3,1},... | collective-permute-start | bytes 1966088 | tf_op jit(solution)/shard_map/ppermute | solution.py:29
  222.7 48.6 %collective-permute-start.26 = (bf16[512,2048]{1,0:T(8,128)(2,1)S(1)}, bf16[512,2048]{1,0:T(8,128)(2,1)S(1)}, u32[]{:S(2)}, u32[]{:S(2)}) collective-permute-start(bf16[512,2048]{1,0:T(8,128)(2,1)S(1)} %bitcast.618), channel_id=1, source_target_pairs={{0,1},{1,0},{2,3},{3,2},{4,5},{5,4},{6,7},{7,6},{8,9},{9,8},{10,11... | collective-permute-start | bytes 6291464 | tf_op jit(solution)/shard_map/ppermute | solution.py:29
  242.6 47.7 %collective-permute-start.31 = (bf16[1024,512]{1,0:T(8,128)(2,1)S(1)}, bf16[1024,512]{1,0:T(8,128)(2,1)S(1)}, u32[]{:S(2)}, u32[]{:S(2)}) collective-permute-start(bf16[1024,512]{1,0:T(8,128)(2,1)S(1)} %bitcast.647), channel_id=1, source_target_pairs={{0,1},{1,0},{2,3},{3,2},{4,5},{5,4},{6,7},{7,6},{8,9},{9,8},{10,11... | collective-permute-start | bytes 3145736 | tf_op jit(solution)/shard_map/ppermute | solution.py:29
  274.6 50.8 %collective-permute-start.27 = (bf16[512,4096]{1,0:T(8,128)(2,1)}, bf16[512,4096]{1,0:T(8,128)(2,1)}, u32[]{:S(2)}, u32[]{:S(2)}) collective-permute-start(bf16[512,4096]{1,0:T(8,128)(2,1)} %pad_maximum_fusion.3), channel_id=1, source_target_pairs={{0,16},{16,0},{1,17},{17,1},{2,18},{18,2},{3,19},{19,3},{4,20},{20... | collective-permute-start | bytes 12582920 | tf_op jit(solution)/shard_map/ppermute | solution.py:29
  292.7 29.9 %collective-permute-start.32 = (bf16[1024,1024]{1,0:T(8,128)(2,1)}, bf16[1024,1024]{1,0:T(8,128)(2,1)}, u32[]{:S(2)}, u32[]{:S(2)}) collective-permute-start(bf16[1024,1024]{1,0:T(8,128)(2,1)} %pad_maximum_fusion.12), channel_id=1, source_target_pairs={{0,16},{16,0},{1,17},{17,1},{2,18},{18,2},{3,19},{19,3},{4,20},{20... | collective-permute-start | bytes 6291464 | tf_op jit(solution)/shard_map/ppermute | solution.py:29
  360.9 260.7 %collective-permute-start.68 = (bf16[8,2,64,1024]{3,2,1,0:T(8,128)(2,1)}, bf16[8,2,64,1024]{3,2,1,0:T(8,128)(2,1)}, u32[]{:S(2)}, u32[]{:S(2)}) collective-permute-start(bf16[8,2,64,1024]{3,2,1,0:T(8,128)(2,1)} %bitcast.186), channel_id=1, source_target_pairs={{0,16},{16,0},{1,17},{17,1},{2,18},{18,2},{3,19},{19,3},{4,20},{20... | collective-permute-start | bytes 6291464 | tf_op jit(solution)/shard_map/ppermute | solution.py:29
  365.5 361.6 %collective-permute-start.63 = (bf16[8,2,32,4096]{3,2,0,1:T(8,128)(2,1)}, bf16[8,2,32,4096]{3,2,0,1:T(8,128)(2,1)}, u32[]{:S(2)}, u32[]{:S(2)}) collective-permute-start(bf16[8,2,32,4096]{3,2,0,1:T(8,128)(2,1)} %copy.488), channel_id=1, source_target_pairs={{0,16},{16,0},{1,17},{17,1},{2,18},{18,2},{3,19},{19,3},{4,20},{20... | collective-permute-start | bytes 12582920 | tf_op jit(solution)/shard_map/ppermute | solution.py:29
  377.2 28.9 %collective-permute-start.34 = (f32[640]{0:T(1024)S(1)}, f32[640]{0:T(1024)S(1)}, u32[]{:S(2)}, u32[]{:S(2)}) collective-permute-start(f32[640]{0:T(1024)S(1)} %get-tuple-element.131), channel_id=1, source_target_pairs={{0,1},{1,0},{2,3},{3,2},{4,5},{5,4},{6,7},{7,6},{8,9},{9,8},{10,11... | collective-permute-start | bytes 7688 | tf_op jit(solution)/shard_map/ppermute | solution.py:29
  383.7 210.1 %collective-permute-start.58 = (bf16[8,64,1024]{2,1,0:T(8,128)(2,1)}, bf16[8,64,1024]{2,1,0:T(8,128)(2,1)}, u32[]{:S(2)}, u32[]{:S(2)}) collective-permute-start(bf16[8,64,1024]{2,1,0:T(8,128)(2,1)} %select_bitcast_fusion.1), channel_id=1, source_target_pairs={{0,16},{16,0},{1,17},{17,1},{2,18},{18,2},{3,19},{19,3},{4,20},{20... | collective-permute-start | bytes 3145736 | tf_op jit(solution)/shard_map/ppermute | solution.py:29
  398.5 111.6 %collective-permute-start.35 = (bf16[2,2,640,128]{3,2,0,1:T(8,128)(2,1)}, bf16[2,2,640,128]{3,2,0,1:T(8,128)(2,1)}, u32[]{:S(2)}, u32[]{:S(2)}) collective-permute-start(bf16[2,2,640,128]{3,2,0,1:T(8,128)(2,1)} %select_bitcast_fusion.6), channel_id=1, source_target_pairs={{0,2},{2,0},{4,6},{6,4},{8,10},{10,8},{12,14},{14,12},{1,3},{3,1},... | collective-permute-start | bytes 1966088 | tf_op jit(solution)/shard_map/ppermute | solution.py:29
  458.9 60.9 %collective-permute-start.40 = (bf16[144,768]{1,0:T(8,128)(2,1)S(1)}, bf16[144,768]{1,0:T(8,128)(2,1)S(1)}, u32[]{:S(2)}, u32[]{:S(2)}) collective-permute-start(bf16[144,768]{1,0:T(8,128)(2,1)S(1)} %maximum_maximum_fusion.3), channel_id=1, source_target_pairs={{0,8},{2,10},{4,12},{6,14},{8,0},{10,2},{12,4},{14,6},{1,9},{3,11}... | collective-permute-start | bytes 663560 | tf_op jit(solution)/shard_map/ppermute | solution.py:29
  512.5 76.5 %collective-permute-start.36 = (bf16[2,640,128]{2,1,0:T(8,128)(2,1)}, bf16[2,640,128]{2,1,0:T(8,128)(2,1)}, u32[]{:S(2)}, u32[]{:S(2)}) collective-permute-start(bf16[2,640,128]{2,1,0:T(8,128)(2,1)} %select_bitcast_fusion.20), channel_id=1, source_target_pairs={{0,4},{2,6},{4,0},{6,2},{8,12},{10,14},{12,8},{14,10},{1,5},{3,7},... | collective-permute-start | bytes 983048 | tf_op jit(solution)/shard_map/ppermute | solution.py:29
  584.5 65.4 %collective-permute-start.50 = (bf16[8,64,1152]{2,1,0:T(8,128)(2,1)}, bf16[8,64,1152]{2,1,0:T(8,128)(2,1)}, u32[]{:S(2)}, u32[]{:S(2)}) collective-permute-start(bf16[8,64,1152]{2,1,0:T(8,128)(2,1)} %bitcast.136), channel_id=1, source_target_pairs={{0,16},{16,0},{1,17},{17,1},{2,18},{18,2},{3,19},{19,3},{4,20},{20... | collective-permute-start | bytes 3538952 | tf_op jit(solution)/shard_map/ppermute | solution.py:29
  597.3 29.6 %collective-permute-start.59 = (bf16[2,2,64,1024]{3,2,1,0:T(8,128)(2,1)}, bf16[2,2,64,1024]{3,2,1,0:T(8,128)(2,1)}, u32[]{:S(2)}, u32[]{:S(2)}) collective-permute-start(bf16[2,2,64,1024]{3,2,1,0:T(8,128)(2,1)} %fusion.84), channel_id=1, source_target_pairs={{0,2},{2,0},{4,6},{6,4},{8,10},{10,8},{12,14},{14,12},{1,3},{3,1},... | collective-permute-start | bytes 1572872 | tf_op jit(solution)/shard_map/ppermute | solution.py:29
  618.3 74.3 %collective-permute-start.43 = (bf16[8,64,1152]{2,1,0:T(8,128)(2,1)}, bf16[8,64,1152]{2,1,0:T(8,128)(2,1)}, u32[]{:S(2)}, u32[]{:S(2)}) collective-permute-start(bf16[8,64,1152]{2,1,0:T(8,128)(2,1)} %bitcast.114), channel_id=1, source_target_pairs={{0,16},{16,0},{1,17},{17,1},{2,18},{18,2},{3,19},{19,3},{4,20},{20... | collective-permute-start | bytes 3538952 | tf_op jit(solution)/shard_map/ppermute | solution.py:29
  627.0 78.0 %collective-permute-start.69 = (bf16[2,2,2,64,1024]{4,3,2,1,0:T(8,128)(2,1)}, bf16[2,2,2,64,1024]{4,3,2,1,0:T(8,128)(2,1)}, u32[]{:S(2)}, u32[]{:S(2)}) collective-permute-start(bf16[2,2,2,64,1024]{4,3,2,1,0:T(8,128)(2,1)} %fusion.55), channel_id=1, source_target_pairs={{0,2},{2,0},{4,6},{6,4},{8,10},{10,8},{12,14},{14,12},{1,3},{3,1},... | collective-permute-start | bytes 3145736 | tf_op jit(solution)/shard_map/ppermute | solution.py:29
  706.9 30.7 %collective-permute-start.70 = (bf16[2,2,64,1024]{3,2,1,0:T(8,128)(2,1)S(1)}, bf16[2,2,64,1024]{3,2,1,0:T(8,128)(2,1)S(1)}, u32[]{:S(2)}, u32[]{:S(2)}) collective-permute-start(bf16[2,2,64,1024]{3,2,1,0:T(8,128)(2,1)S(1)} %fusion.86), channel_id=1, source_target_pairs={{0,4},{2,6},{4,0},{6,2},{8,12},{10,14},{12,8},{14,10},{1,5},{3,7},... | collective-permute-start | bytes 1572872 | tf_op jit(solution)/shard_map/ppermute | solution.py:29
  730.8 48.0 %collective-permute-start.64 = (bf16[8,32,4096]{2,1,0:T(8,128)(2,1)S(1)}, bf16[8,32,4096]{2,1,0:T(8,128)(2,1)S(1)}, u32[]{:S(2)}, u32[]{:S(2)}) collective-permute-start(bf16[8,32,4096]{2,1,0:T(8,128)(2,1)S(1)} %select_bitcast_fusion), channel_id=1, source_target_pairs={{0,1},{1,0},{2,3},{3,2},{4,5},{5,4},{6,7},{7,6},{8,9},{9,8},{10,11... | collective-permute-start | bytes 6291464 | tf_op jit(solution)/shard_map/ppermute | solution.py:29
  735.5 45.7 %collective-permute-start.57 = (bf16[32,2304]{1,0:T(8,128)(2,1)S(1)}, bf16[32,2304]{1,0:T(8,128)(2,1)S(1)}, u32[]{:S(2)}, u32[]{:S(2)}) collective-permute-start(bf16[32,2304]{1,0:T(8,128)(2,1)S(1)} %broadcast_select_fusion.27), channel_id=1, source_target_pairs={{0,1},{1,0},{2,3},{3,2},{4,5},{5,4},{6,7},{7,6},{8,9},{9,8},{10,11... | collective-permute-start | bytes 442376 | tf_op jit(solution)/shard_map/ppermute | solution.py:29
  737.9 64.3 %collective-permute-start.71 = (bf16[2,64,1024]{2,1,0:T(8,128)(2,1)S(1)}, bf16[2,64,1024]{2,1,0:T(8,128)(2,1)S(1)}, u32[]{:S(2)}, u32[]{:S(2)}) collective-permute-start(bf16[2,64,1024]{2,1,0:T(8,128)(2,1)S(1)} %select_bitcast_fusion.23), channel_id=1, source_target_pairs={{0,8},{2,10},{4,12},{6,14},{8,0},{10,2},{12,4},{14,6},{1,9},{3,11}... | collective-permute-start | bytes 786440 | tf_op jit(solution)/shard_map/ppermute | solution.py:29
  (233 other events, 2244.2 us)

commit v2 on v1

v2 whole, which is shorter than its diff:
```python
import math

import jax
import jax.numpy as jnp
from jax import lax
from jax.experimental import pallas as pl
from jax.experimental.pallas import tpu as pltpu
from jax.sharding import PartitionSpec as P

HM = 24
HDIM = 64
NST = 128
QH = 8
KVH = 2
FF = 2048

eps_norm = 1e-05
rope_base = 100000000000.0
masked = -1e30
highest = lax.Precision.HIGHEST
low_type = jnp.bfloat16
f32 = jnp.float32
chunk_len = 128
vmem_bytes = 56 * 1024 * 1024


def swap(value, axis, bit):
    count = lax.axis_size(axis)
    return lax.ppermute(value, axis, [(i, i ^ bit) for i in range(count)])


def shifted(value, axis, steps):
    count = lax.axis_size(axis)
    initial, last = (max(0, -steps), min(count, count - steps))
    return lax.ppermute(value, axis, [(source, source + steps) for source in range(initial, last)])


def has_bit(axis, bit):
    return (lax.axis_index(axis) & bit) != 0


def in_order(mine, other, high, dim, join):
    return join([jnp.where(high, other, mine), jnp.where(high, mine, other)], dim)


def gather_cp(value, gates=()):
    rows, cols = value.shape
    held = value[None]
    steps = []
    bit = lax.axis_size("cp") // 2
    while bit:
        ahead = bit.bit_length() - 1
        if ahead < len(gates) and gates[-1 - ahead] is not None:
            held = after(held, gates[-1 - ahead])
        other = swap(held, "cp", bit)
        held = in_order(held, other, has_bit("cp", bit), 1, jnp.stack).reshape(-1, rows, cols)
        steps.append(held)
        bit //= 2
    return held.reshape(-1, cols), steps


def gather_pair(value, axis, dim):
    return in_order(value, swap(value, axis, 1), has_bit(axis, 1), dim, jnp.concatenate)


def fold(value, axis, bit, dim):
    high = has_bit(axis, bit)
    first = lax.index_in_dim(value, 0, dim, False)
    second = lax.index_in_dim(value, 1, dim, False)
    got = swap(jnp.where(high, first, second).astype(low_type), axis, bit)
    return jnp.where(high, second, first).astype(f32) + got.astype(f32)


def fold_cp(value, order, gates=(None,) * 8):
    count = lax.axis_size("cp")
    bits = count.bit_length() - 1
    held = value.reshape((2,) * bits + value.shape[1:])
    left = [1 << (bits - 1 - d) for d in range(bits)]
    steps = []
    for gate, bit in zip(gates, order):
        dim = left.index(bit)
        if gate is not None:
            held = after(held, gate)
        held = fold(held, "cp", bit, dim)
        left.pop(dim)
        if left:
            held = held.astype(low_type)
        steps.append(held)
    return held, steps


def low_first():
    return [1 << d for d in range(lax.axis_size("cp").bit_length() - 1)]


def low_last():
    bits = low_first()
    return bits[1:] + bits[:1]


def after(value, earlier):
    first = lax.slice(earlier, (0,) * earlier.ndim, (1,) * earlier.ndim).reshape(())
    return value + (first.astype(f32) * 0.0).astype(value.dtype)


def state_scan(log_decay, state, forward):
    heads = log_decay.shape[0]
    width = state.shape[1] // heads
    pre_log, pre_state = jnp.zeros_like(log_decay), jnp.zeros_like(state)
    count = lax.axis_size("cp")
    bit = 1

    def spread(values):
        return dot(jnp.exp(values)[None, :], expander(heads, width), highest)

    while bit < count:
        top = log_decay.astype(low_type)
        rest = (log_decay - top.astype(f32)).astype(low_type)
        tail = jnp.concatenate([top, rest, jnp.zeros((state.shape[1] - 2 * heads,), low_type)])
        tail = jnp.concatenate([tail[None], jnp.zeros((15, state.shape[1]), low_type)], axis=0)
        sent = jnp.concatenate([state.astype(low_type), tail], axis=0)
        gate = yield sent
        if gate is not None:
            sent = after(sent, gate)
        got = swap(sent, "cp", bit)
        got_state = got[:-16].astype(f32)
        got_log = got[-16, :heads].astype(f32) + got[-16, heads : 2 * heads].astype(f32)
        joins = has_bit("cp", bit) if forward else jnp.logical_not(has_bit("cp", bit))
        pre_state = jnp.where(joins, spread(pre_log) * got_state + pre_state, pre_state)
        pre_log = jnp.where(joins, pre_log + got_log, pre_log)
        state = jnp.where(
            joins, spread(log_decay) * got_state + state, spread(got_log) * state + got_state
        )
        log_decay = log_decay + got_log
        bit *= 2
    yield pre_state


def rms_norm(values, gain_vec):
    return (
        values * lax.rsqrt(jnp.mean(values * values, axis=-1, keepdims=True) + eps_norm) * gain_vec
    )


def expander(heads, width):
    column = jnp.arange(heads * width, dtype=jnp.int32)[None, :] // width
    return (column == jnp.arange(heads, dtype=jnp.int32)[:, None]).astype(f32)


def half_turner(width):
    column = jnp.arange(width, dtype=jnp.int32)
    half = HDIM // 2
    partner = jnp.where(column % HDIM < half, column + half, column - half)
    return (column[:, None] == partner[None, :]).astype(f32)


def causal_conv(padded, conv_taps, conv_shift):
    tap_count = conv_taps.shape[0]
    out_rows = padded.shape[0] - tap_count + 1
    summed = conv_shift[None, :]
    for tap_index in range(tap_count):
        summed = summed + conv_taps[tap_index][None, :] * padded[tap_index : tap_index + out_rows]
    return summed


def t_dot(left, right, precision=None):
    return lax.dot_general(
        left,
        right,
        (((0,), (0,)), ((), ())),
        preferred_element_type=f32,
        precision=precision,
    )


def dot_t(left, right, precision=None):
    return lax.dot_general(
        left,
        right,
        (((1,), (1,)), ((), ())),
        preferred_element_type=f32,
        precision=precision,
    )


def dot(left, right, precision=None):
    return jnp.dot(left, right, preferred_element_type=f32, precision=precision)


def left_half(shape):
    return lax.broadcasted_iota(jnp.int32, shape, 1) < HDIM


def both_heads(pair):
    left = left_half(pair.shape)
    pair = pair.astype(f32)
    return (
        jnp.where(left, pair, 0.0).astype(low_type),
        jnp.where(left, 0.0, pair).astype(low_type),
    )


def att_fwd_kernel(where_ref, q_ref, kk_ref, vv_ref, start_ref, *rest):
    out_ref, lse_ref, top_s, sum_s, acc_s = rest[-5:]
    span = q_ref.shape[0]
    place = where_ref[0]
    latest = where_ref[1]
    queries = both_heads(q_ref[...])
    top_s[...] = jnp.full(top_s.shape, masked, f32)
    sum_s[...] = jnp.zeros(sum_s.shape, f32)
    acc_s[...] = jnp.zeros(acc_s.shape, f32)

    def block(turn_index, _):
        j = place - turn_index
        base = pl.multiple_of(j * span, span)
        keys = kk_ref[pl.ds(base, span), :]
        values = vv_ref[pl.ds(base, span), :]

        def hide(scores):
            key_pos = base + lax.broadcasted_iota(jnp.int32, scores.shape, 1)
            row_pos = place * span + lax.broadcasted_iota(jnp.int32, scores.shape, 0)
            return jnp.where((key_pos <= row_pos) & (key_pos >= start_ref[...]), scores, masked)

        def work(shape_scores):
            for e in range(2):
                scores = shape_scores(dot_t(queries[e], keys))
                old_top = top_s[e]
                new_top = jnp.maximum(old_top, jnp.max(scores, axis=1, keepdims=True))
                weights = jnp.exp(scores - new_top)
                fall = jnp.exp(old_top - new_top)
                sum_s[e] = sum_s[e] * fall + jnp.sum(weights, axis=1, keepdims=True)
                acc_s[e] = acc_s[e] * fall + dot(weights.astype(low_type), values)
                top_s[e] = new_top

        needs = (j == place) | (latest > base)

        @pl.when(needs)
        def _():
            work(hide)

        @pl.when(jnp.logical_not(needs))
        def _():
            work(lambda scores: scores)

        return 0

    lax.fori_loop(0, place + 1, block, 0)
    outs = [acc_s[e] / sum_s[e] for e in range(2)]
    out_ref[...] = jnp.where(left_half(outs[0].shape), outs[0], outs[1])
    for e in range(2):
        lse_ref[e] = top_s[e] + jnp.log(sum_s[e])


def att_bwd_kernel(
    where_ref, q_ref, do_ref, kk_ref, vv_ref, start_ref, lse_ref, delta_ref, *rest
):
    dq_ref, dkv_ref, dq_s = rest[-3:]
    span = q_ref.shape[0]
    place = where_ref[0]
    latest = where_ref[1]
    queries = both_heads(q_ref[...])
    grads = both_heads(do_ref[...])
    dq_s[...] = jnp.zeros(dq_s.shape, f32)

    def block(j, _):
        base = pl.multiple_of(j * span, span)
        keys = kk_ref[pl.ds(base, span), :]
        values = vv_ref[pl.ds(base, span), :]

        def hide(scores):
            key_pos = base + lax.broadcasted_iota(jnp.int32, scores.shape, 0)
            row_pos = place * span + lax.broadcasted_iota(jnp.int32, scores.shape, 1)
            return jnp.where((key_pos <= row_pos) & (key_pos >= start_ref[...]), scores, masked)

        def work(shape_scores):
            dkk, dvv = [], []
            for e in range(2):
                scores = shape_scores(dot_t(keys, queries[e]))
                grad_probs = dot_t(values, grads[e])
                probs = jnp.exp(scores - lse_ref[e])
                grad_scores = (probs * (grad_probs - delta_ref[e])).astype(low_type)
                dq_s[e] += t_dot(grad_scores, keys)
                dkk.append(dot(grad_scores, queries[e]))
                dvv.append(dot(probs.astype(low_type), grads[e]))
            dkk, dvv = dkk[0] + dkk[1], dvv[0] + dvv[1]
            dkk = dkk + pltpu.roll(dkk, HDIM, 1)
            dvv = dvv + pltpu.roll(dvv, HDIM, 1)
            dkv_ref[pl.ds(base, span), :] = jnp.where(left_half(dkk.shape), dkk, dvv).astype(
                low_type
            )

        needs = (j == place) | (latest > base)

        @pl.when(needs)
        def _():
            work(hide)

        @pl.when(jnp.logical_not(needs))
        def _():
            work(lambda scores: scores)

        return 0

    lax.fori_loop(0, place + 1, block, 0)

    def clear(j, _):
        base = pl.multiple_of(j * span, span)
        dkv_ref[pl.ds(base, span), :] = jnp.zeros((span, 2 * HDIM), low_type)
        return 0

    lax.fori_loop(place + 1, dkv_ref.shape[0] // span, clear, 0)
    dq_ref[...] = jnp.where(left_half(dq_ref.shape), dq_s[0], dq_s[1])


def whole_spec(shape):
    return pl.BlockSpec(shape, lambda *_: (0,) * len(shape))


def any_specs(count):
    return [pl.BlockSpec(memory_space=pl.ANY)] * count


def att_cost(span, keys, matmuls):
    return pl.CostEstimate(
        flops=2 * matmuls * span * 2 * keys * 256,
        bytes_accessed=4 * keys * 128,
        transcendentals=span * 2 * keys,
    )


def attention_forward(where, queries, kk, vv, starts, deps):
    span, width = queries.shape
    return pl.pallas_call(
        att_fwd_kernel,
        in_specs=[
            pl.BlockSpec(memory_space=pltpu.SMEM),
            whole_spec((span, width)),
            whole_spec(kk.shape),
            whole_spec(vv.shape),
            whole_spec((span, 1)),
        ]
        + any_specs(len(deps)),
        out_specs=[whole_spec((span, width)), whole_spec((2, span, 1))],
        out_shape=[
            jax.ShapeDtypeStruct((span, width), f32),
            jax.ShapeDtypeStruct((2, span, 1), f32),
        ],
        grid=(1,),
        scratch_shapes=[
            pltpu.VMEM((2, span, 1), f32),
            pltpu.VMEM((2, span, 1), f32),
            pltpu.VMEM((2, span, width), f32),
        ],
        compiler_params=pltpu.CompilerParams(vmem_limit_bytes=vmem_bytes),
        cost_estimate=att_cost(span, kk.shape[0], 4),
        name="attention_forward",
    )(where, queries, kk, vv, starts.reshape(span, 1), *deps)


def attention_backward(where, queries, grads, kk, vv, starts, lse, delta, deps):
    span, width = queries.shape
    return pl.pallas_call(
        att_bwd_kernel,
        in_specs=[
            pl.BlockSpec(memory_space=pltpu.SMEM),
            whole_spec((span, width)),
            whole_spec((span, width)),
            whole_spec(kk.shape),
            whole_spec(vv.shape),
            whole_spec((1, span)),
            whole_spec((2, 1, span)),
            whole_spec((2, 1, span)),
        ]
        + any_specs(len(deps)),
        out_specs=[whole_spec((span, width)), whole_spec(kk.shape)],
        out_shape=[
            jax.ShapeDtypeStruct((span, width), f32),
            jax.ShapeDtypeStruct(kk.shape, low_type),
        ],
        grid=(1,),
        scratch_shapes=[
            pltpu.VMEM((2, span, width), f32),
        ],
        compiler_params=pltpu.CompilerParams(vmem_limit_bytes=vmem_bytes),
        cost_estimate=att_cost(span, kk.shape[0], 10),
        name="attention_backward",
    )(
        where,
        queries,
        grads,
        kk,
        vv,
        starts.reshape(1, span),
        lse.reshape(2, 1, span),
        delta.reshape(2, 1, span),
        *deps,
    )


def pair_blocks(pair):
    left = lax.broadcasted_iota(jnp.int32, pair.shape, 1) < HDIM
    return jnp.where(left, pair, 0.0), jnp.where(left, 0.0, pair)


def ssd_fwd_kernel(xd_ref, b_ref, c_ref, cs_ref, cst_ref, csx_ref, in_ref, *rest):
    y_ref, before_ref, s_s = rest[-3:]

    @pl.when(pl.program_id(0) == 0)
    def _():
        s_s[...] = in_ref[...]

    rows = xd_ref.shape[0]
    b, c = b_ref[...], c_ref[...]
    inner = dot_t(c, b, highest)
    lower = lax.broadcasted_iota(jnp.int32, (rows, rows), 0) >= lax.broadcasted_iota(
        jnp.int32, (rows, rows), 1
    )
    state = s_s[...]
    before_ref[...] = state
    csx = csx_ref[...]
    last = csx[rows - 1 :, :]
    carried = jnp.exp(csx) * dot(c, state, highest)

    def mixing(h):
        spread = jnp.where(lower, cs_ref[:, h : h + 1] - cst_ref[h : h + 1, :], masked)
        return jnp.exp(spread) * inner

    for pair in range(xd_ref.shape[1] // (2 * HDIM)):
        cols = slice(pair * 2 * HDIM, (pair + 1) * 2 * HDIM)
        mix = jnp.concatenate([mixing(2 * pair), mixing(2 * pair + 1)], axis=1)
        blocks = jnp.concatenate(pair_blocks(xd_ref[:, cols]), axis=0)
        y_ref[:, cols] = carried[:, cols] + dot(mix, blocks, highest)
    s_s[...] = jnp.exp(last) * state + t_dot(b, jnp.exp(last - csx) * xd_ref[...], highest)


def ssd_bwd_kernel(
    xd_ref,
    dy_ref,
    b_ref,
    c_ref,
    cs_ref,
    cst_ref,
    csx_ref,
    before_ref,
    future_ref,
    *rest,
):
    dxd_ref, db_ref, dc_ref, ds_s = rest[-4:]

    @pl.when(pl.program_id(0) == 0)
    def _():
        ds_s[...] = future_ref[...]

    rows = xd_ref.shape[0]
    b, c = b_ref[...], c_ref[...]
    inner_t = dot_t(b, c, highest)
    row_id = lax.broadcasted_iota(jnp.int32, (rows, rows), 0)
    col_id = lax.broadcasted_iota(jnp.int32, (rows, rows), 1)
    csx = csx_ref[...]
    last = csx[rows - 1 :, :]
    grad_state = ds_s[...]
    end_fall = jnp.exp(last - csx)
    from_state = end_fall * dot(b, grad_state, highest)
    scaled_dy = jnp.exp(csx) * dy_ref[...]
    grad_inner = jnp.zeros((rows, rows), f32)

    def falls(h):
        spread = cs_ref[:, h : h + 1] - cst_ref[h : h + 1, :]
        return jnp.exp(jnp.where(row_id >= col_id, spread, masked))

    def falls_t(h):
        spread = cst_ref[h : h + 1, :] - cs_ref[:, h : h + 1]
        return jnp.exp(jnp.where(row_id <= col_id, spread, masked))

    for pair in range(xd_ref.shape[1] // (2 * HDIM)):
        cols = slice(pair * 2 * HDIM, (pair + 1) * 2 * HDIM)
        dy_left, dy_right = pair_blocks(dy_ref[:, cols])
        mix_t = jnp.concatenate(
            [falls_t(2 * pair) * inner_t, falls_t(2 * pair + 1) * inner_t], axis=1
        )
        blocks = jnp.concatenate([dy_left, dy_right], axis=0)
        dxd_ref[:, cols] = from_state[:, cols] + dot(mix_t, blocks, highest)
        xd = xd_ref[:, cols]
        grad_inner = grad_inner + falls(2 * pair) * dot_t(dy_left, xd, highest)
        grad_inner = grad_inner + falls(2 * pair + 1) * dot_t(dy_right, xd, highest)
    dc_ref[...] = dot(grad_inner, b, highest) + dot_t(scaled_dy, before_ref[...], highest)
    db_ref[...] = t_dot(grad_inner, c, highest) + dot_t(
        end_fall * xd_ref[...], grad_state, highest
    )
    ds_s[...] = jnp.exp(last) * grad_state + t_dot(c, scaled_dy, highest)


def ssd_forward(xd, b, c, cs, cst, csx, entering, deps):
    length, width = xd.shape
    blocks = length // chunk_len
    heads = cs.shape[1]

    def rows(w):
        return pl.BlockSpec((chunk_len, w), lambda i: (i, 0))

    return pl.pallas_call(
        ssd_fwd_kernel,
        grid=(blocks,),
        in_specs=[
            rows(width),
            rows(NST),
            rows(NST),
            rows(heads),
            pl.BlockSpec((None, heads, chunk_len), lambda i: (i, 0, 0)),
            rows(width),
            whole_spec((NST, width)),
        ]
        + any_specs(len(deps)),
        out_specs=[rows(width), pl.BlockSpec((None, NST, width), lambda i: (i, 0, 0))],
        out_shape=[
            jax.ShapeDtypeStruct((length, width), f32),
            jax.ShapeDtypeStruct((blocks, NST, width), f32),
        ],
        scratch_shapes=[pltpu.VMEM((NST, width), f32)],
        compiler_params=pltpu.CompilerParams(vmem_limit_bytes=vmem_bytes),
        cost_estimate=pl.CostEstimate(
            flops=12 * 3 * length * width * NST, bytes_accessed=20 * length * width, transcendentals=0
        ),
        name="ssd_forward",
    )(xd, b, c, cs, cst, csx, entering, *deps)


def ssd_backward(xd, dy, b, c, cs, cst, csx, before, future, deps):
    length, width = xd.shape
    blocks = length // chunk_len
    heads = cs.shape[1]

    def rows(w):
        return pl.BlockSpec((chunk_len, w), lambda i: (blocks - 1 - i, 0))

    def slabs(*shape):
        return pl.BlockSpec((None,) + shape, lambda i: (blocks - 1 - i, 0, 0))

    return pl.pallas_call(
        ssd_bwd_kernel,
        grid=(blocks,),
        in_specs=[
            rows(width),
            rows(width),
            rows(NST),
            rows(NST),
            rows(heads),
            slabs(heads, chunk_len),
            rows(width),
            slabs(NST, width),
            whole_spec((NST, width)),
        ]
        + any_specs(len(deps)),
        out_specs=[rows(width), rows(NST), rows(NST)],
        out_shape=[
            jax.ShapeDtypeStruct((length, width), f32),
            jax.ShapeDtypeStruct((length, NST), f32),
            jax.ShapeDtypeStruct((length, NST), f32),
        ],
        scratch_shapes=[pltpu.VMEM((NST, width), f32)],
        compiler_params=pltpu.CompilerParams(vmem_limit_bytes=vmem_bytes),
        cost_estimate=pl.CostEstimate(
            flops=12 * 8 * length * width * NST, bytes_accessed=24 * length * width, transcendentals=0
        ),
        name="ssd_backward",
    )(xd, dy, b, c, cs, cst, csx, before, future, *deps)


def per_device(
    tokens,
    doc_ids,
    cotangent,
    w_in,
    w_dt,
    w_mo,
    w_ao,
    w_gu,
    w_down,
    norm1,
    norm2,
    gate_norm,
    conv_w,
    conv_b,
    dt_bias,
    a_log,
    d_skip,
):
    n_hd = lax.axis_size("hd")
    n_cp = lax.axis_size("cp")
    hd_index = lax.axis_index("hd")
    cp_index = lax.axis_index("cp")
    dp_index = lax.axis_index("dp")
    hd_high = has_bit("hd", 1)
    x_in = tokens[0].astype(f32)
    tok_count, d_model = x_in.shape
    span = tok_count * n_hd
    d_ssm = HM * HDIM
    q_width = QH * HDIM
    k_width = KVH * HDIM
    x_part = d_ssm // n_hd
    heads = HM // n_hd
    q_part = q_width // n_hd
    k_part = k_width // n_hd
    bc_width = 2 * NST
    qkv_cols = q_part + 2 * k_part
    tap_count = conv_w.shape[0]
    score_scale = 1.0 / math.sqrt(HDIM)
    documents = doc_ids[0]

    def group(array, begin, width, dim=1):
        part = width // n_hd
        return lax.dynamic_slice_in_dim(array, begin + hd_index * part, part, dim)

    tokens_all = gather_pair(tokens[0], "hd", 0)

    normed1_all = rms_norm(tokens_all.astype(f32), norm1).astype(low_type)
    rim_tokens = shifted(tokens_all[span - 16 :], "cp", 1)
    normed1_rim = rms_norm(rim_tokens.astype(f32), norm1).astype(low_type)

    own_docs = lax.dynamic_slice_in_dim(documents, cp_index * span, span, 0)
    doc_begin = jnp.sum(documents[None, :] < own_docs[:, None], axis=1).astype(jnp.int32)
    where = jnp.stack([cp_index, jnp.max(doc_begin)]).astype(jnp.int32)

    positions = cp_index * span + jnp.arange(span, dtype=jnp.int32)
    half_width = HDIM // 2
    column = jnp.arange(qkv_cols, dtype=jnp.int32)
    turns = column < q_part + k_part
    power = (column % half_width).astype(f32)
    frequency = jnp.where(turns, rope_base ** (-2.0 * power / HDIM), 0.0)
    sign = jnp.where(column % HDIM < half_width, -1.0, 1.0)
    angles = positions.astype(f32)[:, None] * frequency[None, :]
    cosines = jnp.cos(angles)
    sines = jnp.sin(angles) * sign[None, :]
    cosines, sines = lax.optimization_barrier((cosines, sines))
    turner = half_turner(qkv_cols).astype(low_type)

    def half_turn(values):
        top = values.astype(low_type)
        return dot(top, turner) + dot((values - top.astype(f32)).astype(low_type), turner)

    q_start = 2 * d_ssm + bc_width
    k_start = q_start + q_width
    v_start = k_start + k_width
    dt_pad = 128 - heads
    shard_misc = jnp.concatenate(
        [
            group(w_in, q_start, q_width),
            group(w_in, k_start, k_width),
            group(w_in, v_start, k_width),
            w_in[:, 2 * d_ssm : q_start],
            group(w_dt, 0, HM),
            jnp.zeros((w_dt.shape[0], dt_pad), low_type),
        ],
        axis=1,
    )
    misc_cp, _ = gather_cp(shard_misc, (where, normed1_all))
    w_misc = gather_pair(after(after(misc_cp, cosines), normed1_rim), "dp", 0)
    xs_cp, xs_steps = gather_cp(after(group(w_in, d_ssm, d_ssm), w_misc))
    out_rows = jnp.concatenate([w_mo, w_ao], axis=0)
    half_cols = d_model // 2
    handed = swap(out_rows[:, half_cols:], "dp", 1)
    holds = dp_index == hd_index
    out_half = jnp.where(holds, out_rows[:, :half_cols], handed)
    w_back = lax.all_gather(w_down, ("dp", "cp"), axis=0, tiled=True)
    w_xs = gather_pair(after(xs_cp, w_back), "dp", 0)

    proj = dot(normed1_all, w_misc)
    qkv = proj[:, :qkv_cols]
    qkv_low = (qkv * cosines + half_turn(qkv) * sines).astype(low_type)
    kv_all, _ = gather_cp(qkv_low[:, q_part:], (xs_steps[0], xs_steps[1]))
    q_scaled = qkv_low[:, :q_part] * jnp.asarray(score_scale, low_type)
    bc = proj[:, qkv_cols : qkv_cols + bc_width].astype(low_type)
    at = qkv_cols + bc_width
    dt_raw = proj[:, at : at + heads].astype(low_type).astype(f32)
    x_bc = jnp.concatenate([dot(normed1_all, w_xs).astype(low_type), bc], axis=1)
    w_bc = w_misc[:, qkv_cols : qkv_cols + bc_width]
    rim_rows = jnp.concatenate([dot(normed1_rim, w_xs), dot(normed1_rim, w_bc)], axis=1)
    rim_rows = rim_rows.astype(low_type)[16 - (tap_count - 1) :]

    padded = jnp.concatenate([rim_rows, x_bc], axis=0).astype(f32)
    conv_taps = jnp.concatenate([group(conv_w, 0, d_ssm), conv_w[:, d_ssm:]], axis=1)
    conv_shift = jnp.concatenate([group(conv_b, 0, d_ssm, 0), conv_b[d_ssm:]], axis=0)
    dt_shift = group(dt_bias, 0, HM, 0)
    log_scale = group(a_log, 0, HM, 0)
    skip_gain = group(d_skip, 0, HM, 0)
    expand = expander(heads, HDIM)

    def wide(values):
        return dot(values, expand, highest)

    def per_head(values):
        return dot_t(values, expand, highest)

    skip_x = wide(skip_gain[None, :])

    def prepare(padded_in, taps_in, shift_in, dt_in, dt_shift_in, log_in):
        activated = jax.nn.silu(causal_conv(padded_in, taps_in, shift_in))
        return (
            activated[:, :x_part],
            activated[:, x_part : x_part + NST],
            activated[:, x_part + NST :],
            jax.nn.softplus(dt_in + dt_shift_in),
            -jnp.exp(log_in),
        )

    (x_conv, b_conv, c_conv, dt_value, decay_rate), prep_pull = jax.vjp(
        prepare, padded, conv_taps, conv_shift, dt_raw, dt_shift, log_scale
    )
    blocks = span // chunk_len
    ones_low = jnp.tril(jnp.ones((chunk_len, chunk_len), f32))
    cs_block = jnp.einsum(
        "ts,bsh->bth",
        ones_low,
        (dt_value * decay_rate[None, :]).reshape(blocks, chunk_len, heads),
        precision=highest,
    )
    block_total = cs_block[:, -1]
    block_base = jnp.concatenate(
        [jnp.zeros((1, heads), f32), jnp.cumsum(block_total, axis=0)], axis=0
    )
    cs_dev = (cs_block + block_base[:-1, None, :]).reshape(span, heads)
    cs = cs_block.reshape(span, heads)
    cst = jnp.swapaxes(cs_block, 1, 2)
    log_dev = block_base[-1]
    csx = wide(cs)
    csx_dev = wide(cs_dev)
    dtx = wide(dt_value)
    xd = dtx * x_conv
    state_local = t_dot(b_conv, jnp.exp(csx_dev[-1:] - csx_dev) * xd, highest)
    scan = state_scan(log_dev, state_local, True)
    in_sent = [next(scan)]
    while len(in_sent) < n_cp.bit_length():
        in_sent.append(scan.send(None))
    state_in = in_sent[-1]

    kk = jnp.concatenate([kv_all[:, :HDIM], kv_all[:, :HDIM]], axis=1)
    vv = jnp.concatenate([kv_all[:, HDIM:], kv_all[:, HDIM:]], axis=1)
    w_gate_up = lax.all_gather(after(after(w_gu, kk), xs_cp), ("dp", "cp"), axis=0, tiled=True)
    pairs = [slice(p * 2 * HDIM, (p + 1) * 2 * HDIM) for p in range(q_part // (2 * HDIM))]
    att_deps = [(in_sent[0],), (in_sent[1],)]
    att_outs, lses = [], []
    for cols, deps in zip(pairs, att_deps):
        att_out, lse = attention_forward(
            where, q_scaled[:, cols], kk, vv, doc_begin, deps + tuple(att_outs)
        )
        att_outs.append(att_out)
        lses.append(lse)
    att_f32 = jnp.concatenate(att_outs, axis=1)
    att_low = att_f32.astype(low_type)

    shard_rows, out_cols = w_in.shape[0], out_half.size // w_in.shape[0]
    z_out = jnp.concatenate(
        [group(w_in, 0, d_ssm), out_half.reshape(shard_rows, out_cols)], axis=1
    )
    z_out, _ = gather_cp(after(z_out, kk), (in_sent[0], att_outs[0]))
    z_out = after(z_out, att_outs[1])
    z_out_other = swap(z_out, "dp", 1)
    w_z = in_order(
        z_out[:, :x_part], z_out_other[:, :x_part], has_bit("dp", 1), 0, jnp.concatenate
    )
    out_sides = [a[:, x_part:].reshape(-1, half_cols) for a in (z_out, z_out_other)]
    w_out = in_order(*out_sides, jnp.logical_not(holds), 1, jnp.concatenate)
    mo_rows, ao_rows = w_mo.shape[0], w_ao.shape[0]
    w_out = w_out.reshape(n_cp, mo_rows + ao_rows, d_model)
    w_out = jnp.concatenate(
        [
            w_out[:, :mo_rows].reshape(n_cp * mo_rows, d_model),
            w_out[:, mo_rows:].reshape(n_cp * ao_rows, d_model),
        ],
        axis=0,
    )

    y_core, before = ssd_forward(
        xd, b_conv, c_conv, cs, cst, csx, state_in, (att_outs[-1],)
    )
    y_low = (y_core + skip_x * x_conv).astype(low_type).astype(f32)

    gate_z = dot(normed1_all, w_z)
    gain = group(gate_norm, 0, d_ssm, 0)[None, :]
    sig_z = jax.nn.sigmoid(gate_z)
    silu_z = gate_z * sig_z
    mixed_y = y_low * silu_z
    squares = jnp.sum(mixed_y * mixed_y, axis=-1)
    squares = squares + swap(squares, "hd", 1)
    inv = lax.rsqrt(squares / d_ssm + eps_norm)[:, None]
    gated_low = (mixed_y * inv * gain).astype(low_type)
    branches = jnp.concatenate([gated_low, att_low], axis=1)
    partial = dot(branches, w_out).reshape(n_hd, tok_count, d_model)
    x_mid = x_in + fold(partial, "hd", 1, 0)

    normed2, norm2_pull = jax.vjp(rms_norm, x_mid, norm2)
    normed2_low = normed2.astype(low_type)
    gate_up = dot(normed2_low, w_gate_up)

    def swiglu(both_halves):
        return jax.nn.silu(both_halves[:, :FF]) * both_halves[:, FF:]

    hidden, swiglu_pull = jax.vjp(swiglu, gate_up)
    hidden_low = hidden.astype(low_type)

    grad_out_low = cotangent[0]
    grad_hidden = dot_t(grad_out_low, w_back)
    grad_gate_up = swiglu_pull(grad_hidden)[0].astype(low_type)
    grad_normed2 = dot_t(grad_gate_up, w_gate_up)
    grad_mid_part, g_norm2 = norm2_pull(grad_normed2)
    grad_mid = grad_out_low.astype(f32) + grad_mid_part
    grad_mid_low = grad_mid.astype(low_type)
    grad_mid_all = gather_pair(grad_mid_low, "hd", 0)

    def rows_by_owner(grad):
        rows, cols = grad.shape
        return grad.reshape(2, n_cp, n_hd, rows // (2 * n_cp * n_hd), cols)

    def to_owner(grad):
        grad = grad.reshape((-1,) + grad.shape[-1:])
        return lax.psum_scatter(grad, ("cp", "hd"), scatter_dimension=0, tiled=True).astype(f32)

    def halves_by_core(values):
        part = values.shape[1] // 2
        kept = lax.dynamic_slice_in_dim(values, dp_index * part, part, 1)
        given = lax.dynamic_slice_in_dim(values, (1 - dp_index) * part, part, 1)
        return jnp.concatenate([kept, swap(given, "dp", 1)], axis=0)

    def cores(values):
        return jnp.concatenate([values, swap(values, "dp", 1)], axis=0)

    g_down = t_dot(halves_by_core(hidden_low), cores(grad_out_low)).astype(low_type)
    s_down = to_owner(g_down)
    g_gate_up = t_dot(
        halves_by_core(after(normed2_low, grad_mid_low)), cores(grad_gate_up)
    ).astype(low_type)
    s_gu = to_owner(g_gate_up)
    result_seq = x_mid + dot(after(hidden_low, grad_mid_low), w_back)

    grad_branches = dot_t(grad_mid_all, w_out)
    grad_gated = grad_branches[:, :x_part]
    grad_att = grad_branches[:, x_part:].astype(low_type)
    delta = jnp.transpose(
        dot_t(grad_att.astype(f32) * att_f32, expander(q_part // HDIM, HDIM), highest)
    )

    gain_grad = grad_gated * gain
    along = jnp.sum(gain_grad * mixed_y, axis=-1)
    along = along + swap(along, "hd", 1)
    grad_mixed = inv * gain_grad - mixed_y * (inv * inv * inv * (along / d_ssm)[:, None])
    g_gain = jnp.sum(grad_gated * mixed_y * inv, axis=0)
    grad_y = (grad_mixed * silu_z).astype(low_type).astype(f32)
    grad_z = (grad_mixed * y_low * sig_z * (1.0 + gate_z * (1.0 - sig_z))).astype(low_type)

    scaled_dy = jnp.exp(csx_dev) * grad_y
    scan = state_scan(log_dev, t_dot(c_conv, scaled_dy, highest), False)
    future = next(scan)

    normed1_half = halves_by_core(normed1_all)

    def by_owner(grad):
        grad = t_dot(normed1_half, cores(grad)).astype(low_type)
        return grad.reshape(n_cp, d_model // (2 * n_cp), grad.shape[1])

    g_out = t_dot(after(branches, scaled_dy), grad_mid_all).astype(low_type)
    g_out = jnp.concatenate(
        [
            g_out[:x_part].reshape(n_cp, n_hd, mo_rows // n_hd, d_model),
            g_out[x_part:].reshape(n_cp, n_hd, ao_rows // n_hd, d_model),
        ],
        axis=2,
    )
    g_out = fold(g_out, "dp", 1, 1).astype(low_type)
    dqs, dkvs = [], []
    bwd_deps = (g_gate_up, g_down, g_out)
    for p, cols in enumerate(pairs):
        dq, dkv = attention_backward(
            where,
            q_scaled[:, cols],
            grad_att[:, cols],
            kk,
            vv,
            doc_begin,
            lses[p],
            delta[2 * p : 2 * p + 2],
            bwd_deps + (future,),
        )
        dqs.append(dq)
        future = scan.send(dq)
        bwd_deps = ()
        dkvs.append(dkv.reshape(n_cp, span, 2 * HDIM))
    dkv_sum = dkvs[0].astype(f32)
    for dkv in dkvs[1:]:
        dkv_sum = dkv_sum + dkv.astype(f32)
    dkv_low = dkv_sum.astype(low_type)
    dkv, dkv_steps = fold_cp(dkv_low, low_first())
    for last_sent in scan:
        future = last_sent

    out_grad, out_folds = fold_cp(g_out, low_first(), (None, dqs[0], dqs[1]) + (None,) * 5)
    s_out = lax.ppermute(out_grad, ("dp", "hd"), [(0, 0), (1, 2), (2, 1), (3, 3)])
    s_mo, s_ao = s_out[: mo_rows // n_hd], s_out[mo_rows // n_hd :]


    dxd, db, dc = ssd_backward(
        xd,
        grad_y,
        b_conv,
        c_conv,
        cs,
        cst,
        csx,
        before,
        future,
        (dqs[-1], out_folds[0], dkv_low, s_down),
    )

    ddt_direct = per_head(x_conv * dxd)
    dcs = per_head(grad_y * y_core) - dt_value * ddt_direct
    state_end = jnp.exp(csx_dev[-1:]) * state_in + state_local
    end_term = per_head(jnp.sum(future * state_end, axis=0)[None, :])
    ones_up = jnp.triu(jnp.ones((span, span), f32))
    da = dot(ones_up, dcs, highest) + end_term
    g_skip = per_head(jnp.sum(grad_y * x_conv, axis=0)[None, :])[0]
    grad_padded, grad_taps, grad_shift, grad_dt, grad_dt_shift, grad_log = prep_pull(
        (
            dtx * dxd + skip_x * grad_y,
            after(db, dkv_steps[0]),
            dc,
            ddt_direct + decay_rate[None, :] * da,
            jnp.sum(da * dt_value, axis=0),
        )
    )
    rim_back = shifted(grad_padded[: tap_count - 1], "cp", -1)
    grad_conv_in = jnp.concatenate(
        [
            grad_padded[tap_count - 1 : span],
            grad_padded[span:] + rim_back,
        ],
        axis=0,
    ).astype(low_type)
    grad_xs = after(after(grad_conv_in, dkv_steps[1]), s_gu)[:, :x_part]
    grad_bc_dt = jnp.concatenate(
        [
            grad_conv_in[:, x_part:],
            grad_dt.astype(low_type),
            jnp.zeros((span, dt_pad), low_type),
        ],
        axis=1,
    )
    g_early = by_owner(jnp.concatenate([grad_xs, grad_bc_dt], axis=1))
    grad_qkv = jnp.concatenate([dq * score_scale for dq in dqs] + [after(dkv, g_early)], axis=1)
    grad_qkv = (grad_qkv * cosines - half_turn(grad_qkv) * sines).astype(low_type)
    g_late = by_owner(jnp.concatenate([grad_z, grad_qkv], axis=1))
    r_late, _ = fold_cp(g_late, low_last())
    r_early, early_steps = fold_cp(g_early, low_first())
    grad_misc = jnp.concatenate([grad_qkv, grad_bc_dt], axis=1)

    grad_misc = after(after(grad_misc, g_early), g_late)
    grad_normed1 = dot_t(grad_z, w_z) + dot_t(grad_misc, w_misc) + dot_t(grad_xs, w_xs)
    grad_normed1 = fold(grad_normed1.reshape(n_hd, tok_count, d_model), "hd", 1, 0)
    _, norm1_pull = jax.vjp(rms_norm, x_in, norm1)
    grad_x_part, g_norm1 = norm1_pull(grad_normed1)
    grad_tokens_out = (grad_mid + grad_x_part).astype(low_type)

    reduced_in = jnp.concatenate([r_late, r_early], axis=1).astype(low_type)
    own_rows = reduced_in.shape[0] // n_hd
    halves = reduced_in.reshape(n_hd, own_rows, reduced_in.shape[1])
    got = swap(jnp.where(hd_high, halves[0], halves[1]), "hd", 1)
    mine = jnp.where(hd_high, halves[1], halves[0])
    group0 = jnp.where(hd_high, got, mine).astype(f32)
    group1 = jnp.where(hd_high, mine, got).astype(f32)

    def both(begin, width):
        return [group0[:, begin : begin + width], group1[:, begin : begin + width]]

    xs_at = x_part + qkv_cols
    bc0, bc1 = both(xs_at + x_part, bc_width)
    s_in = jnp.concatenate(
        both(0, x_part)
        + both(xs_at, x_part)
        + [bc0 + bc1]
        + both(x_part, q_part)
        + both(x_part + q_part, k_part)
        + both(x_part + q_part + k_part, k_part),
        axis=1,
    )
    s_dt = jnp.concatenate(both(xs_at + x_part + bc_width, heads), axis=1)

    def placed(values, width):
        full = jnp.zeros(values.shape[:-1] + (width,), f32)
        return lax.dynamic_update_slice_in_dim(
            full, values, hd_index * values.shape[-1], values.ndim - 1
        )

    g_conv_w = jnp.concatenate([placed(grad_taps[:, :x_part], d_ssm), grad_taps[:, x_part:]], axis=1)
    g_conv_b = jnp.concatenate([placed(grad_shift[:x_part], d_ssm), grad_shift[x_part:]], axis=0)
    small = [
        g_norm1,
        g_norm2,
        placed(g_gain, d_ssm),
        g_conv_w,
        g_conv_b,
        placed(grad_dt_shift, HM),
        placed(grad_log, HM),
        placed(g_skip, HM),
    ]
    flat = jnp.concatenate([s.reshape(-1) for s in small])
    length = flat.shape[0]
    flat = jnp.pad(flat, (0, -length % 1024)).reshape(-1, 128)
    flat = flat + swap(flat, "dp", 1)
    flat = flat + swap(flat, "hd", 1)
    for bit in low_first():
        flat = flat + swap(flat, "cp", bit)
    flat = flat.reshape(-1)
    sums = []
    begin = 0
    for s in small:
        sums.append(flat[begin : begin + s.size].reshape(s.shape))
        begin += s.size
    return (
        result_seq.astype(low_type)[None],
        grad_tokens_out[None],
        s_in,
        s_dt,
        s_mo,
        s_ao,
        s_gu,
        s_down,
        *sums,
    )


def solution(mesh):
    weight = P(("dp", "cp"), None)
    grad = P(("dp", "cp", "hd"), None)
    seq = P("dp", ("cp", "hd"), None)
    in_specs = (seq, P("dp", None), seq) + (weight,) * 6 + (P(),) * 8
    out_specs = (seq, seq) + (grad,) * 6 + (P(),) * 8
    return jax.shard_map(
        per_device, mesh=mesh, in_specs=in_specs, out_specs=out_specs, check_vma=False
    )
```

time: 830 us -> 660 us (0.80)
  waiting for transfers between devices: 282 us -> 169 us
  other arithmetic: 148 us -> 89.6 us
  local copies, waits for them, and re-layouts: 108 us -> 73.2 us
  between operations: 6.33 us -> 30.8 us
  matrix products: 67.6 us -> 88.8 us
  starting transfers between devices: 160 us -> 144 us
    ppermute x75 -> x54, waiting for transfers between devices: 282 us -> 167 us  [swap(): return lax.ppermute(value, axis, [(i, i ^ bit) for i in range(count)])]
    dot_general x6 -> x29, matrix products: 17.9 us -> 38.7 us  [dot(): return jnp.dot(left, right, preferred_element_type=f32, precision=precision)]
    ppermute x75 -> x54, starting transfers between devices: 154 us -> 138 us  [swap(): return lax.ppermute(value, axis, [(i, i ^ bit) for i in range(count)])]
    select_n x31 -> x13, other arithmetic: 16.1 us -> 4.17 us  [fold(): got = swap(jnp.where(high, first, second).astype(low_type), axis, bit)]
    mul x14 -> x0, local copies, waits for them, and re-layouts: 11.1 us -> none  [the longest x1 2.86 us: per_device(): ddt_direct = per_head(x_conv * dxd)]
    select_n x9 -> x5, other arithmetic: 13.1 us -> 3.5 us  [in_order(): jnp.where(high, other, mine)]
    slice x18 -> x29, local copies, waits for them, and re-layouts: 9.42 us -> 18.8 us  [the longest x21 15 us: after(): lax.slice(earlier, (0,) * earlier.ndim, (1,) * earlier.ndim).reshape(())]
    add x1 -> x20, other arithmetic: 0.02 us -> 8.48 us  [the longest x19 5.76 us: after(): return value + (first.astype(f32) * 0.0).astype(value.dtype)]
  transfers between devices with their start and end apart: 78 -> 61, of which waited for: 38 -> 23; matrix products, arithmetic and copies ran while one was open for 33% -> 36% of each run, Pallas kernels for 6% -> 9%
where the time goes in v2:
time: 660 us; the launch traced here: 652 us
  waiting for transfers between devices  169 us (26%)
  starting transfers between devices  144 us (22%)
  other arithmetic  89.6 us (14%)
  matrix products  88.8 us (13%)
  local copies, waits for them, and re-layouts  73.2 us (11%)
  Pallas kernels  56.2 us (9%)
  between operations  30.8 us (5%)
    ppermute x54, waiting for transfers between devices, swap(): return lax.ppermute(value, axis, [(i, i ^ bit) for i in range(count)])  167 us
    ppermute x54, starting transfers between devices, swap(): return lax.ppermute(value, axis, [(i, i ^ bit) for i in range(count)])  138 us
    dot_general x29, matrix products, dot(): return jnp.dot(left, right, preferred_element_type=f32, precision=precision)  38.7 us
    dot_general x7, matrix products, t_dot(): lax.dot_general(left, right, (((0,), (0,)), ((), ())), preferred_element_...  28.2 us
    dot_general x11, matrix products, dot_t(): lax.dot_general(left, right, (((1,), (1,)), ((), ())), preferred_element_...  21.2 us
    pallas_call x1, Pallas kernels, ssd_backward(): pl.pallas_call(ssd_bwd_kernel, grid=(blocks,), in_specs=[rows(width), row...  20.9 us
    unnamed x333, local copies, waits for them, and re-layouts  19.8 us
    slice x21, local copies, waits for them, and re-layouts, after(): lax.slice(earlier, (0,) * earlier.ndim, (1,) * earlier.ndim).reshape(())  15 us
  transfers between devices with their start and end apart: 61, of which 23 were waited for; matrix products, arithmetic and copies ran while one was open for 36% of the time, Pallas kernels for 9%

profile of v2, /device:TPU:0, one launch (start us, length us, event | category | flops | bytes accessed | tf_op | source)
XLA Modules:
  0.0 651.6 jit_solution(5700231717293644907)
XLA Ops:
  32.4 6.3 collective-permute-done.2
  47.7 15.2 %collective-permute-done.3 = bf16[4,64,768]{2,1,0:T(8,128)(2,1)S(1)} collective-permute-done((bf16[4,64,768]{2,1,0:T(8,128)(2,1)S(1)}, bf16[4,64,768]{2,1,0:T(8,128)(2,1)S(1)}, u32[]{:S(2)}, u32[]{:S(2)}) %collective-permute-start.3) | collective-permute-done | bytes 393248 | tf_op jit(solution)/shard_map/ppermute | solution.py:29
  117.1 11.6 %collective-permute-done.15 = bf16[4,640,128]{2,1,0:T(8,128)(2,1)S(1)} collective-permute-done((bf16[4,640,128]{2,1,0:T(8,128)(2,1)S(1)}, bf16[4,640,128]{2,1,0:T(8,128)(2,1)S(1)}, u32[]{:S(2)}, u32[]{:S(2)}) %collective-permute-start.15) | collective-permute-done | bytes 655392 | tf_op jit(solution)/shard_map/ppermute | solution.py:29
  155.3 5.8 attention_forward.2
  166.1 6.3 collective-permute-start.11
  185.1 30.8 %collective-permute-done.19 = bf16[4,64,1792]{2,1,0:T(8,128)(2,1)S(1)} collective-permute-done((bf16[4,64,1792]{2,1,0:T(8,128)(2,1)S(1)}, bf16[4,64,1792]{2,1,0:T(8,128)(2,1)S(1)}, u32[]{:S(2)}, u32[]{:S(2)}) %collective-permute-start.19) | collective-permute-done | bytes 917536 | tf_op jit(solution)/shard_map/ppermute | solution.py:29
  219.9 14.0 %collective-permute-done.12 = bf16[144,768]{1,0:T(8,128)(2,1)S(1)} collective-permute-done((bf16[144,768]{1,0:T(8,128)(2,1)S(1)}, bf16[144,768]{1,0:T(8,128)(2,1)S(1)}, u32[]{:S(2)}, u32[]{:S(2)}) %collective-permute-start.12) | collective-permute-done | bytes 221216 | tf_op jit(solution)/shard_map/ppermute | solution.py:29
  234.8 10.7 %ssd_forward.1 = (f32[640,768]{1,0:T(8,128)}, f32[5,128,768]{2,1,0:T(8,128)}) custom-call(f32[640,768]{1,0:T(8,128)} %copy-done.27, f32[640,128]{1,0:T(8,128)} %get-tuple-element.178.b_ref, f32[640,128]{1,0:T(8,128)} %get-tuple-element.177.c_ref, f32[640,12]{1,0:T(8,128)} %bitcast.447, f32[5,12,128]{2,1,0:T(8,128)} %copy-done.85, ...), custom_call_target="tpu_custom_call" | custom-call | flops 2264924160 | bytes 9830400 | tf_op jit(solution)/shard_map/ssd_forward/pallas_call | solution.py:501
  274.1 8.1 %collective-permute-done.22 = bf16[320,1024]{1,0:T(8,128)(2,1)} collective-permute-done((bf16[320,1024]{1,0:T(8,128)(2,1)}, bf16[320,1024]{1,0:T(8,128)(2,1)}, u32[]{:S(2)}, u32[]{:S(2)}) %collective-permute-start.22) | collective-permute-done | bytes 655392 | tf_op jit(solution)/shard_map/ppermute | solution.py:29
  286.1 9.2 %fusion.263 = f32[320,4096]{1,0:T(8,128)} fusion(bf16[1024,4096]{1,0:T(8,128)(2,1)} %all-gather.5.cloned.1.call-done, f32[320,1024]{1,0:T(8,128)} %get-tuple-element.155, f32[1024]{0:T(1024)S(1)} %copy-done.123, f32[320]{0:T(512)S(1)} %fusion.209), kind=kOutput, calls=%fused_computation.605 | convolution fusion | flops 2685337600 | bytes 14947584 | tf_op jit(solution)/shard_map/dot_general | solution.py:187
  302.4 5.5 multiply_reduce_fusion.8
  315.5 9.8 %collective-permute-done.23 = bf16[320,1024]{1,0:T(8,128)(2,1)S(1)} collective-permute-done((bf16[320,1024]{1,0:T(8,128)(2,1)S(1)}, bf16[320,1024]{1,0:T(8,128)(2,1)S(1)}, u32[]{:S(2)}, u32[]{:S(2)}) %collective-permute-start.23) | collective-permute-done | bytes 655392 | tf_op jit(solution)/shard_map/ppermute | solution.py:29
  363.0 8.2 %convolution_convert_fusion.rest_0_ = bf16[512,4096]{1,0:T(8,128)(2,1)} fusion(bf16[320,4096]{1,0:T(8,128)(2,1)} %collective-permute-done.26, bf16[320,4096]{1,0:T(8,128)(2,1)} %add_convert_fusion, bf16[320,512]{1,0:T(8,128)(2,1)} %collective-permute-done.25, bf16[320,512]{1,0:T(8,128)(2,1)S(1)} %copy-done.95), kind=kOutput, calls=%fused_computation.1 | convolution fusion | flops 2698248192 | bytes 10092544 | tf_op jit(solution)/shard_map/dot_general | solution.py:167
  371.2 6.5 %attention_backward.2 = (f32[640,128]{1,0:T(8,128)}, bf16[5120,128]{1,0:T(8,128)(2,1)}) custom-call(s32[2]{0:T(128)} %pad_add_fusion.4.where_ref, bf16[640,128]{1,0:T(8,128)(2,1)} %get-tuple-element.232.q_ref, bf16[640,128]{1,0:T(8,128)(2,1)} %get-tuple-element.191.do_ref, bf16[5120,128]{1,0:T(8,128)(2,1)} %pad_maximum_fusion.10.kk_ref, ...), custom_call_target="tpu_custom_call" | custom-call | flops 33554432000 | bytes 2621440 | tf_op jit(solution)/shard_map/attention_backward/pallas_call | solution.py:362
  387.2 11.6 %collective-permute-start.49 = (bf16[2,64,1024]{2,1,0:T(8,128)(2,1)S(1)}, bf16[2,64,1024]{2,1,0:T(8,128)(2,1)S(1)}, u32[]{:S(2)}, u32[]{:S(2)}) collective-permute-start(bf16[2,64,1024]{2,1,0:T(8,128)(2,1)S(1)} %fusion.147), channel_id=1, source_target_pairs={{0,4},{2,6},{4,0},{6,2},{8,12},{10,14},{12,8},{14,10},{1,5},{3,7},... | collective-permute-start | bytes 786440 | tf_op jit(solution)/shard_map/ppermute | solution.py:29
  400.0 6.9 %attention_backward.3 = (f32[640,128]{1,0:T(8,128)}, bf16[5120,128]{1,0:T(8,128)(2,1)}) custom-call(s32[2]{0:T(128)} %pad_add_fusion.4.where_ref, bf16[640,128]{1,0:T(8,128)(2,1)} %get-tuple-element.231.q_ref, bf16[640,128]{1,0:T(8,128)(2,1)} %get-tuple-element.190.do_ref, bf16[5120,128]{1,0:T(8,128)(2,1)} %pad_maximum_fusion.10.kk_ref, ...), custom_call_target="tpu_custom_call" | custom-call | flops 33554432000 | bytes 2621440 | tf_op jit(solution)/shard_map/attention_backward/pallas_call | solution.py:362
  408.8 10.6 %collective-permute-start.35 = (bf16[144,768]{1,0:T(8,128)(2,1)S(1)}, bf16[144,768]{1,0:T(8,128)(2,1)S(1)}, u32[]{:S(2)}, u32[]{:S(2)}) collective-permute-start(bf16[144,768]{1,0:T(8,128)(2,1)S(1)} %broadcast_add_fusion.4), channel_id=1, source_target_pairs={{0,4},{2,6},{4,0},{6,2},{8,12},{10,14},{12,8},{14,10},{1,5},{3,7},... | collective-permute-start | bytes 663560 | tf_op jit(solution)/shard_map/ppermute | solution.py:29
  427.8 27.3 %collective-permute-start.50 = (bf16[64,1024]{1,0:T(8,128)(2,1)}, bf16[64,1024]{1,0:T(8,128)(2,1)}, u32[]{:S(2)}, u32[]{:S(2)}) collective-permute-start(bf16[64,1024]{1,0:T(8,128)(2,1)} %select_bitcast_fusion.31), channel_id=1, source_target_pairs={{0,8},{2,10},{4,12},{6,14},{8,0},{10,2},{12,4},{14,6},{1,9},{3,11}... | collective-permute-start | bytes 393224 | tf_op jit(solution)/shard_map/ppermute | solution.py:29
  457.1 20.8 %collective-permute-done.36 = bf16[144,768]{1,0:T(8,128)(2,1)S(1)} collective-permute-done((bf16[144,768]{1,0:T(8,128)(2,1)S(1)}, bf16[144,768]{1,0:T(8,128)(2,1)S(1)}, u32[]{:S(2)}, u32[]{:S(2)}) %collective-permute-start.36) | collective-permute-done | bytes 221216 | tf_op jit(solution)/shard_map/ppermute | solution.py:29
  486.6 20.9 %ssd_backward.1 = (f32[640,768]{1,0:T(8,128)}, f32[640,128]{1,0:T(8,128)}, f32[640,128]{1,0:T(8,128)}) custom-call(f32[640,768]{1,0:T(8,128)} %copy-done.27, f32[640,768]{1,0:T(8,128)} %convert_element_type.774.dy_ref, f32[640,128]{1,0:T(8,128)} %get-tuple-element.178.b_ref, f32[640,128]{1,0:T(8,128)} %get-tuple-element.177.c_ref, f32[640,12]{1,0:T(8,128)} %bitcast.448, ...), custom_call_target="tpu_custom_call" | custom-call | flops 6039797760 | bytes 11796480 | tf_op jit(solution)/shard_map/ssd_backward/pallas_call | solution.py:539
  534.8 16.6 %collective-permute-start.33 = (bf16[640,128]{1,0:T(8,128)(2,1)S(1)}, bf16[640,128]{1,0:T(8,128)(2,1)S(1)}, u32[]{:S(2)}, u32[]{:S(2)}) collective-permute-start(bf16[640,128]{1,0:T(8,128)(2,1)S(1)} %select_bitcast_fusion.26), channel_id=1, source_target_pairs={{0,8},{2,10},{4,12},{6,14},{8,0},{10,2},{12,4},{14,6},{1,9},{3,11}... | collective-permute-start | bytes 491528 | tf_op jit(solution)/shard_map/ppermute | solution.py:29
  563.6 7.1 %collective-permute-start.40 = (bf16[640,1152]{1,0:T(8,128)(2,1)}, bf16[640,1152]{1,0:T(8,128)(2,1)}, u32[]{:S(2)}, u32[]{:S(2)}) collective-permute-start(bf16[640,1152]{1,0:T(8,128)(2,1)} %pad_maximum_fusion.4), channel_id=1, source_target_pairs={{0,16},{16,0},{1,17},{17,1},{2,18},{18,2},{3,19},{19,3},{4,20},{20... | collective-permute-start | bytes 4423688 | tf_op jit(solution)/shard_map/ppermute | solution.py:29
  588.0 5.9 collective-permute-start.41
  596.4 12.3 %collective-permute-done.41 = bf16[320,1024]{1,0:T(8,128)(2,1)S(1)} collective-permute-done((bf16[320,1024]{1,0:T(8,128)(2,1)S(1)}, bf16[320,1024]{1,0:T(8,128)(2,1)S(1)}, u32[]{:S(2)}, u32[]{:S(2)}) %collective-permute-start.41) | collective-permute-done | bytes 655392 | tf_op jit(solution)/shard_map/ppermute | solution.py:29
  (778 shorter events, 332.9 us)
Async XLA Ops:
  7.2 126.7 %all-gather.3.cloned.1.call-start = ((), (), s32[]{:S(2)}) async-start(), calls=%async_computation.2 | async-start | bytes 4456448 | tf_op jit(solution)/shard_map/all_gather | solution.py:664
  7.9 278.2 %all-gather.5.cloned.1.call-start = ((), (), s32[]{:S(2)}) async-start(), calls=%async_computation.3 | async-start | bytes 8912896 | tf_op jit(solution)/shard_map/all_gather | solution.py:738
  9.9 19.9 %collective-permute-start.1 = (bf16[1,64,768]{2,1,0:T(8,128)(2,1)S(1)}, bf16[1,64,768]{2,1,0:T(8,128)(2,1)}, u32[]{:S(2)}, u32[]{:S(2)}) collective-permute-start(bf16[1,64,768]{2,1,0:T(8,128)(2,1)S(1)} %bitcast.457), channel_id=1, source_target_pairs={{0,8},{2,10},{4,12},{6,14},{8,0},{10,2},{12,4},{14,6},{1,9},{3,11}... | collective-permute-start | bytes 294920 | tf_op jit(solution)/shard_map/ppermute | solution.py:29
  16.5 55.5 %collective-permute-start.16 = (bf16[128,512]{1,0:T(8,128)(2,1)S(1)}, bf16[128,512]{1,0:T(8,128)(2,1)}, u32[]{:S(2)}, u32[]{:S(2)}) collective-permute-start(bf16[128,512]{1,0:T(8,128)(2,1)S(1)} %slice.678), channel_id=1, source_target_pairs={{0,16},{16,0},{1,17},{17,1},{2,18},{18,2},{3,19},{19,3},{4,20},{20... | collective-permute-start | bytes 393224 | tf_op jit(solution)/shard_map/ppermute | solution.py:29
  16.5 22.1 %collective-permute-start = (bf16[320,1024]{1,0:T(8,128)(2,1)}, bf16[320,1024]{1,0:T(8,128)(2,1)S(1)}, u32[]{:S(2)}, u32[]{:S(2)}) collective-permute-start(bf16[320,1024]{1,0:T(8,128)(2,1)} %bitcast.425), channel_id=1, source_target_pairs={{0,1},{1,0},{2,3},{3,2},{4,5},{5,4},{6,7},{7,6},{8,9},{9,8},{10,11... | collective-permute-start | bytes 1966088 | tf_op jit(solution)/shard_map/ppermute | solution.py:29
  133.6 351.3 %reduce-scatter.3.cloned.1.call-start = ((), (), s32[]{:S(2)}) async-start(), calls=%async_computation.4 | async-start | bytes 2228224 | tf_op jit(solution)/shard_map/reduce_scatter | solution.py:816
  166.1 50.4 %collective-permute-start.11 = (bf16[144,768]{1,0:T(8,128)(2,1)}, bf16[144,768]{1,0:T(8,128)(2,1)S(1)}, u32[]{:S(2)}, u32[]{:S(2)}) collective-permute-start(bf16[144,768]{1,0:T(8,128)(2,1)} %maximum_maximum_fusion.rest_0_), channel_id=1, source_target_pairs={{0,4},{2,6},{4,0},{6,2},{8,12},{10,14},{12,8},{14,10},{1,5},{3,7},... | collective-permute-start | bytes 663560 | tf_op jit(solution)/shard_map/ppermute | solution.py:29
  172.6 43.3 %collective-permute-start.19 = (bf16[4,64,1792]{2,1,0:T(8,128)(2,1)S(1)}, bf16[4,64,1792]{2,1,0:T(8,128)(2,1)S(1)}, u32[]{:S(2)}, u32[]{:S(2)}) collective-permute-start(bf16[4,64,1792]{2,1,0:T(8,128)(2,1)S(1)} %bitcast.439), channel_id=1, source_target_pairs={{0,2},{2,0},{4,6},{6,4},{8,10},{10,8},{12,14},{14,12},{1,3},{3,1},... | collective-permute-start | bytes 2752520 | tf_op jit(solution)/shard_map/ppermute | solution.py:29
  216.4 29.2 %collective-permute-start.20 = (bf16[512,1792]{1,0:T(8,128)(2,1)S(1)}, bf16[512,1792]{1,0:T(8,128)(2,1)S(1)}, u32[]{:S(2)}, u32[]{:S(2)}) collective-permute-start(bf16[512,1792]{1,0:T(8,128)(2,1)S(1)} %bitcast.428), channel_id=1, source_target_pairs={{0,16},{16,0},{1,17},{17,1},{2,18},{18,2},{3,19},{19,3},{4,20},{20... | collective-permute-start | bytes 5505032 | tf_op jit(solution)/shard_map/ppermute | solution.py:29
  266.1 64.1 %collective-permute-start.28 = (bf16[320,1024]{1,0:T(8,128)(2,1)}, bf16[320,1024]{1,0:T(8,128)(2,1)}, u32[]{:S(2)}, u32[]{:S(2)}) collective-permute-start(bf16[320,1024]{1,0:T(8,128)(2,1)} %bitcast.83), channel_id=1, source_target_pairs={{0,16},{16,0},{1,17},{17,1},{2,18},{18,2},{3,19},{19,3},{4,20},{20... | collective-permute-start | bytes 1966088 | tf_op jit(solution)/shard_map/ppermute | solution.py:29
  269.7 283.4 %collective-permute-start.34 = (bf16[640,512]{1,0:T(8,128)(2,1)}, bf16[640,512]{1,0:T(8,128)(2,1)}, u32[]{:S(2)}, u32[]{:S(2)}) collective-permute-start(bf16[640,512]{1,0:T(8,128)(2,1)} %get-tuple-element.187), channel_id=1, source_target_pairs={{0,16},{16,0},{1,17},{17,1},{2,18},{18,2},{3,19},{19,3},{4,20},{20... | collective-permute-start | bytes 1966088 | tf_op jit(solution)/shard_map/ppermute | solution.py:29
  310.7 52.3 %collective-permute-start.26 = (bf16[320,4096]{1,0:T(8,128)(2,1)}, bf16[320,4096]{1,0:T(8,128)(2,1)}, u32[]{:S(2)}, u32[]{:S(2)}) collective-permute-start(bf16[320,4096]{1,0:T(8,128)(2,1)} %add_convert_fusion), channel_id=1, source_target_pairs={{0,16},{16,0},{1,17},{17,1},{2,18},{18,2},{3,19},{19,3},{4,20},{20... | collective-permute-start | bytes 7864328 | tf_op jit(solution)/shard_map/ppermute | solution.py:29
  312.5 50.5 %collective-permute-start.25 = (bf16[320,512]{1,0:T(8,128)(2,1)}, bf16[320,512]{1,0:T(8,128)(2,1)}, u32[]{:S(2)}, u32[]{:S(2)}) collective-permute-start(bf16[320,512]{1,0:T(8,128)(2,1)} %get-tuple-element.211), channel_id=1, source_target_pairs={{0,16},{16,0},{1,17},{17,1},{2,18},{18,2},{3,19},{19,3},{4,20},{20... | collective-permute-start | bytes 983048 | tf_op jit(solution)/shard_map/ppermute | solution.py:29
  335.4 191.4 %reduce-scatter.5.cloned.1.call-start = ((), (), s32[]{:S(2)}) async-start(), calls=%async_computation.5 | async-start | bytes 4456448 | tf_op jit(solution)/shard_map/reduce_scatter | solution.py:816
  363.0 21.8 %collective-permute-start.37 = (bf16[2,2,64,1024]{3,2,1,0:T(8,128)(2,1)}, bf16[2,2,64,1024]{3,2,1,0:T(8,128)(2,1)S(1)}, u32[]{:S(2)}, u32[]{:S(2)}) collective-permute-start(bf16[2,2,64,1024]{3,2,1,0:T(8,128)(2,1)} %select_bitcast_fusion.8), channel_id=1, source_target_pairs={{0,2},{2,0},{4,6},{6,4},{8,10},{10,8},{12,14},{14,12},{1,3},{3,1},... | collective-permute-start | bytes 1572872 | tf_op jit(solution)/shard_map/ppermute | solution.py:29
  387.2 39.8 %collective-permute-start.49 = (bf16[2,64,1024]{2,1,0:T(8,128)(2,1)S(1)}, bf16[2,64,1024]{2,1,0:T(8,128)(2,1)S(1)}, u32[]{:S(2)}, u32[]{:S(2)}) collective-permute-start(bf16[2,64,1024]{2,1,0:T(8,128)(2,1)S(1)} %fusion.147), channel_id=1, source_target_pairs={{0,4},{2,6},{4,0},{6,2},{8,12},{10,14},{12,8},{14,10},{1,5},{3,7},... | collective-permute-start | bytes 786440 | tf_op jit(solution)/shard_map/ppermute | solution.py:29
  408.8 46.3 %collective-permute-start.35 = (bf16[144,768]{1,0:T(8,128)(2,1)S(1)}, bf16[144,768]{1,0:T(8,128)(2,1)S(1)}, u32[]{:S(2)}, u32[]{:S(2)}) collective-permute-start(bf16[144,768]{1,0:T(8,128)(2,1)S(1)} %broadcast_add_fusion.4), channel_id=1, source_target_pairs={{0,4},{2,6},{4,0},{6,2},{8,12},{10,14},{12,8},{14,10},{1,5},{3,7},... | collective-permute-start | bytes 663560 | tf_op jit(solution)/shard_map/ppermute | solution.py:29
  422.1 34.2 %collective-permute-start.31 = (bf16[2,2,640,128]{3,2,0,1:T(8,128)(2,1)S(1)}, bf16[2,2,640,128]{3,2,0,1:T(8,128)(2,1)S(1)}, u32[]{:S(2)}, u32[]{:S(2)}) collective-permute-start(bf16[2,2,640,128]{3,2,0,1:T(8,128)(2,1)S(1)} %select_bitcast_fusion.3), channel_id=1, source_target_pairs={{0,2},{2,0},{4,6},{6,4},{8,10},{10,8},{12,14},{14,12},{1,3},{3,1},... | collective-permute-start | bytes 1966088 | tf_op jit(solution)/shard_map/ppermute | solution.py:29
  427.8 103.8 %collective-permute-start.50 = (bf16[64,1024]{1,0:T(8,128)(2,1)}, bf16[64,1024]{1,0:T(8,128)(2,1)}, u32[]{:S(2)}, u32[]{:S(2)}) collective-permute-start(bf16[64,1024]{1,0:T(8,128)(2,1)} %select_bitcast_fusion.31), channel_id=1, source_target_pairs={{0,8},{2,10},{4,12},{6,14},{8,0},{10,2},{12,4},{14,6},{1,9},{3,11}... | collective-permute-start | bytes 393224 | tf_op jit(solution)/shard_map/ppermute | solution.py:29
  455.8 22.1 %collective-permute-start.36 = (bf16[144,768]{1,0:T(8,128)(2,1)S(1)}, bf16[144,768]{1,0:T(8,128)(2,1)S(1)}, u32[]{:S(2)}, u32[]{:S(2)}) collective-permute-start(bf16[144,768]{1,0:T(8,128)(2,1)S(1)} %maximum_maximum_fusion.3), channel_id=1, source_target_pairs={{0,8},{2,10},{4,12},{6,14},{8,0},{10,2},{12,4},{14,6},{1,9},{3,11}... | collective-permute-start | bytes 663560 | tf_op jit(solution)/shard_map/ppermute | solution.py:29
  456.7 26.2 %collective-permute-start.32 = (bf16[2,640,128]{2,1,0:T(8,128)(2,1)S(1)}, bf16[2,640,128]{2,1,0:T(8,128)(2,1)S(1)}, u32[]{:S(2)}, u32[]{:S(2)}) collective-permute-start(bf16[2,640,128]{2,1,0:T(8,128)(2,1)S(1)} %select_bitcast_fusion.15), channel_id=1, source_target_pairs={{0,4},{2,6},{4,0},{6,2},{8,12},{10,14},{12,8},{14,10},{1,5},{3,7},... | collective-permute-start | bytes 983048 | tf_op jit(solution)/shard_map/ppermute | solution.py:29
  531.5 21.6 %collective-permute-start.39 = (bf16[640,1152]{1,0:T(8,128)(2,1)}, bf16[640,1152]{1,0:T(8,128)(2,1)}, u32[]{:S(2)}, u32[]{:S(2)}) collective-permute-start(bf16[640,1152]{1,0:T(8,128)(2,1)} %concatenate.206), channel_id=1, source_target_pairs={{0,16},{16,0},{1,17},{17,1},{2,18},{18,2},{3,19},{19,3},{4,20},{20... | collective-permute-start | bytes 4423688 | tf_op jit(solution)/shard_map/ppermute | solution.py:29
  534.8 25.8 %collective-permute-start.33 = (bf16[640,128]{1,0:T(8,128)(2,1)S(1)}, bf16[640,128]{1,0:T(8,128)(2,1)S(1)}, u32[]{:S(2)}, u32[]{:S(2)}) collective-permute-start(bf16[640,128]{1,0:T(8,128)(2,1)S(1)} %select_bitcast_fusion.26), channel_id=1, source_target_pairs={{0,8},{2,10},{4,12},{6,14},{8,0},{10,2},{12,4},{14,6},{1,9},{3,11}... | collective-permute-start | bytes 491528 | tf_op jit(solution)/shard_map/ppermute | solution.py:29
  588.0 20.8 %collective-permute-start.41 = (bf16[320,1024]{1,0:T(8,128)(2,1)S(1)}, bf16[320,1024]{1,0:T(8,128)(2,1)S(1)}, u32[]{:S(2)}, u32[]{:S(2)}) collective-permute-start(bf16[320,1024]{1,0:T(8,128)(2,1)S(1)} %select_convert_fusion), channel_id=1, source_target_pairs={{0,1},{1,0},{2,3},{3,2},{4,5},{5,4},{6,7},{7,6},{8,9},{9,8},{10,11... | collective-permute-start | bytes 1966088 | tf_op jit(solution)/shard_map/ppermute | solution.py:29
  (201 other events, 1795.1 us)
Sparse Core Ops, SparseCore 0:
  10.2 63.8 all-gather.2
  133.7 99.4 all-gather.4
  335.5 86.8 reduce-scatter.2
  424.5 93.3 reduce-scatter.4

commit v3 on v2

--- a/solution.py
+++ b/solution.py
@@ -63,11 +63,14 @@
     return in_order(value, swap(value, axis, 1), has_bit(axis, 1), dim, jnp.concatenate)
 
 
-def fold(value, axis, bit, dim):
+def fold(value, axis, bit, dim, sents=None):
     high = has_bit(axis, bit)
     first = lax.index_in_dim(value, 0, dim, False)
     second = lax.index_in_dim(value, 1, dim, False)
-    got = swap(jnp.where(high, first, second).astype(low_type), axis, bit)
+    sent = jnp.where(high, first, second).astype(low_type)
+    if sents is not None:
+        sents.append(sent)
+    got = swap(sent, axis, bit)
     return jnp.where(high, second, first).astype(f32) + got.astype(f32)
 
 
@@ -76,17 +79,17 @@
     bits = count.bit_length() - 1
     held = value.reshape((2,) * bits + value.shape[1:])
     left = [1 << (bits - 1 - d) for d in range(bits)]
-    steps = []
+    steps, sents = [], []
     for gate, bit in zip(gates, order):
         dim = left.index(bit)
         if gate is not None:
             held = after(held, gate)
-        held = fold(held, "cp", bit, dim)
+        held = fold(held, "cp", bit, dim, sents)
         left.pop(dim)
         if left:
             held = held.astype(low_type)
         steps.append(held)
-    return held, steps
+    return held, steps, sents
 
 
 def low_first():
@@ -109,6 +112,7 @@
     pre_log, pre_state = jnp.zeros_like(log_decay), jnp.zeros_like(state)
     count = lax.axis_size("cp")
     bit = 1
+    gate = None
 
     def spread(values):
         return dot(jnp.exp(values)[None, :], expander(heads, width), highest)
@@ -119,9 +123,9 @@
         tail = jnp.concatenate([top, rest, jnp.zeros((state.shape[1] - 2 * heads,), low_type)])
         tail = jnp.concatenate([tail[None], jnp.zeros((15, state.shape[1]), low_type)], axis=0)
         sent = jnp.concatenate([state.astype(low_type), tail], axis=0)
-        gate = yield sent
         if gate is not None:
             sent = after(sent, gate)
+        gate = yield sent
         got = swap(sent, "cp", bit)
         got_state = got[:-16].astype(f32)
         got_log = got[-16, :heads].astype(f32) + got[-16, heads : 2 * heads].astype(f32)
@@ -402,12 +406,12 @@
     return jnp.where(left, pair, 0.0), jnp.where(left, 0.0, pair)
 
 
-def ssd_fwd_kernel(xd_ref, b_ref, c_ref, cs_ref, cst_ref, csx_ref, in_ref, *rest):
+def ssd_fwd_kernel(xd_ref, b_ref, c_ref, cs_ref, cst_ref, csx_ref, *rest):
     y_ref, before_ref, s_s = rest[-3:]
 
     @pl.when(pl.program_id(0) == 0)
     def _():
-        s_s[...] = in_ref[...]
+        s_s[...] = jnp.zeros(s_s.shape, f32)
 
     rows = xd_ref.shape[0]
     b, c = b_ref[...], c_ref[...]
@@ -442,14 +446,13 @@
     cst_ref,
     csx_ref,
     before_ref,
-    future_ref,
     *rest,
 ):
     dxd_ref, db_ref, dc_ref, ds_s = rest[-4:]
 
     @pl.when(pl.program_id(0) == 0)
     def _():
-        ds_s[...] = future_ref[...]
+        ds_s[...] = jnp.zeros(ds_s.shape, f32)
 
     rows = xd_ref.shape[0]
     b, c = b_ref[...], c_ref[...]
@@ -490,7 +493,7 @@
     ds_s[...] = jnp.exp(last) * grad_state + t_dot(c, scaled_dy, highest)
 
 
-def ssd_forward(xd, b, c, cs, cst, csx, entering, deps):
+def ssd_forward(xd, b, c, cs, cst, csx, deps):
     length, width = xd.shape
     blocks = length // chunk_len
     heads = cs.shape[1]
@@ -508,7 +511,6 @@
             rows(heads),
             pl.BlockSpec((None, heads, chunk_len), lambda i: (i, 0, 0)),
             rows(width),
-            whole_spec((NST, width)),
         ]
         + any_specs(len(deps)),
         out_specs=[rows(width), pl.BlockSpec((None, NST, width), lambda i: (i, 0, 0))],
@@ -522,10 +524,10 @@
             flops=12 * 3 * length * width * NST, bytes_accessed=20 * length * width, transcendentals=0
         ),
         name="ssd_forward",
-    )(xd, b, c, cs, cst, csx, entering, *deps)
-
-
-def ssd_backward(xd, dy, b, c, cs, cst, csx, before, future, deps):
+    )(xd, b, c, cs, cst, csx, *deps)
+
+
+def ssd_backward(xd, dy, b, c, cs, cst, csx, before, deps):
     length, width = xd.shape
     blocks = length // chunk_len
     heads = cs.shape[1]
@@ -548,7 +550,6 @@
             slabs(heads, chunk_len),
             rows(width),
             slabs(NST, width),
-            whole_spec((NST, width)),
         ]
         + any_specs(len(deps)),
         out_specs=[rows(width), rows(NST), rows(NST)],
@@ -563,7 +564,7 @@
             flops=12 * 8 * length * width * NST, bytes_accessed=24 * length * width, transcendentals=0
         ),
         name="ssd_backward",
-    )(xd, dy, b, c, cs, cst, csx, before, future, *deps)
+    )(xd, dy, b, c, cs, cst, csx, before, *deps)
 
 
 def per_device(
@@ -661,8 +662,7 @@
     handed = swap(out_rows[:, half_cols:], "dp", 1)
     holds = dp_index == hd_index
     out_half = jnp.where(holds, out_rows[:, :half_cols], handed)
-    w_back = lax.all_gather(w_down, ("dp", "cp"), axis=0, tiled=True)
-    w_xs = gather_pair(after(xs_cp, w_back), "dp", 0)
+    w_xs = gather_pair(xs_cp, "dp", 0)
 
     proj = dot(normed1_all, w_misc)
     qkv = proj[:, :qkv_cols]
@@ -726,34 +726,41 @@
     csx_dev = wide(cs_dev)
     dtx = wide(dt_value)
     xd = dtx * x_conv
-    state_local = t_dot(b_conv, jnp.exp(csx_dev[-1:] - csx_dev) * xd, highest)
+    ending_xd = jnp.exp(csx_dev[-1:] - csx_dev) * xd
+    state_local = t_dot(b_conv, ending_xd, highest)
     scan = state_scan(log_dev, state_local, True)
-    in_sent = [next(scan)]
-    while len(in_sent) < n_cp.bit_length():
-        in_sent.append(scan.send(None))
-    state_in = in_sent[-1]
-
-    kk = jnp.concatenate([kv_all[:, :HDIM], kv_all[:, :HDIM]], axis=1)
+    in_sent = next(scan)
+    y_own, before = ssd_forward(xd, b_conv, c_conv, cs, cst, csx, (in_sent,))
+    in_sent = scan.send(y_own)
+
+    kk = after(jnp.concatenate([kv_all[:, :HDIM], kv_all[:, :HDIM]], axis=1), w_xs)
     vv = jnp.concatenate([kv_all[:, HDIM:], kv_all[:, HDIM:]], axis=1)
-    w_gate_up = lax.all_gather(after(after(w_gu, kk), xs_cp), ("dp", "cp"), axis=0, tiled=True)
+    w_gate_up = after(after(w_gu, kk), xs_cp)
+    w_gate_up = lax.all_gather(w_gate_up, ("dp", "cp"), axis=0, tiled=True)
     pairs = [slice(p * 2 * HDIM, (p + 1) * 2 * HDIM) for p in range(q_part // (2 * HDIM))]
-    att_deps = [(in_sent[0],), (in_sent[1],)]
+    att_deps = [(), ()]
     att_outs, lses = [], []
     for cols, deps in zip(pairs, att_deps):
         att_out, lse = attention_forward(
-            where, q_scaled[:, cols], kk, vv, doc_begin, deps + tuple(att_outs)
+            where, q_scaled[:, cols], kk, vv, doc_begin, deps + tuple(att_outs) + (in_sent,)
         )
         att_outs.append(att_out)
         lses.append(lse)
+        in_sent = scan.send(att_out)
+    for last_sent in scan:
+        in_sent = last_sent
+    state_in = in_sent
     att_f32 = jnp.concatenate(att_outs, axis=1)
     att_low = att_f32.astype(low_type)
+
+    w_back = lax.all_gather(after(w_down, att_outs[0]), ("dp", "cp"), axis=0, tiled=True)
 
     shard_rows, out_cols = w_in.shape[0], out_half.size // w_in.shape[0]
     z_out = jnp.concatenate(
         [group(w_in, 0, d_ssm), out_half.reshape(shard_rows, out_cols)], axis=1
     )
-    z_out, _ = gather_cp(after(z_out, kk), (in_sent[0], att_outs[0]))
-    z_out = after(z_out, att_outs[1])
+    z_out, _ = gather_cp(after(z_out, w_misc), (xs_cp, y_own))
+    z_out = after(z_out, att_outs[0])
     z_out_other = swap(z_out, "dp", 1)
     w_z = in_order(
         z_out[:, :x_part], z_out_other[:, :x_part], has_bit("dp", 1), 0, jnp.concatenate
@@ -770,9 +777,8 @@
         axis=0,
     )
 
-    y_core, before = ssd_forward(
-        xd, b_conv, c_conv, cs, cst, csx, state_in, (att_outs[-1],)
-    )
+    state_in = after(after(state_in, w_out), w_z)
+    y_core = y_own + jnp.exp(csx_dev) * dot(c_conv, state_in, highest)
     y_low = (y_core + skip_x * x_conv).astype(low_type).astype(f32)
 
     gate_z = dot(normed1_all, w_z)
@@ -805,7 +811,6 @@
     grad_mid_part, g_norm2 = norm2_pull(grad_normed2)
     grad_mid = grad_out_low.astype(f32) + grad_mid_part
     grad_mid_low = grad_mid.astype(low_type)
-    grad_mid_all = gather_pair(grad_mid_low, "hd", 0)
 
     def rows_by_owner(grad):
         rows, cols = grad.shape
@@ -824,13 +829,21 @@
     def cores(values):
         return jnp.concatenate([values, swap(values, "dp", 1)], axis=0)
 
-    g_down = t_dot(halves_by_core(hidden_low), cores(grad_out_low)).astype(low_type)
-    s_down = to_owner(g_down)
+    g_down = t_dot(halves_by_core(after(hidden_low, grad_mid_low)), cores(grad_out_low))
+    g_down = g_down.astype(low_type)
+    result_low = (x_mid + dot(after(hidden_low, grad_mid_low), w_back)).astype(low_type)
+    grad_mid_all = in_order(
+        after(after(grad_mid_low, g_down), result_low),
+        swap(grad_mid_low, "hd", 1),
+        hd_high,
+        0,
+        jnp.concatenate,
+    )
+    s_down = to_owner(after(g_down, grad_mid_all))
     g_gate_up = t_dot(
-        halves_by_core(after(normed2_low, grad_mid_low)), cores(grad_gate_up)
+        halves_by_core(after(normed2_low, grad_mid_all)), cores(grad_gate_up)
     ).astype(low_type)
     s_gu = to_owner(g_gate_up)
-    result_seq = x_mid + dot(after(hidden_low, grad_mid_low), w_back)
 
     grad_branches = dot_t(grad_mid_all, w_out)
     grad_gated = grad_branches[:, :x_part]
@@ -857,17 +870,12 @@
         grad = t_dot(normed1_half, cores(grad)).astype(low_type)
         return grad.reshape(n_cp, d_model // (2 * n_cp), grad.shape[1])
 
-    g_out = t_dot(after(branches, scaled_dy), grad_mid_all).astype(low_type)
-    g_out = jnp.concatenate(
-        [
-            g_out[:x_part].reshape(n_cp, n_hd, mo_rows // n_hd, d_model),
-            g_out[x_part:].reshape(n_cp, n_hd, ao_rows // n_hd, d_model),
-        ],
-        axis=2,
-    )
-    g_out = fold(g_out, "dp", 1, 1).astype(low_type)
     dqs, dkvs = [], []
-    bwd_deps = (g_gate_up, g_down, g_out)
+    bwd_deps = (g_gate_up, g_down)
+    dxd_own, db_own, dc_own = ssd_backward(
+        xd, grad_y, b_conv, c_conv, cs, cst, csx, before, (future,) + bwd_deps
+    )
+    future = scan.send(dxd_own)
     for p, cols in enumerate(pairs):
         dq, dkv = attention_backward(
             where,
@@ -888,27 +896,26 @@
     for dkv in dkvs[1:]:
         dkv_sum = dkv_sum + dkv.astype(f32)
     dkv_low = dkv_sum.astype(low_type)
-    dkv, dkv_steps = fold_cp(dkv_low, low_first())
+    dkv, dkv_steps, _ = fold_cp(dkv_low, low_first())
     for last_sent in scan:
         future = last_sent
-
-    out_grad, out_folds = fold_cp(g_out, low_first(), (None, dqs[0], dqs[1]) + (None,) * 5)
+    g_out = t_dot(after(branches, dqs[0]), grad_mid_all).astype(low_type)
+    g_out = jnp.concatenate(
+        [
+            g_out[:x_part].reshape(n_cp, n_hd, mo_rows // n_hd, d_model),
+            g_out[x_part:].reshape(n_cp, n_hd, ao_rows // n_hd, d_model),
+        ],
+        axis=2,
+    )
+    g_out = fold(g_out, "dp", 1, 1).astype(low_type)
+    out_grad, out_folds, _ = fold_cp(g_out, low_first(), (dqs[1],) + (None,) * 7)
     s_out = lax.ppermute(out_grad, ("dp", "hd"), [(0, 0), (1, 2), (2, 1), (3, 3)])
     s_mo, s_ao = s_out[: mo_rows // n_hd], s_out[mo_rows // n_hd :]
 
 
-    dxd, db, dc = ssd_backward(
-        xd,
-        grad_y,
-        b_conv,
-        c_conv,
-        cs,
-        cst,
-        csx,
-        before,
-        future,
-        (dqs[-1], out_folds[0], dkv_low, s_down),
-    )
+    dxd = dxd_own + jnp.exp(csx_dev[-1:] - csx_dev) * dot(b_conv, future, highest)
+    db = db_own + dot_t(ending_xd, future, highest)
+    dc = dc_own + dot_t(scaled_dy, state_in, highest)
 
     ddt_direct = per_head(x_conv * dxd)
     dcs = per_head(grad_y * y_core) - dt_value * ddt_direct
@@ -947,13 +954,14 @@
     grad_qkv = jnp.concatenate([dq * score_scale for dq in dqs] + [after(dkv, g_early)], axis=1)
     grad_qkv = (grad_qkv * cosines - half_turn(grad_qkv) * sines).astype(low_type)
     g_late = by_owner(jnp.concatenate([grad_z, grad_qkv], axis=1))
-    r_late, _ = fold_cp(g_late, low_last())
-    r_early, early_steps = fold_cp(g_early, low_first())
+    r_late, late_steps, late_sents = fold_cp(g_late, low_last())
+    r_early, _, early_sents = fold_cp(g_early, low_first())
     grad_misc = jnp.concatenate([grad_qkv, grad_bc_dt], axis=1)
 
-    grad_misc = after(after(grad_misc, g_early), g_late)
+    grad_misc = after(after(grad_misc, early_sents[0]), late_sents[0])
     grad_normed1 = dot_t(grad_z, w_z) + dot_t(grad_misc, w_misc) + dot_t(grad_xs, w_xs)
     grad_normed1 = fold(grad_normed1.reshape(n_hd, tok_count, d_model), "hd", 1, 0)
+    grad_normed1 = after(grad_normed1, late_steps[0])
     _, norm1_pull = jax.vjp(rms_norm, x_in, norm1)
     grad_x_part, g_norm1 = norm1_pull(grad_normed1)
     grad_tokens_out = (grad_mid + grad_x_part).astype(low_type)
@@ -1014,7 +1022,7 @@
         sums.append(flat[begin : begin + s.size].reshape(s.shape))
         begin += s.size
     return (
-        result_seq.astype(low_type)[None],
+        result_low[None],
         grad_tokens_out[None],
         s_in,
         s_dt,

time: 660 us -> 672 us (1.018)
  matrix products: 88.8 us -> 99.3 us
  starting transfers between devices: 144 us -> 135 us
  waiting for transfers between devices: 169 us -> 176 us
    ppermute x54, starting transfers between devices: 138 us -> 126 us  [swap(): return lax.ppermute(value, axis, [(i, i ^ bit) for i in range(count)])]
    dot_general x11 -> x13, matrix products: 21.2 us -> 31.5 us  [dot_t(): lax.dot_general(left, right, (((1,), (1,)), ((), ())), preferred_element_...]
    ppermute x54, waiting for transfers between devices: 167 us -> 176 us  [swap(): return lax.ppermute(value, axis, [(i, i ^ bit) for i in range(count)])]
    slice x21 -> x27, local copies, waits for them, and re-layouts: 15 us -> 18.9 us  [after(): lax.slice(earlier, (0,) * earlier.ndim, (1,) * earlier.ndim).reshape(())]
    dot_general x29 -> x31, matrix products: 38.7 us -> 41 us  [dot(): return jnp.dot(left, right, preferred_element_type=f32, precision=precision)]
    unnamed x333 -> x403, local copies, waits for them, and re-layouts: 19.8 us -> 18.7 us
  transfers between devices with their start and end apart: 61 -> 61, of which waited for: 23 -> 31; matrix products, arithmetic and copies ran while one was open for 36% -> 33% of each run, Pallas kernels for 9% -> 8%
where the time goes in v3:
time: 672 us; the launch traced here: 661 us
  waiting for transfers between devices  176 us (26%)
  starting transfers between devices  135 us (20%)
  matrix products  99.3 us (15%)
  other arithmetic  86.6 us (13%)
  local copies, waits for them, and re-layouts  72.1 us (11%)
  Pallas kernels  55.4 us (8%)
  between operations  36.6 us (5%)
    ppermute x54, waiting for transfers between devices, swap(): return lax.ppermute(value, axis, [(i, i ^ bit) for i in range(count)])  176 us
    ppermute x54, starting transfers between devices, swap(): return lax.ppermute(value, axis, [(i, i ^ bit) for i in range(count)])  126 us
    dot_general x31, matrix products, dot(): return jnp.dot(left, right, preferred_element_type=f32, precision=precision)  41 us
    dot_general x13, matrix products, dot_t(): lax.dot_general(left, right, (((1,), (1,)), ((), ())), preferred_element_...  31.5 us
    dot_general x7, matrix products, t_dot(): lax.dot_general(left, right, (((0,), (0,)), ((), ())), preferred_element_...  26.2 us
    pallas_call x1, Pallas kernels, ssd_backward(): pl.pallas_call(ssd_bwd_kernel, grid=(blocks,), in_specs=[rows(width), row...  20.6 us
    slice x27, local copies, waits for them, and re-layouts, after(): lax.slice(earlier, (0,) * earlier.ndim, (1,) * earlier.ndim).reshape(())  18.9 us
    unnamed x403, local copies, waits for them, and re-layouts  18.7 us
  transfers between devices with their start and end apart: 61, of which 31 were waited for; matrix products, arithmetic and copies ran while one was open for 33% of the time, Pallas kernels for 8%

profile of v3, /device:TPU:0, one launch (start us, length us, event | category | flops | bytes accessed | tf_op | source)
XLA Modules:
  0.0 661.0 jit_solution(17074942178115046226)
XLA Ops:
  38.9 6.4 collective-permute-done.3
  86.8 10.9 %collective-permute-done.14 = bf16[4,640,128]{2,1,0:T(8,128)(2,1)S(1)} collective-permute-done((bf16[4,640,128]{2,1,0:T(8,128)(2,1)S(1)}, bf16[4,640,128]{2,1,0:T(8,128)(2,1)S(1)}, u32[]{:S(2)}, u32[]{:S(2)}) %collective-permute-start.14) | collective-permute-done | bytes 655392 | tf_op jit(solution)/shard_map/ppermute | solution.py:29
  121.2 19.0 %collective-permute-done.17 = bf16[1,64,1792]{2,1,0:T(8,128)(2,1)} collective-permute-done((bf16[1,64,1792]{2,1,0:T(8,128)(2,1)S(1)}, bf16[1,64,1792]{2,1,0:T(8,128)(2,1)}, u32[]{:S(2)}, u32[]{:S(2)}) %collective-permute-start.17) | collective-permute-done | bytes 229408 | tf_op jit(solution)/shard_map/ppermute | solution.py:29
  143.7 18.4 %collective-permute-done.18 = bf16[2,64,1792]{2,1,0:T(8,128)(2,1)S(1)} collective-permute-done((bf16[2,64,1792]{2,1,0:T(8,128)(2,1)S(1)}, bf16[2,64,1792]{2,1,0:T(8,128)(2,1)S(1)}, u32[]{:S(2)}, u32[]{:S(2)}) %collective-permute-start.18) | collective-permute-done | bytes 458784 | tf_op jit(solution)/shard_map/ppermute | solution.py:29
  177.9 10.4 %ssd_forward.1 = (f32[640,768]{1,0:T(8,128)}, f32[5,128,768]{2,1,0:T(8,128)}) custom-call(f32[640,768]{1,0:T(8,128)} %copy-done.11, f32[640,128]{1,0:T(8,128)} %get-tuple-element.157.b_ref, f32[640,128]{1,0:T(8,128)} %get-tuple-element.156.c_ref, f32[640,12]{1,0:T(8,128)} %bitcast.453, f32[5,12,128]{2,1,0:T(8,128)} %copy-done.109, ...), custom_call_target="tpu_custom_call" | custom-call | flops 2264924160 | bytes 9830400 | tf_op jit(solution)/shard_map/ssd_forward/pallas_call | solution.py:504
  203.4 6.6 collective-permute-done.19
  247.1 13.2 %collective-permute-done.22 = bf16[320,1024]{1,0:T(8,128)(2,1)} collective-permute-done((bf16[320,1024]{1,0:T(8,128)(2,1)S(1)}, bf16[320,1024]{1,0:T(8,128)(2,1)}, u32[]{:S(2)}, u32[]{:S(2)}) %collective-permute-start.22) | collective-permute-done | bytes 655392 | tf_op jit(solution)/shard_map/ppermute | solution.py:29
  263.0 8.9 %fusion.268 = f32[320,4096]{1,0:T(8,128)} fusion(bf16[1024,4096]{1,0:T(8,128)(2,1)} %all-gather.3.cloned.1.call-done, f32[320,1024]{1,0:T(8,128)S(1)} %get-tuple-element.135, f32[1024]{0:T(1024)S(1)} %copy-done.152, f32[320]{0:T(512)S(1)} %fusion.214), kind=kOutput, calls=%fused_computation.611 | convolution fusion | flops 2685337600 | bytes 14947584 | tf_op jit(solution)/shard_map/dot_general | solution.py:191
  271.9 6.4 fusion.152
  314.0 8.2 %convolution_convert_fusion.rest_1_.rest_0_ = bf16[512,4096]{1,0:T(8,128)(2,1)} fusion(bf16[320,4096]{1,0:T(8,128)(2,1)} %collective-permute-done.28, bf16[320,4096]{1,0:T(8,128)(2,1)} %add_convert_fusion, bf16[320,512]{1,0:T(8,128)(2,1)S(1)} %collective-permute-done.27, bf16[320,512]{1,0:T(8,128)(2,1)S(1)} %get-tuple-element.191), kind=kOutput, calls=%fused_computation.1 | convolution fusion | flops 2698248192 | bytes 10092544 | tf_op jit(solution)/shard_map/dot_general | solution.py:171
  368.4 20.6 %ssd_backward.1 = (f32[640,768]{1,0:T(8,128)}, f32[640,128]{1,0:T(8,128)}, f32[640,128]{1,0:T(8,128)}) custom-call(f32[640,768]{1,0:T(8,128)} %copy-done.11, f32[640,768]{1,0:T(8,128)} %convert_element_type.824.dy_ref, f32[640,128]{1,0:T(8,128)} %get-tuple-element.157.b_ref, f32[640,128]{1,0:T(8,128)} %get-tuple-element.156.c_ref, f32[640,12]{1,0:T(8,128)} %bitcast.454, ...), custom_call_target="tpu_custom_call" | custom-call | flops 6039797760 | bytes 11796480 | tf_op jit(solution)/shard_map/ssd_backward/pallas_call | solution.py:541
  391.6 9.7 %collective-permute-start.30 = (bf16[144,768]{1,0:T(8,128)(2,1)}, bf16[144,768]{1,0:T(8,128)(2,1)S(1)}, u32[]{:S(2)}, u32[]{:S(2)}) collective-permute-start(bf16[144,768]{1,0:T(8,128)(2,1)} %maximum_add_fusion.12.rest_2_), channel_id=1, source_target_pairs={{0,4},{2,6},{4,0},{6,2},{8,12},{10,14},{12,8},{14,10},{1,5},{3,7},... | collective-permute-start | bytes 663560 | tf_op jit(solution)/shard_map/ppermute | solution.py:29
  401.3 6.9 %attention_backward.2 = (f32[640,128]{1,0:T(8,128)}, bf16[5120,128]{1,0:T(8,128)(2,1)}) custom-call(s32[2]{0:T(128)} %pad_add_fusion.4.where_ref, bf16[640,128]{1,0:T(8,128)(2,1)} %get-tuple-element.213.q_ref, bf16[640,128]{1,0:T(8,128)(2,1)} %get-tuple-element.169.do_ref, bf16[5120,128]{1,0:T(8,128)(2,1)} %copy-done.92, ...), custom_call_target="tpu_custom_call" | custom-call | flops 33554432000 | bytes 2621440 | tf_op jit(solution)/shard_map/attention_backward/pallas_call | solution.py:366
  419.6 20.5 %collective-permute-start.35 = (bf16[144,768]{1,0:T(8,128)(2,1)S(1)}, bf16[144,768]{1,0:T(8,128)(2,1)S(1)}, u32[]{:S(2)}, u32[]{:S(2)}) collective-permute-start(bf16[144,768]{1,0:T(8,128)(2,1)S(1)} %maximum_add_fusion.13.rest_0_), channel_id=1, source_target_pairs={{0,8},{2,10},{4,12},{6,14},{8,0},{10,2},{12,4},{14,6},{1,9},{3,11}... | collective-permute-start | bytes 663560 | tf_op jit(solution)/shard_map/ppermute | solution.py:29
  440.1 6.6 %attention_backward.3 = (f32[640,128]{1,0:T(8,128)}, bf16[5120,128]{1,0:T(8,128)(2,1)}) custom-call(s32[2]{0:T(128)} %pad_add_fusion.4.where_ref, bf16[640,128]{1,0:T(8,128)(2,1)} %get-tuple-element.212.q_ref, bf16[640,128]{1,0:T(8,128)(2,1)} %get-tuple-element.170.do_ref, bf16[5120,128]{1,0:T(8,128)(2,1)} %copy-done.92, ...), custom_call_target="tpu_custom_call" | custom-call | flops 33554432000 | bytes 2621440 | tf_op jit(solution)/shard_map/attention_backward/pallas_call | solution.py:366
  451.5 8.3 %collective-permute-start.31 = (bf16[2,2,640,128]{3,2,0,1:T(8,128)(2,1)}, bf16[2,2,640,128]{3,2,0,1:T(8,128)(2,1)}, u32[]{:S(2)}, u32[]{:S(2)}) collective-permute-start(bf16[2,2,640,128]{3,2,0,1:T(8,128)(2,1)} %select_bitcast_fusion.3), channel_id=1, source_target_pairs={{0,2},{2,0},{4,6},{6,4},{8,10},{10,8},{12,14},{14,12},{1,3},{3,1},... | collective-permute-start | bytes 1966088 | tf_op jit(solution)/shard_map/ppermute | solution.py:29
  473.3 8.2 %collective-permute-done.31 = bf16[2,2,640,128]{3,2,0,1:T(8,128)(2,1)} collective-permute-done((bf16[2,2,640,128]{3,2,0,1:T(8,128)(2,1)}, bf16[2,2,640,128]{3,2,0,1:T(8,128)(2,1)}, u32[]{:S(2)}, u32[]{:S(2)}) %collective-permute-start.31) | collective-permute-done | bytes 655392 | tf_op jit(solution)/shard_map/ppermute | solution.py:29
  483.4 14.0 %collective-permute-start.32 = (bf16[2,640,128]{2,1,0:T(8,128)(2,1)S(1)}, bf16[2,640,128]{2,1,0:T(8,128)(2,1)S(1)}, u32[]{:S(2)}, u32[]{:S(2)}) collective-permute-start(bf16[2,640,128]{2,1,0:T(8,128)(2,1)S(1)} %select_bitcast_fusion.14), channel_id=1, source_target_pairs={{0,4},{2,6},{4,0},{6,2},{8,12},{10,14},{12,8},{14,10},{1,5},{3,7},... | collective-permute-start | bytes 983048 | tf_op jit(solution)/shard_map/ppermute | solution.py:29
  516.1 9.0 %collective-permute-done.48 = bf16[2,2,64,1024]{3,2,1,0:T(8,128)(2,1)S(1)} collective-permute-done((bf16[2,2,64,1024]{3,2,1,0:T(8,128)(2,1)S(1)}, bf16[2,2,64,1024]{3,2,1,0:T(8,128)(2,1)S(1)}, u32[]{:S(2)}, u32[]{:S(2)}) %collective-permute-start.48) | collective-permute-done | bytes 524320 | tf_op jit(solution)/shard_map/ppermute | solution.py:29
  534.5 6.4 collective-permute-done.49
  541.0 11.0 %collective-permute-start.50 = (bf16[64,1024]{1,0:T(8,128)(2,1)S(1)}, bf16[64,1024]{1,0:T(8,128)(2,1)S(1)}, u32[]{:S(2)}, u32[]{:S(2)}) collective-permute-start(bf16[64,1024]{1,0:T(8,128)(2,1)S(1)} %select_bitcast_fusion.29), channel_id=1, source_target_pairs={{0,8},{2,10},{4,12},{6,14},{8,0},{10,2},{12,4},{14,6},{1,9},{3,11}... | collective-permute-start | bytes 393224 | tf_op jit(solution)/shard_map/ppermute | solution.py:29
  552.1 10.6 %collective-permute-done.50 = bf16[64,1024]{1,0:T(8,128)(2,1)S(1)} collective-permute-done((bf16[64,1024]{1,0:T(8,128)(2,1)S(1)}, bf16[64,1024]{1,0:T(8,128)(2,1)S(1)}, u32[]{:S(2)}, u32[]{:S(2)}) %collective-permute-start.50) | collective-permute-done | bytes 131104 | tf_op jit(solution)/shard_map/ppermute | solution.py:29
  575.8 8.7 %collective-permute-done.43 = bf16[2,2,64,1152]{3,2,0,1:T(8,128)(2,1)S(1)} collective-permute-done((bf16[2,2,64,1152]{3,2,0,1:T(8,128)(2,1)S(1)}, bf16[2,2,64,1152]{3,2,0,1:T(8,128)(2,1)S(1)}, u32[]{:S(2)}, u32[]{:S(2)}) %collective-permute-start.43) | collective-permute-done | bytes 589856 | tf_op jit(solution)/shard_map/ppermute | solution.py:29
  609.1 6.7 %collective-permute-done.40 = bf16[2,2,64,1152]{3,2,0,1:T(8,128)(2,1)S(1)} collective-permute-done((bf16[2,2,64,1152]{3,2,0,1:T(8,128)(2,1)S(1)}, bf16[2,2,64,1152]{3,2,0,1:T(8,128)(2,1)S(1)}, u32[]{:S(2)}, u32[]{:S(2)}) %collective-permute-start.40) | collective-permute-done | bytes 589856 | tf_op jit(solution)/shard_map/ppermute | solution.py:29
  (854 shorter events, 369.3 us)
Async XLA Ops:
  7.2 255.8 %all-gather.3.cloned.1.call-start = ((), (), s32[]{:S(2)}) async-start(), calls=%async_computation.2 | async-start | bytes 8912896 | tf_op jit(solution)/shard_map/all_gather | solution.py:739
  77.6 20.1 %collective-permute-start.14 = (bf16[4,640,128]{2,1,0:T(8,128)(2,1)S(1)}, bf16[4,640,128]{2,1,0:T(8,128)(2,1)S(1)}, u32[]{:S(2)}, u32[]{:S(2)}) collective-permute-start(bf16[4,640,128]{2,1,0:T(8,128)(2,1)S(1)} %bitcast.446), channel_id=1, source_target_pairs={{0,2},{2,0},{4,6},{6,4},{8,10},{10,8},{12,14},{14,12},{1,3},{3,1},... | collective-permute-start | bytes 1966088 | tf_op jit(solution)/shard_map/ppermute | solution.py:29
  105.8 166.1 %all-gather.5.cloned.1.call-start = ((), (), s32[]{:S(2)}) async-start(), calls=%async_computation.3 | async-start | bytes 4456448 | tf_op jit(solution)/shard_map/all_gather | solution.py:756
  114.3 25.8 %collective-permute-start.17 = (bf16[1,64,1792]{2,1,0:T(8,128)(2,1)S(1)}, bf16[1,64,1792]{2,1,0:T(8,128)(2,1)}, u32[]{:S(2)}, u32[]{:S(2)}) collective-permute-start(bf16[1,64,1792]{2,1,0:T(8,128)(2,1)S(1)} %maximum_add_fusion.9), channel_id=1, source_target_pairs={{0,8},{2,10},{4,12},{6,14},{8,0},{10,2},{12,4},{14,6},{1,9},{3,11}... | collective-permute-start | bytes 688136 | tf_op jit(solution)/shard_map/ppermute | solution.py:29
  141.2 20.9 %collective-permute-start.18 = (bf16[2,64,1792]{2,1,0:T(8,128)(2,1)S(1)}, bf16[2,64,1792]{2,1,0:T(8,128)(2,1)S(1)}, u32[]{:S(2)}, u32[]{:S(2)}) collective-permute-start(bf16[2,64,1792]{2,1,0:T(8,128)(2,1)S(1)} %fusion.121), channel_id=1, source_target_pairs={{0,4},{2,6},{4,0},{6,2},{8,12},{10,14},{12,8},{14,10},{1,5},{3,7},... | collective-permute-start | bytes 1376264 | tf_op jit(solution)/shard_map/ppermute | solution.py:29
  191.3 18.7 %collective-permute-start.19 = (bf16[4,64,1792]{2,1,0:T(8,128)(2,1)}, bf16[4,64,1792]{2,1,0:T(8,128)(2,1)}, u32[]{:S(2)}, u32[]{:S(2)}) collective-permute-start(bf16[4,64,1792]{2,1,0:T(8,128)(2,1)} %bitcast.73), channel_id=1, source_target_pairs={{0,2},{2,0},{4,6},{6,4},{8,10},{10,8},{12,14},{14,12},{1,3},{3,1},... | collective-permute-start | bytes 2752520 | tf_op jit(solution)/shard_map/ppermute | solution.py:29
  200.8 324.6 %reduce-scatter.3.cloned.1.call-start = ((), (), s32[]{:S(2)}) async-start(), calls=%async_computation.4 | async-start | bytes 4456448 | tf_op jit(solution)/shard_map/reduce_scatter | solution.py:821
  213.5 19.2 %collective-permute-start.15 = (bf16[144,768]{1,0:T(8,128)(2,1)}, bf16[144,768]{1,0:T(8,128)(2,1)S(1)}, u32[]{:S(2)}, u32[]{:S(2)}) collective-permute-start(bf16[144,768]{1,0:T(8,128)(2,1)} %maximum_add_fusion.11.rest_1_), channel_id=1, source_target_pairs={{0,8},{2,10},{4,12},{6,14},{8,0},{10,2},{12,4},{14,6},{1,9},{3,11}... | collective-permute-start | bytes 663560 | tf_op jit(solution)/shard_map/ppermute | solution.py:29
  247.1 52.6 %collective-permute-start.25 = (bf16[320,1024]{1,0:T(8,128)(2,1)}, bf16[320,1024]{1,0:T(8,128)(2,1)}, u32[]{:S(2)}, u32[]{:S(2)}) collective-permute-start(bf16[320,1024]{1,0:T(8,128)(2,1)} %bitcast.84), channel_id=1, source_target_pairs={{0,16},{16,0},{1,17},{17,1},{2,18},{18,2},{3,19},{19,3},{4,20},{20... | collective-permute-start | bytes 1966088 | tf_op jit(solution)/shard_map/ppermute | solution.py:29
  280.3 33.7 %collective-permute-start.28 = (bf16[320,4096]{1,0:T(8,128)(2,1)}, bf16[320,4096]{1,0:T(8,128)(2,1)}, u32[]{:S(2)}, u32[]{:S(2)}) collective-permute-start(bf16[320,4096]{1,0:T(8,128)(2,1)} %add_convert_fusion), channel_id=1, source_target_pairs={{0,16},{16,0},{1,17},{17,1},{2,18},{18,2},{3,19},{19,3},{4,20},{20... | collective-permute-start | bytes 7864328 | tf_op jit(solution)/shard_map/ppermute | solution.py:29
  292.7 17.1 %collective-permute-start.23 = (bf16[320,1024]{1,0:T(8,128)(2,1)}, bf16[320,1024]{1,0:T(8,128)(2,1)S(1)}, u32[]{:S(2)}, u32[]{:S(2)}) collective-permute-start(bf16[320,1024]{1,0:T(8,128)(2,1)} %copy-done.74), channel_id=1, source_target_pairs={{0,1},{1,0},{2,3},{3,2},{4,5},{5,4},{6,7},{7,6},{8,9},{9,8},{10,11... | collective-permute-start | bytes 1966088 | tf_op jit(solution)/shard_map/ppermute | solution.py:29
  322.2 268.2 %reduce-scatter.5.cloned.1.call-start = ((), (), s32[]{:S(2)}) async-start(), calls=%async_computation.5 | async-start | bytes 2228224 | tf_op jit(solution)/shard_map/reduce_scatter | solution.py:821
  325.2 242.0 %collective-permute-start.34 = (bf16[640,512]{1,0:T(8,128)(2,1)}, bf16[640,512]{1,0:T(8,128)(2,1)}, u32[]{:S(2)}, u32[]{:S(2)}) collective-permute-start(bf16[640,512]{1,0:T(8,128)(2,1)} %get-tuple-element.166), channel_id=1, source_target_pairs={{0,16},{16,0},{1,17},{17,1},{2,18},{18,2},{3,19},{19,3},{4,20},{20... | collective-permute-start | bytes 1966088 | tf_op jit(solution)/shard_map/ppermute | solution.py:29
  391.6 27.2 %collective-permute-start.30 = (bf16[144,768]{1,0:T(8,128)(2,1)}, bf16[144,768]{1,0:T(8,128)(2,1)S(1)}, u32[]{:S(2)}, u32[]{:S(2)}) collective-permute-start(bf16[144,768]{1,0:T(8,128)(2,1)} %maximum_add_fusion.12.rest_2_), channel_id=1, source_target_pairs={{0,4},{2,6},{4,0},{6,2},{8,12},{10,14},{12,8},{14,10},{1,5},{3,7},... | collective-permute-start | bytes 663560 | tf_op jit(solution)/shard_map/ppermute | solution.py:29
  414.7 93.8 %collective-permute-start.47 = (bf16[8,64,1024]{2,1,0:T(8,128)(2,1)}, bf16[8,64,1024]{2,1,0:T(8,128)(2,1)}, u32[]{:S(2)}, u32[]{:S(2)}) collective-permute-start(bf16[8,64,1024]{2,1,0:T(8,128)(2,1)} %select_bitcast_fusion), channel_id=1, source_target_pairs={{0,16},{16,0},{1,17},{17,1},{2,18},{18,2},{3,19},{19,3},{4,20},{20... | collective-permute-start | bytes 3145736 | tf_op jit(solution)/shard_map/ppermute | solution.py:29
  419.6 40.9 %collective-permute-start.35 = (bf16[144,768]{1,0:T(8,128)(2,1)S(1)}, bf16[144,768]{1,0:T(8,128)(2,1)S(1)}, u32[]{:S(2)}, u32[]{:S(2)}) collective-permute-start(bf16[144,768]{1,0:T(8,128)(2,1)S(1)} %maximum_add_fusion.13.rest_0_), channel_id=1, source_target_pairs={{0,8},{2,10},{4,12},{6,14},{8,0},{10,2},{12,4},{14,6},{1,9},{3,11}... | collective-permute-start | bytes 663560 | tf_op jit(solution)/shard_map/ppermute | solution.py:29
  451.5 30.0 %collective-permute-start.31 = (bf16[2,2,640,128]{3,2,0,1:T(8,128)(2,1)}, bf16[2,2,640,128]{3,2,0,1:T(8,128)(2,1)}, u32[]{:S(2)}, u32[]{:S(2)}) collective-permute-start(bf16[2,2,640,128]{3,2,0,1:T(8,128)(2,1)} %select_bitcast_fusion.3), channel_id=1, source_target_pairs={{0,2},{2,0},{4,6},{6,4},{8,10},{10,8},{12,14},{14,12},{1,3},{3,1},... | collective-permute-start | bytes 1966088 | tf_op jit(solution)/shard_map/ppermute | solution.py:29
  483.4 31.3 %collective-permute-start.32 = (bf16[2,640,128]{2,1,0:T(8,128)(2,1)S(1)}, bf16[2,640,128]{2,1,0:T(8,128)(2,1)S(1)}, u32[]{:S(2)}, u32[]{:S(2)}) collective-permute-start(bf16[2,640,128]{2,1,0:T(8,128)(2,1)S(1)} %select_bitcast_fusion.14), channel_id=1, source_target_pairs={{0,4},{2,6},{4,0},{6,2},{8,12},{10,14},{12,8},{14,10},{1,5},{3,7},... | collective-permute-start | bytes 983048 | tf_op jit(solution)/shard_map/ppermute | solution.py:29
  530.8 36.4 %collective-permute-start.37 = (bf16[640,1152]{1,0:T(8,128)(2,1)}, bf16[640,1152]{1,0:T(8,128)(2,1)S(1)}, u32[]{:S(2)}, u32[]{:S(2)}) collective-permute-start(bf16[640,1152]{1,0:T(8,128)(2,1)} %concatenate.205), channel_id=1, source_target_pairs={{0,16},{16,0},{1,17},{17,1},{2,18},{18,2},{3,19},{19,3},{4,20},{20... | collective-permute-start | bytes 4423688 | tf_op jit(solution)/shard_map/ppermute | solution.py:29
  541.0 21.6 %collective-permute-start.50 = (bf16[64,1024]{1,0:T(8,128)(2,1)S(1)}, bf16[64,1024]{1,0:T(8,128)(2,1)S(1)}, u32[]{:S(2)}, u32[]{:S(2)}) collective-permute-start(bf16[64,1024]{1,0:T(8,128)(2,1)S(1)} %select_bitcast_fusion.29), channel_id=1, source_target_pairs={{0,8},{2,10},{4,12},{6,14},{8,0},{10,2},{12,4},{14,6},{1,9},{3,11}... | collective-permute-start | bytes 393224 | tf_op jit(solution)/shard_map/ppermute | solution.py:29
  552.0 20.7 %collective-permute-start.33 = (bf16[640,128]{1,0:T(8,128)(2,1)S(1)}, bf16[640,128]{1,0:T(8,128)(2,1)S(1)}, u32[]{:S(2)}, u32[]{:S(2)}) collective-permute-start(bf16[640,128]{1,0:T(8,128)(2,1)S(1)} %select_bitcast_fusion.24), channel_id=1, source_target_pairs={{0,8},{2,10},{4,12},{6,14},{8,0},{10,2},{12,4},{14,6},{1,9},{3,11}... | collective-permute-start | bytes 491528 | tf_op jit(solution)/shard_map/ppermute | solution.py:29
  563.4 23.9 %collective-permute-start.51 = (f32[64,1024]{1,0:T(8,128)}, f32[64,1024]{1,0:T(8,128)}, u32[]{:S(2)}, u32[]{:S(2)}) collective-permute-start(f32[64,1024]{1,0:T(8,128)} %convert_add_fusion.18), channel_id=1, source_target_pairs={{0,0},{1,16},{16,1},{17,17},{2,2},{3,18},{18,3},{19,19},{4,4},{5,2... | collective-permute-start | bytes 786440 | tf_op jit(solution)/shard_map/ppermute | solution.py:912
  575.8 20.1 %collective-permute-start.38 = (bf16[640,1152]{1,0:T(8,128)(2,1)}, bf16[640,1152]{1,0:T(8,128)(2,1)}, u32[]{:S(2)}, u32[]{:S(2)}) collective-permute-start(bf16[640,1152]{1,0:T(8,128)(2,1)} %pad_maximum_fusion.4), channel_id=1, source_target_pairs={{0,16},{16,0},{1,17},{17,1},{2,18},{18,2},{3,19},{19,3},{4,20},{20... | collective-permute-start | bytes 4423688 | tf_op jit(solution)/shard_map/ppermute | solution.py:29
  623.5 17.9 %collective-permute-start.41 = (bf16[2,64,1152]{2,1,0:T(8,128)(2,1)S(1)}, bf16[2,64,1152]{2,1,0:T(8,128)(2,1)S(1)}, u32[]{:S(2)}, u32[]{:S(2)}) collective-permute-start(bf16[2,64,1152]{2,1,0:T(8,128)(2,1)S(1)} %fusion.144), channel_id=1, source_target_pairs={{0,8},{2,10},{4,12},{6,14},{8,0},{10,2},{12,4},{14,6},{1,9},{3,11}... | collective-permute-start | bytes 884744 | tf_op jit(solution)/shard_map/ppermute | solution.py:29
  (236 other events, 2274.6 us)
Sparse Core Ops, SparseCore 0:
  105.9 87.9 all-gather.2
  200.9 64.3 all-gather.4
  322.4 115.8 reduce-scatter.2
  440.4 81.1 reduce-scatter.4

commit v4 on v3

--- a/solution.py
+++ b/solution.py
@@ -654,7 +654,7 @@
         ],
         axis=1,
     )
-    misc_cp, _ = gather_cp(shard_misc, (where, normed1_all))
+    misc_cp, misc_steps = gather_cp(shard_misc, (where, normed1_all))
     w_misc = gather_pair(after(after(misc_cp, cosines), normed1_rim), "dp", 0)
     xs_cp, xs_steps = gather_cp(after(group(w_in, d_ssm, d_ssm), w_misc))
     out_rows = jnp.concatenate([w_mo, w_ao], axis=0)
@@ -662,6 +662,14 @@
     handed = swap(out_rows[:, half_cols:], "dp", 1)
     holds = dp_index == hd_index
     out_half = jnp.where(holds, out_rows[:, :half_cols], handed)
+    shard_rows, out_cols = w_in.shape[0], out_half.size // w_in.shape[0]
+    z_out = jnp.concatenate(
+        [group(w_in, 0, d_ssm), out_half.reshape(shard_rows, out_cols)], axis=1
+    )
+    z_out = lax.all_gather(after(z_out, misc_steps[1]), ("dp", "cp"), axis=0, tiled=True)
+    w_z = z_out[:, :x_part]
+    out_sides = z_out[:, x_part:].reshape(2, -1, half_cols)
+    w_out = in_order(out_sides[0], out_sides[1], hd_high, 1, jnp.concatenate)
     w_xs = gather_pair(xs_cp, "dp", 0)
 
     proj = dot(normed1_all, w_misc)
@@ -738,7 +746,7 @@
     w_gate_up = after(after(w_gu, kk), xs_cp)
     w_gate_up = lax.all_gather(w_gate_up, ("dp", "cp"), axis=0, tiled=True)
     pairs = [slice(p * 2 * HDIM, (p + 1) * 2 * HDIM) for p in range(q_part // (2 * HDIM))]
-    att_deps = [(), ()]
+    att_deps = [(z_out,), ()]
     att_outs, lses = [], []
     for cols, deps in zip(pairs, att_deps):
         att_out, lse = attention_forward(
@@ -755,18 +763,7 @@
 
     w_back = lax.all_gather(after(w_down, att_outs[0]), ("dp", "cp"), axis=0, tiled=True)
 
-    shard_rows, out_cols = w_in.shape[0], out_half.size // w_in.shape[0]
-    z_out = jnp.concatenate(
-        [group(w_in, 0, d_ssm), out_half.reshape(shard_rows, out_cols)], axis=1
-    )
-    z_out, _ = gather_cp(after(z_out, w_misc), (xs_cp, y_own))
-    z_out = after(z_out, att_outs[0])
-    z_out_other = swap(z_out, "dp", 1)
-    w_z = in_order(
-        z_out[:, :x_part], z_out_other[:, :x_part], has_bit("dp", 1), 0, jnp.concatenate
-    )
-    out_sides = [a[:, x_part:].reshape(-1, half_cols) for a in (z_out, z_out_other)]
-    w_out = in_order(*out_sides, jnp.logical_not(holds), 1, jnp.concatenate)
+
     mo_rows, ao_rows = w_mo.shape[0], w_ao.shape[0]
     w_out = w_out.reshape(n_cp, mo_rows + ao_rows, d_model)
     w_out = jnp.concatenate(
@@ -777,7 +774,7 @@
         axis=0,
     )
 
-    state_in = after(after(state_in, w_out), w_z)
+    state_in = after(state_in, w_out)
     y_core = y_own + jnp.exp(csx_dev) * dot(c_conv, state_in, highest)
     y_low = (y_core + skip_x * x_conv).astype(low_type).astype(f32)
 
@@ -871,7 +868,16 @@
         return grad.reshape(n_cp, d_model // (2 * n_cp), grad.shape[1])
 
     dqs, dkvs = [], []
-    bwd_deps = (g_gate_up, g_down)
+    g_out = t_dot(branches, grad_mid_all).astype(low_type)
+    g_out = jnp.concatenate(
+        [
+            g_out[:x_part].reshape(n_cp, n_hd, mo_rows // n_hd, d_model),
+            g_out[x_part:].reshape(n_cp, n_hd, ao_rows // n_hd, d_model),
+        ],
+        axis=2,
+    )
+    g_out = fold(g_out, "dp", 1, 1).astype(low_type)
+    bwd_deps = (g_gate_up, g_down, g_out)
     dxd_own, db_own, dc_own = ssd_backward(
         xd, grad_y, b_conv, c_conv, cs, cst, csx, before, (future,) + bwd_deps
     )
@@ -899,16 +905,7 @@
     dkv, dkv_steps, _ = fold_cp(dkv_low, low_first())
     for last_sent in scan:
         future = last_sent
-    g_out = t_dot(after(branches, dqs[0]), grad_mid_all).astype(low_type)
-    g_out = jnp.concatenate(
-        [
-            g_out[:x_part].reshape(n_cp, n_hd, mo_rows // n_hd, d_model),
-            g_out[x_part:].reshape(n_cp, n_hd, ao_rows // n_hd, d_model),
-        ],
-        axis=2,
-    )
-    g_out = fold(g_out, "dp", 1, 1).astype(low_type)
-    out_grad, out_folds, _ = fold_cp(g_out, low_first(), (dqs[1],) + (None,) * 7)
+    out_grad, out_folds, _ = fold_cp(g_out, low_first(), (None, dxd_own, dqs[0]) + (None,) * 5)
     s_out = lax.ppermute(out_grad, ("dp", "hd"), [(0, 0), (1, 2), (2, 1), (3, 3)])
     s_mo, s_ao = s_out[: mo_rows // n_hd], s_out[mo_rows // n_hd :]
 

time: 672 us -> 620 us (0.923)
  waiting for transfers between devices: 176 us -> 144 us
  starting transfers between devices: 135 us -> 122 us
    ppermute x54 -> x50, waiting for transfers between devices: 176 us -> 138 us  [swap(): return lax.ppermute(value, axis, [(i, i ^ bit) for i in range(count)])]
    ppermute x54 -> x50, starting transfers between devices: 126 us -> 116 us  [swap(): return lax.ppermute(value, axis, [(i, i ^ bit) for i in range(count)])]
    unnamed x403 -> x381, local copies, waits for them, and re-layouts: 18.7 us -> 14.6 us
    slice x27 -> x26, local copies, waits for them, and re-layouts: 18.9 us -> 18.4 us  [after(): lax.slice(earlier, (0,) * earlier.ndim, (1,) * earlier.ndim).reshape(())]
  transfers between devices with their start and end apart: 61 -> 58, of which waited for: 31 -> 32; matrix products, arithmetic and copies ran while one was open for 33% -> 35% of each run, Pallas kernels for 8% -> 9%
where the time goes in v4:
time: 620 us; the launch traced here: 609 us
  waiting for transfers between devices  144 us (23%)
  starting transfers between devices  122 us (20%)
  matrix products  101 us (16%)
  other arithmetic  81.9 us (13%)
  local copies, waits for them, and re-layouts  68.5 us (11%)
  Pallas kernels  55.4 us (9%)
  between operations  35.9 us (6%)
    ppermute x50, waiting for transfers between devices, swap(): return lax.ppermute(value, axis, [(i, i ^ bit) for i in range(count)])  138 us
    ppermute x50, starting transfers between devices, swap(): return lax.ppermute(value, axis, [(i, i ^ bit) for i in range(count)])  116 us
    dot_general x31, matrix products, dot(): return jnp.dot(left, right, preferred_element_type=f32, precision=precision)  43.5 us
    dot_general x13, matrix products, dot_t(): lax.dot_general(left, right, (((1,), (1,)), ((), ())), preferred_element_...  28.8 us
    dot_general x7, matrix products, t_dot(): lax.dot_general(left, right, (((0,), (0,)), ((), ())), preferred_element_...  27.6 us
    pallas_call x1, Pallas kernels, ssd_backward(): pl.pallas_call(ssd_bwd_kernel, grid=(blocks,), in_specs=[rows(width), row...  20.5 us
    slice x26, local copies, waits for them, and re-layouts, after(): lax.slice(earlier, (0,) * earlier.ndim, (1,) * earlier.ndim).reshape(())  18.4 us
    unnamed x381, local copies, waits for them, and re-layouts  14.6 us
  transfers between devices with their start and end apart: 58, of which 32 were waited for; matrix products, arithmetic and copies ran while one was open for 35% of the time, Pallas kernels for 9%

profile of v4, /device:TPU:0, one launch (start us, length us, event | category | flops | bytes accessed | tf_op | source)
XLA Modules:
  0.0 609.0 jit_solution(11698423188974665434)
XLA Ops:
  38.9 6.4 %collective-permute-done.3 = bf16[4,64,768]{2,1,0:T(8,128)(2,1)S(1)} collective-permute-done((bf16[4,64,768]{2,1,0:T(8,128)(2,1)S(1)}, bf16[4,64,768]{2,1,0:T(8,128)(2,1)S(1)}, u32[]{:S(2)}, u32[]{:S(2)}) %collective-permute-start.3) | collective-permute-done | bytes 393248 | tf_op jit(solution)/shard_map/ppermute | solution.py:29
  69.9 11.2 %collective-permute-done.12 = bf16[1,640,128]{2,1,0:T(8,128)(2,1)S(1)} collective-permute-done((bf16[1,640,128]{2,1,0:T(8,128)(2,1)S(1)}, bf16[1,640,128]{2,1,0:T(8,128)(2,1)S(1)}, u32[]{:S(2)}, u32[]{:S(2)}) %collective-permute-start.12) | collective-permute-done | bytes 163872 | tf_op jit(solution)/shard_map/ppermute | solution.py:29
  93.9 9.5 %collective-permute-done.8 = bf16[4,64,768]{2,1,0:T(8,128)(2,1)S(1)} collective-permute-done((bf16[4,64,768]{2,1,0:T(8,128)(2,1)S(1)}, bf16[4,64,768]{2,1,0:T(8,128)(2,1)S(1)}, u32[]{:S(2)}, u32[]{:S(2)}) %collective-permute-start.8) | collective-permute-done | bytes 393248 | tf_op jit(solution)/shard_map/ppermute | solution.py:29
  104.8 13.4 %collective-permute-done.14 = bf16[4,640,128]{2,1,0:T(8,128)(2,1)S(1)} collective-permute-done((bf16[4,640,128]{2,1,0:T(8,128)(2,1)S(1)}, bf16[4,640,128]{2,1,0:T(8,128)(2,1)S(1)}, u32[]{:S(2)}, u32[]{:S(2)}) %collective-permute-start.14) | collective-permute-done | bytes 655392 | tf_op jit(solution)/shard_map/ppermute | solution.py:29
  155.7 10.4 %ssd_forward.1 = (f32[640,768]{1,0:T(8,128)}, f32[5,128,768]{2,1,0:T(8,128)}) custom-call(f32[640,768]{1,0:T(8,128)} %copy-done.11, f32[640,128]{1,0:T(8,128)} %get-tuple-element.155.b_ref, f32[640,128]{1,0:T(8,128)} %get-tuple-element.154.c_ref, f32[640,12]{1,0:T(8,128)} %bitcast.393, f32[5,12,128]{2,1,0:T(8,128)} %copy-done.91, ...), custom_call_target="tpu_custom_call" | custom-call | flops 2264924160 | bytes 9830400 | tf_op jit(solution)/shard_map/ssd_forward/pallas_call | solution.py:504
  177.7 10.0 %collective-permute-done.11 = bf16[144,768]{1,0:T(8,128)(2,1)S(1)} collective-permute-done((bf16[144,768]{1,0:T(8,128)(2,1)S(1)}, bf16[144,768]{1,0:T(8,128)(2,1)S(1)}, u32[]{:S(2)}, u32[]{:S(2)}) %collective-permute-start.11) | collective-permute-done | bytes 221216 | tf_op jit(solution)/shard_map/ppermute | solution.py:29
  198.7 5.7 attention_forward.3
  225.5 14.3 %collective-permute-done.18 = bf16[320,1024]{1,0:T(8,128)(2,1)} collective-permute-done((bf16[320,1024]{1,0:T(8,128)(2,1)S(1)}, bf16[320,1024]{1,0:T(8,128)(2,1)}, u32[]{:S(2)}, u32[]{:S(2)}) %collective-permute-start.18) | collective-permute-done | bytes 655392 | tf_op jit(solution)/shard_map/ppermute | solution.py:29
  242.5 8.9 %fusion.260 = f32[320,4096]{1,0:T(8,128)} fusion(bf16[1024,4096]{1,0:T(8,128)(2,1)} %all-gather.6.cloned.1.call-done, f32[320,1024]{1,0:T(8,128)S(1)} %get-tuple-element.135, f32[1024]{0:T(1024)S(1)} %copy-done.135, f32[320]{0:T(512)S(1)} %fusion.208), kind=kOutput, calls=%fused_computation.590 | convolution fusion | flops 2685337600 | bytes 14947584 | tf_op jit(solution)/shard_map/dot_general | solution.py:191
  251.4 5.8 all-gather.8.cloned.1.call-done
  257.2 6.4 %fusion.147 = (f32[320,2048]{1,0:T(8,128)S(1)}, f32[320,2048]{1,0:T(8,128)S(1)}) fusion(f32[320,4096]{1,0:T(8,128)} %fusion.260, bf16[2048,1024]{1,0:T(8,128)(2,1)} %all-gather.8.cloned.1.call-done, bf16[1,320,1024]{2,1,0:T(8,128)(2,1)} %param.19), kind=kOutput, calls=%fused_computation.325 | convolution fusion | flops 1350041600 | bytes 15335424 | tf_op jit(solution)/shard_map/dot_general | solution.py:181
  265.7 5.9 multiply_reduce_fusion.8
  299.5 8.2 %convolution_convert_fusion.rest_1_.rest_0_ = bf16[512,4096]{1,0:T(8,128)(2,1)} fusion(bf16[320,4096]{1,0:T(8,128)(2,1)} %collective-permute-done.24, bf16[320,4096]{1,0:T(8,128)(2,1)} %add_convert_fusion, bf16[320,512]{1,0:T(8,128)(2,1)S(1)} %collective-permute-done.23, bf16[320,512]{1,0:T(8,128)(2,1)S(1)} %get-tuple-element.187), kind=kOutput, calls=%fused_computation.1 | convolution fusion | flops 2698248192 | bytes 10092544 | tf_op jit(solution)/shard_map/dot_general | solution.py:171
  360.9 20.5 %ssd_backward.1 = (f32[640,768]{1,0:T(8,128)}, f32[640,128]{1,0:T(8,128)}, f32[640,128]{1,0:T(8,128)}) custom-call(f32[640,768]{1,0:T(8,128)} %copy-done.11, f32[640,768]{1,0:T(8,128)} %convert_element_type.826.dy_ref, f32[640,128]{1,0:T(8,128)} %get-tuple-element.155.b_ref, f32[640,128]{1,0:T(8,128)} %get-tuple-element.154.c_ref, f32[640,12]{1,0:T(8,128)} %bitcast.394, ...), custom_call_target="tpu_custom_call" | custom-call | flops 6039797760 | bytes 11796480 | tf_op jit(solution)/shard_map/ssd_backward/pallas_call | solution.py:541
  387.1 6.7 %attention_backward.2 = (f32[640,128]{1,0:T(8,128)}, bf16[5120,128]{1,0:T(8,128)(2,1)}) custom-call(s32[2]{0:T(128)} %pad_add_fusion.4.where_ref, bf16[640,128]{1,0:T(8,128)(2,1)} %get-tuple-element.207.q_ref, bf16[640,128]{1,0:T(8,128)(2,1)} %get-tuple-element.165.do_ref, bf16[5120,128]{1,0:T(8,128)(2,1)} %copy-done.79, ...), custom_call_target="tpu_custom_call" | custom-call | flops 33554432000 | bytes 2621440 | tf_op jit(solution)/shard_map/attention_backward/pallas_call | solution.py:366
  397.2 6.4 %collective-permute-start.45 = (bf16[2,64,1024]{2,1,0:T(8,128)(2,1)S(1)}, bf16[2,64,1024]{2,1,0:T(8,128)(2,1)S(1)}, u32[]{:S(2)}, u32[]{:S(2)}) collective-permute-start(bf16[2,64,1024]{2,1,0:T(8,128)(2,1)S(1)} %select_bitcast_fusion.15), channel_id=1, source_target_pairs={{0,4},{2,6},{4,0},{6,2},{8,12},{10,14},{12,8},{14,10},{1,5},{3,7},... | collective-permute-start | bytes 786440 | tf_op jit(solution)/shard_map/ppermute | solution.py:29
  404.3 19.1 %collective-permute-start.32 = (bf16[144,768]{1,0:T(8,128)(2,1)S(1)}, bf16[144,768]{1,0:T(8,128)(2,1)S(1)}, u32[]{:S(2)}, u32[]{:S(2)}) collective-permute-start(bf16[144,768]{1,0:T(8,128)(2,1)S(1)} %maximum_add_fusion.9.rest_0_), channel_id=1, source_target_pairs={{0,8},{2,10},{4,12},{6,14},{8,0},{10,2},{12,4},{14,6},{1,9},{3,11}... | collective-permute-start | bytes 663560 | tf_op jit(solution)/shard_map/ppermute | solution.py:29
  423.4 6.5 %attention_backward.3 = (f32[640,128]{1,0:T(8,128)}, bf16[5120,128]{1,0:T(8,128)(2,1)}) custom-call(s32[2]{0:T(128)} %pad_add_fusion.4.where_ref, bf16[640,128]{1,0:T(8,128)(2,1)} %get-tuple-element.206.q_ref, bf16[640,128]{1,0:T(8,128)(2,1)} %get-tuple-element.166.do_ref, bf16[5120,128]{1,0:T(8,128)(2,1)} %copy-done.79, ...), custom_call_target="tpu_custom_call" | custom-call | flops 33554432000 | bytes 2621440 | tf_op jit(solution)/shard_map/attention_backward/pallas_call | solution.py:366
  432.2 8.1 %collective-permute-start.28 = (bf16[2,2,640,128]{3,2,0,1:T(8,128)(2,1)S(1)}, bf16[2,2,640,128]{3,2,0,1:T(8,128)(2,1)S(1)}, u32[]{:S(2)}, u32[]{:S(2)}) collective-permute-start(bf16[2,2,640,128]{3,2,0,1:T(8,128)(2,1)S(1)} %select_bitcast_fusion.1), channel_id=1, source_target_pairs={{0,2},{2,0},{4,6},{6,4},{8,10},{10,8},{12,14},{14,12},{1,3},{3,1},... | collective-permute-start | bytes 1966088 | tf_op jit(solution)/shard_map/ppermute | solution.py:29
  441.3 11.6 %collective-permute-start.46 = (bf16[64,1024]{1,0:T(8,128)(2,1)}, bf16[64,1024]{1,0:T(8,128)(2,1)}, u32[]{:S(2)}, u32[]{:S(2)}) collective-permute-start(bf16[64,1024]{1,0:T(8,128)(2,1)} %select_bitcast_fusion.25), channel_id=1, source_target_pairs={{0,8},{2,10},{4,12},{6,14},{8,0},{10,2},{12,4},{14,6},{1,9},{3,11}... | collective-permute-start | bytes 393224 | tf_op jit(solution)/shard_map/ppermute | solution.py:29
  473.9 7.7 %collective-permute-start.29 = (bf16[2,640,128]{2,1,0:T(8,128)(2,1)S(1)}, bf16[2,640,128]{2,1,0:T(8,128)(2,1)S(1)}, u32[]{:S(2)}, u32[]{:S(2)}) collective-permute-start(bf16[2,640,128]{2,1,0:T(8,128)(2,1)S(1)} %select_bitcast_fusion.11), channel_id=1, source_target_pairs={{0,4},{2,6},{4,0},{6,2},{8,12},{10,14},{12,8},{14,10},{1,5},{3,7},... | collective-permute-start | bytes 983048 | tf_op jit(solution)/shard_map/ppermute | solution.py:29
  482.0 7.6 %collective-permute-done.29 = bf16[2,640,128]{2,1,0:T(8,128)(2,1)S(1)} collective-permute-done((bf16[2,640,128]{2,1,0:T(8,128)(2,1)S(1)}, bf16[2,640,128]{2,1,0:T(8,128)(2,1)S(1)}, u32[]{:S(2)}, u32[]{:S(2)}) %collective-permute-start.29) | collective-permute-done | bytes 327712 | tf_op jit(solution)/shard_map/ppermute | solution.py:29
  503.7 6.9 %collective-permute-start.30 = (bf16[640,128]{1,0:T(8,128)(2,1)S(1)}, bf16[640,128]{1,0:T(8,128)(2,1)S(1)}, u32[]{:S(2)}, u32[]{:S(2)}) collective-permute-start(bf16[640,128]{1,0:T(8,128)(2,1)S(1)} %select_bitcast_fusion.20), channel_id=1, source_target_pairs={{0,8},{2,10},{4,12},{6,14},{8,0},{10,2},{12,4},{14,6},{1,9},{3,11}... | collective-permute-start | bytes 491528 | tf_op jit(solution)/shard_map/ppermute | solution.py:29
  553.0 7.7 %collective-permute-done.37 = bf16[2,2,64,1152]{3,2,0,1:T(8,128)(2,1)S(1)} collective-permute-done((bf16[2,2,64,1152]{3,2,0,1:T(8,128)(2,1)S(1)}, bf16[2,2,64,1152]{3,2,0,1:T(8,128)(2,1)S(1)}, u32[]{:S(2)}, u32[]{:S(2)}) %collective-permute-start.37) | collective-permute-done | bytes 589856 | tf_op jit(solution)/shard_map/ppermute | solution.py:29
  (822 shorter events, 347.9 us)
Async XLA Ops:
  7.2 161.9 %all-gather.4.cloned.1.call-start = ((), (), s32[]{:S(2)}) async-start(), calls=%async_computation.2 | async-start | bytes 3899392 | tf_op jit(solution)/shard_map/all_gather | solution.py:669
  58.9 183.5 %all-gather.6.cloned.1.call-start = ((), (), s32[]{:S(2)}) async-start(), calls=%async_computation.3 | async-start | bytes 8912896 | tf_op jit(solution)/shard_map/all_gather | solution.py:747
  83.9 19.4 %collective-permute-start.8 = (bf16[4,64,768]{2,1,0:T(8,128)(2,1)S(1)}, bf16[4,64,768]{2,1,0:T(8,128)(2,1)S(1)}, u32[]{:S(2)}, u32[]{:S(2)}) collective-permute-start(bf16[4,64,768]{2,1,0:T(8,128)(2,1)S(1)} %bitcast.392), channel_id=1, source_target_pairs={{0,2},{2,0},{4,6},{6,4},{8,10},{10,8},{12,14},{14,12},{1,3},{3,1},... | collective-permute-start | bytes 1179656 | tf_op jit(solution)/shard_map/ppermute | solution.py:29
  91.5 26.7 %collective-permute-start.14 = (bf16[4,640,128]{2,1,0:T(8,128)(2,1)S(1)}, bf16[4,640,128]{2,1,0:T(8,128)(2,1)S(1)}, u32[]{:S(2)}, u32[]{:S(2)}) collective-permute-start(bf16[4,640,128]{2,1,0:T(8,128)(2,1)S(1)} %bitcast.387), channel_id=1, source_target_pairs={{0,2},{2,0},{4,6},{6,4},{8,10},{10,8},{12,14},{14,12},{1,3},{3,1},... | collective-permute-start | bytes 1966088 | tf_op jit(solution)/shard_map/ppermute | solution.py:29
  126.3 130.9 %all-gather.8.cloned.1.call-start = ((), (), s32[]{:S(2)}) async-start(), calls=%async_computation.4 | async-start | bytes 4456448 | tf_op jit(solution)/shard_map/all_gather | solution.py:764
  168.6 19.1 %collective-permute-start.11 = (bf16[144,768]{1,0:T(8,128)(2,1)S(1)}, bf16[144,768]{1,0:T(8,128)(2,1)S(1)}, u32[]{:S(2)}, u32[]{:S(2)}) collective-permute-start(bf16[144,768]{1,0:T(8,128)(2,1)S(1)} %maximum_add_fusion.6.rest_1_), channel_id=1, source_target_pairs={{0,4},{2,6},{4,0},{6,2},{8,12},{10,14},{12,8},{14,10},{1,5},{3,7},... | collective-permute-start | bytes 663560 | tf_op jit(solution)/shard_map/ppermute | solution.py:29
  177.3 313.6 %reduce-scatter.3.cloned.1.call-start = ((), (), s32[]{:S(2)}) async-start(), calls=%async_computation.5 | async-start | bytes 4456448 | tf_op jit(solution)/shard_map/reduce_scatter | solution.py:818
  225.5 59.6 %collective-permute-start.21 = (bf16[320,1024]{1,0:T(8,128)(2,1)}, bf16[320,1024]{1,0:T(8,128)(2,1)}, u32[]{:S(2)}, u32[]{:S(2)}) collective-permute-start(bf16[320,1024]{1,0:T(8,128)(2,1)} %bitcast.73), channel_id=1, source_target_pairs={{0,16},{16,0},{1,17},{17,1},{2,18},{18,2},{3,19},{19,3},{4,20},{20... | collective-permute-start | bytes 1966088 | tf_op jit(solution)/shard_map/ppermute | solution.py:29
  265.5 34.1 %collective-permute-start.24 = (bf16[320,4096]{1,0:T(8,128)(2,1)}, bf16[320,4096]{1,0:T(8,128)(2,1)}, u32[]{:S(2)}, u32[]{:S(2)}) collective-permute-start(bf16[320,4096]{1,0:T(8,128)(2,1)} %add_convert_fusion), channel_id=1, source_target_pairs={{0,16},{16,0},{1,17},{17,1},{2,18},{18,2},{3,19},{19,3},{4,20},{20... | collective-permute-start | bytes 7864328 | tf_op jit(solution)/shard_map/ppermute | solution.py:29
  278.3 17.1 %collective-permute-start.19 = (bf16[320,1024]{1,0:T(8,128)(2,1)}, bf16[320,1024]{1,0:T(8,128)(2,1)S(1)}, u32[]{:S(2)}, u32[]{:S(2)}) collective-permute-start(bf16[320,1024]{1,0:T(8,128)(2,1)} %copy-done.63), channel_id=1, source_target_pairs={{0,1},{1,0},{2,3},{3,2},{4,5},{5,4},{6,7},{7,6},{8,9},{9,8},{10,11... | collective-permute-start | bytes 1966088 | tf_op jit(solution)/shard_map/ppermute | solution.py:29
  307.8 225.8 %reduce-scatter.5.cloned.1.call-start = ((), (), s32[]{:S(2)}) async-start(), calls=%async_computation.6 | async-start | bytes 2228224 | tf_op jit(solution)/shard_map/reduce_scatter | solution.py:818
  310.8 199.9 %collective-permute-start.31 = (bf16[640,512]{1,0:T(8,128)(2,1)}, bf16[640,512]{1,0:T(8,128)(2,1)}, u32[]{:S(2)}, u32[]{:S(2)}) collective-permute-start(bf16[640,512]{1,0:T(8,128)(2,1)} %get-tuple-element.162), channel_id=1, source_target_pairs={{0,16},{16,0},{1,17},{17,1},{2,18},{18,2},{3,19},{19,3},{4,20},{20... | collective-permute-start | bytes 1966088 | tf_op jit(solution)/shard_map/ppermute | solution.py:29
  333.8 23.6 %collective-permute-start.25 = (bf16[8,64,1024]{2,1,0:T(8,128)(2,1)}, bf16[8,64,1024]{2,1,0:T(8,128)(2,1)}, u32[]{:S(2)}, u32[]{:S(2)}) collective-permute-start(bf16[8,64,1024]{2,1,0:T(8,128)(2,1)} %select_bitcast_fusion), channel_id=1, source_target_pairs={{0,16},{16,0},{1,17},{17,1},{2,18},{18,2},{3,19},{19,3},{4,20},{20... | collective-permute-start | bytes 3145736 | tf_op jit(solution)/shard_map/ppermute | solution.py:29
  359.3 36.5 %collective-permute-start.44 = (bf16[2,2,64,1024]{3,2,0,1:T(8,128)(2,1)S(1)}, bf16[2,2,64,1024]{3,2,0,1:T(8,128)(2,1)}, u32[]{:S(2)}, u32[]{:S(2)}) collective-permute-start(bf16[2,2,64,1024]{3,2,0,1:T(8,128)(2,1)S(1)} %select_bitcast_fusion.6), channel_id=1, source_target_pairs={{0,2},{2,0},{4,6},{6,4},{8,10},{10,8},{12,14},{14,12},{1,3},{3,1},... | collective-permute-start | bytes 1572872 | tf_op jit(solution)/shard_map/ppermute | solution.py:29
  383.4 20.2 %collective-permute-start.27 = (bf16[144,768]{1,0:T(8,128)(2,1)S(1)}, bf16[144,768]{1,0:T(8,128)(2,1)S(1)}, u32[]{:S(2)}, u32[]{:S(2)}) collective-permute-start(bf16[144,768]{1,0:T(8,128)(2,1)S(1)} %maximum_add_fusion.8.rest_3_), channel_id=1, source_target_pairs={{0,4},{2,6},{4,0},{6,2},{8,12},{10,14},{12,8},{14,10},{1,5},{3,7},... | collective-permute-start | bytes 663560 | tf_op jit(solution)/shard_map/ppermute | solution.py:29
  397.2 43.3 %collective-permute-start.45 = (bf16[2,64,1024]{2,1,0:T(8,128)(2,1)S(1)}, bf16[2,64,1024]{2,1,0:T(8,128)(2,1)S(1)}, u32[]{:S(2)}, u32[]{:S(2)}) collective-permute-start(bf16[2,64,1024]{2,1,0:T(8,128)(2,1)S(1)} %select_bitcast_fusion.15), channel_id=1, source_target_pairs={{0,4},{2,6},{4,0},{6,2},{8,12},{10,14},{12,8},{14,10},{1,5},{3,7},... | collective-permute-start | bytes 786440 | tf_op jit(solution)/shard_map/ppermute | solution.py:29
  404.3 48.6 %collective-permute-start.32 = (bf16[144,768]{1,0:T(8,128)(2,1)S(1)}, bf16[144,768]{1,0:T(8,128)(2,1)S(1)}, u32[]{:S(2)}, u32[]{:S(2)}) collective-permute-start(bf16[144,768]{1,0:T(8,128)(2,1)S(1)} %maximum_add_fusion.9.rest_0_), channel_id=1, source_target_pairs={{0,8},{2,10},{4,12},{6,14},{8,0},{10,2},{12,4},{14,6},{1,9},{3,11}... | collective-permute-start | bytes 663560 | tf_op jit(solution)/shard_map/ppermute | solution.py:29
  432.2 33.0 %collective-permute-start.28 = (bf16[2,2,640,128]{3,2,0,1:T(8,128)(2,1)S(1)}, bf16[2,2,640,128]{3,2,0,1:T(8,128)(2,1)S(1)}, u32[]{:S(2)}, u32[]{:S(2)}) collective-permute-start(bf16[2,2,640,128]{3,2,0,1:T(8,128)(2,1)S(1)} %select_bitcast_fusion.1), channel_id=1, source_target_pairs={{0,2},{2,0},{4,6},{6,4},{8,10},{10,8},{12,14},{14,12},{1,3},{3,1},... | collective-permute-start | bytes 1966088 | tf_op jit(solution)/shard_map/ppermute | solution.py:29
  441.3 55.2 %collective-permute-start.46 = (bf16[64,1024]{1,0:T(8,128)(2,1)}, bf16[64,1024]{1,0:T(8,128)(2,1)}, u32[]{:S(2)}, u32[]{:S(2)}) collective-permute-start(bf16[64,1024]{1,0:T(8,128)(2,1)} %select_bitcast_fusion.25), channel_id=1, source_target_pairs={{0,8},{2,10},{4,12},{6,14},{8,0},{10,2},{12,4},{14,6},{1,9},{3,11}... | collective-permute-start | bytes 393224 | tf_op jit(solution)/shard_map/ppermute | solution.py:29
  521.0 18.1 %collective-permute-start.35 = (bf16[640,1152]{1,0:T(8,128)(2,1)}, bf16[640,1152]{1,0:T(8,128)(2,1)}, u32[]{:S(2)}, u32[]{:S(2)}) collective-permute-start(bf16[640,1152]{1,0:T(8,128)(2,1)} %pad_maximum_fusion.3), channel_id=1, source_target_pairs={{0,16},{16,0},{1,17},{17,1},{2,18},{18,2},{3,19},{19,3},{4,20},{20... | collective-permute-start | bytes 4423688 | tf_op jit(solution)/shard_map/ppermute | solution.py:29
  543.5 17.2 %collective-permute-start.37 = (bf16[2,2,64,1152]{3,2,0,1:T(8,128)(2,1)S(1)}, bf16[2,2,64,1152]{3,2,0,1:T(8,128)(2,1)S(1)}, u32[]{:S(2)}, u32[]{:S(2)}) collective-permute-start(bf16[2,2,64,1152]{3,2,0,1:T(8,128)(2,1)S(1)} %select_bitcast_fusion.4), channel_id=1, source_target_pairs={{0,4},{2,6},{4,0},{6,2},{8,12},{10,14},{12,8},{14,10},{1,5},{3,7},... | collective-permute-start | bytes 1769480 | tf_op jit(solution)/shard_map/ppermute | solution.py:29
  549.9 17.8 %collective-permute-start.36 = (bf16[320,1024]{1,0:T(8,128)(2,1)S(1)}, bf16[320,1024]{1,0:T(8,128)(2,1)S(1)}, u32[]{:S(2)}, u32[]{:S(2)}) collective-permute-start(bf16[320,1024]{1,0:T(8,128)(2,1)S(1)} %select_convert_fusion), channel_id=1, source_target_pairs={{0,1},{1,0},{2,3},{3,2},{4,5},{5,4},{6,7},{7,6},{8,9},{9,8},{10,11... | collective-permute-start | bytes 1966088 | tf_op jit(solution)/shard_map/ppermute | solution.py:29
  552.6 17.4 %collective-permute-start.42 = (bf16[64,1152]{1,0:T(8,128)(2,1)S(1)}, bf16[64,1152]{1,0:T(8,128)(2,1)S(1)}, u32[]{:S(2)}, u32[]{:S(2)}) collective-permute-start(bf16[64,1152]{1,0:T(8,128)(2,1)S(1)} %select_bitcast_fusion.23), channel_id=1, source_target_pairs={{0,8},{2,10},{4,12},{6,14},{8,0},{10,2},{12,4},{14,6},{1,9},{3,11}... | collective-permute-start | bytes 442376 | tf_op jit(solution)/shard_map/ppermute | solution.py:29
  572.3 17.0 %collective-permute-start.38 = (bf16[2,64,1152]{2,1,0:T(8,128)(2,1)S(1)}, bf16[2,64,1152]{2,1,0:T(8,128)(2,1)S(1)}, u32[]{:S(2)}, u32[]{:S(2)}) collective-permute-start(bf16[2,64,1152]{2,1,0:T(8,128)(2,1)S(1)} %fusion.139), channel_id=1, source_target_pairs={{0,8},{2,10},{4,12},{6,14},{8,0},{10,2},{12,4},{14,6},{1,9},{3,11}... | collective-permute-start | bytes 884744 | tf_op jit(solution)/shard_map/ppermute | solution.py:29
  (222 other events, 2162.4 us)
Sparse Core Ops, SparseCore 0:
  59.0 63.1 all-gather.3
  126.5 77.4 all-gather.5
  206.7 50.4 all-gather.7
  307.9 104.1 reduce-scatter.2
  414.2 81.5 reduce-scatter.4

commit v5 on v4

--- a/solution.py
+++ b/solution.py
@@ -18,6 +18,7 @@
 rope_base = 100000000000.0
 masked = -1e30
 highest = lax.Precision.HIGHEST
+fine = lax.Precision.HIGH
 low_type = jnp.bfloat16
 f32 = jnp.float32
 chunk_len = 128
@@ -415,7 +416,7 @@
 
     rows = xd_ref.shape[0]
     b, c = b_ref[...], c_ref[...]
-    inner = dot_t(c, b, highest)
+    inner = dot_t(c, b, fine)
     lower = lax.broadcasted_iota(jnp.int32, (rows, rows), 0) >= lax.broadcasted_iota(
         jnp.int32, (rows, rows), 1
     )
@@ -423,7 +424,7 @@
     before_ref[...] = state
     csx = csx_ref[...]
     last = csx[rows - 1 :, :]
-    carried = jnp.exp(csx) * dot(c, state, highest)
+    carried = jnp.exp(csx) * dot(c, state, fine)
 
     def mixing(h):
         spread = jnp.where(lower, cs_ref[:, h : h + 1] - cst_ref[h : h + 1, :], masked)
@@ -433,8 +434,8 @@
         cols = slice(pair * 2 * HDIM, (pair + 1) * 2 * HDIM)
         mix = jnp.concatenate([mixing(2 * pair), mixing(2 * pair + 1)], axis=1)
         blocks = jnp.concatenate(pair_blocks(xd_ref[:, cols]), axis=0)
-        y_ref[:, cols] = carried[:, cols] + dot(mix, blocks, highest)
-    s_s[...] = jnp.exp(last) * state + t_dot(b, jnp.exp(last - csx) * xd_ref[...], highest)
+        y_ref[:, cols] = carried[:, cols] + dot(mix, blocks, fine)
+    s_s[...] = jnp.exp(last) * state + t_dot(b, jnp.exp(last - csx) * xd_ref[...], fine)
 
 
 def ssd_bwd_kernel(
@@ -456,14 +457,14 @@
 
     rows = xd_ref.shape[0]
     b, c = b_ref[...], c_ref[...]
-    inner_t = dot_t(b, c, highest)
+    inner_t = dot_t(b, c, fine)
     row_id = lax.broadcasted_iota(jnp.int32, (rows, rows), 0)
     col_id = lax.broadcasted_iota(jnp.int32, (rows, rows), 1)
     csx = csx_ref[...]
     last = csx[rows - 1 :, :]
     grad_state = ds_s[...]
     end_fall = jnp.exp(last - csx)
-    from_state = end_fall * dot(b, grad_state, highest)
+    from_state = end_fall * dot(b, grad_state, fine)
     scaled_dy = jnp.exp(csx) * dy_ref[...]
     grad_inner = jnp.zeros((rows, rows), f32)
 
@@ -482,15 +483,15 @@
             [falls_t(2 * pair) * inner_t, falls_t(2 * pair + 1) * inner_t], axis=1
         )
         blocks = jnp.concatenate([dy_left, dy_right], axis=0)
-        dxd_ref[:, cols] = from_state[:, cols] + dot(mix_t, blocks, highest)
+        dxd_ref[:, cols] = from_state[:, cols] + dot(mix_t, blocks, fine)
         xd = xd_ref[:, cols]
-        grad_inner = grad_inner + falls(2 * pair) * dot_t(dy_left, xd, highest)
-        grad_inner = grad_inner + falls(2 * pair + 1) * dot_t(dy_right, xd, highest)
-    dc_ref[...] = dot(grad_inner, b, highest) + dot_t(scaled_dy, before_ref[...], highest)
-    db_ref[...] = t_dot(grad_inner, c, highest) + dot_t(
-        end_fall * xd_ref[...], grad_state, highest
-    )
-    ds_s[...] = jnp.exp(last) * grad_state + t_dot(c, scaled_dy, highest)
+        grad_inner = grad_inner + falls(2 * pair) * dot_t(dy_left, xd, fine)
+        grad_inner = grad_inner + falls(2 * pair + 1) * dot_t(dy_right, xd, fine)
+    dc_ref[...] = dot(grad_inner, b, fine) + dot_t(scaled_dy, before_ref[...], fine)
+    db_ref[...] = t_dot(grad_inner, c, fine) + dot_t(
+        end_fall * xd_ref[...], grad_state, fine
+    )
+    ds_s[...] = jnp.exp(last) * grad_state + t_dot(c, scaled_dy, fine)
 
 
 def ssd_forward(xd, b, c, cs, cst, csx, deps):
@@ -668,8 +669,16 @@
     )
     z_out = lax.all_gather(after(z_out, misc_steps[1]), ("dp", "cp"), axis=0, tiled=True)
     w_z = z_out[:, :x_part]
-    out_sides = z_out[:, x_part:].reshape(2, -1, half_cols)
-    w_out = in_order(out_sides[0], out_sides[1], hd_high, 1, jnp.concatenate)
+    mo_rows, ao_rows = w_mo.shape[0], w_ao.shape[0]
+    out_sides = z_out[:, x_part:].reshape(2, n_cp, mo_rows + ao_rows, half_cols)
+    out_left = lax.dynamic_index_in_dim(out_sides, hd_index, 0, False)
+    out_right = lax.dynamic_index_in_dim(out_sides, 1 - hd_index, 0, False)
+
+    def out_part(begin, rows):
+        sides = [a[:, begin : begin + rows].reshape(-1, half_cols) for a in (out_left, out_right)]
+        return jnp.concatenate(sides, axis=1)
+
+    w_out = jnp.concatenate([out_part(0, mo_rows), out_part(mo_rows, ao_rows)], axis=0)
     w_xs = gather_pair(xs_cp, "dp", 0)
 
     proj = dot(normed1_all, w_misc)
@@ -735,7 +744,7 @@
     dtx = wide(dt_value)
     xd = dtx * x_conv
     ending_xd = jnp.exp(csx_dev[-1:] - csx_dev) * xd
-    state_local = t_dot(b_conv, ending_xd, highest)
+    state_local = t_dot(b_conv, ending_xd, fine)
     scan = state_scan(log_dev, state_local, True)
     in_sent = next(scan)
     y_own, before = ssd_forward(xd, b_conv, c_conv, cs, cst, csx, (in_sent,))
@@ -764,18 +773,8 @@
     w_back = lax.all_gather(after(w_down, att_outs[0]), ("dp", "cp"), axis=0, tiled=True)
 
 
-    mo_rows, ao_rows = w_mo.shape[0], w_ao.shape[0]
-    w_out = w_out.reshape(n_cp, mo_rows + ao_rows, d_model)
-    w_out = jnp.concatenate(
-        [
-            w_out[:, :mo_rows].reshape(n_cp * mo_rows, d_model),
-            w_out[:, mo_rows:].reshape(n_cp * ao_rows, d_model),
-        ],
-        axis=0,
-    )
-
     state_in = after(state_in, w_out)
-    y_core = y_own + jnp.exp(csx_dev) * dot(c_conv, state_in, highest)
+    y_core = y_own + jnp.exp(csx_dev) * dot(c_conv, state_in, fine)
     y_low = (y_core + skip_x * x_conv).astype(low_type).astype(f32)
 
     gate_z = dot(normed1_all, w_z)
@@ -858,7 +857,7 @@
     grad_z = (grad_mixed * y_low * sig_z * (1.0 + gate_z * (1.0 - sig_z))).astype(low_type)
 
     scaled_dy = jnp.exp(csx_dev) * grad_y
-    scan = state_scan(log_dev, t_dot(c_conv, scaled_dy, highest), False)
+    scan = state_scan(log_dev, t_dot(c_conv, scaled_dy, fine), False)
     future = next(scan)
 
     normed1_half = halves_by_core(normed1_all)
@@ -910,9 +909,9 @@
     s_mo, s_ao = s_out[: mo_rows // n_hd], s_out[mo_rows // n_hd :]
 
 
-    dxd = dxd_own + jnp.exp(csx_dev[-1:] - csx_dev) * dot(b_conv, future, highest)
-    db = db_own + dot_t(ending_xd, future, highest)
-    dc = dc_own + dot_t(scaled_dy, state_in, highest)
+    dxd = dxd_own + jnp.exp(csx_dev[-1:] - csx_dev) * dot(b_conv, future, fine)
+    db = db_own + dot_t(ending_xd, future, fine)
+    dc = dc_own + dot_t(scaled_dy, state_in, fine)
 
     ddt_direct = per_head(x_conv * dxd)
     dcs = per_head(grad_y * y_core) - dt_value * ddt_direct

time: 620 us -> 624 us (level)
  waiting for transfers between devices: 144 us -> 153 us
    ppermute x50, waiting for transfers between devices: 138 us -> 153 us  [swap(): return lax.ppermute(value, axis, [(i, i ^ bit) for i in range(count)])]
    pallas_call x2, Pallas kernels: 11.2 us -> 22.8 us  [attention_forward(): pl.pallas_call(att_fwd_kernel, in_specs=[pl.BlockSpec(memory_space=pltpu....]
    pallas_call x1, Pallas kernels: 20.5 us -> 12.1 us  [ssd_backward(): pl.pallas_call(ssd_bwd_kernel, grid=(blocks,), in_specs=[rows(width), row...]
    unnamed x381 -> x388, local copies, waits for them, and re-layouts: 14.6 us -> 13.5 us
  transfers between devices with their start and end apart: 58 -> 58, of which waited for: 32 -> 32; matrix products, arithmetic and copies ran while one was open for 35% -> 34% of each run, Pallas kernels for 9% -> 9%
where the time goes in v5:
time: 624 us; the launch traced here: 613 us
  waiting for transfers between devices  153 us (25%)
  starting transfers between devices  123 us (20%)
  matrix products  95.9 us (15%)
  other arithmetic  79.1 us (13%)
  local copies, waits for them, and re-layouts  70.4 us (11%)
  Pallas kernels  55.6 us (9%)
  between operations  35.6 us (6%)
    ppermute x50, waiting for transfers between devices, swap(): return lax.ppermute(value, axis, [(i, i ^ bit) for i in range(count)])  153 us
    ppermute x50, starting transfers between devices, swap(): return lax.ppermute(value, axis, [(i, i ^ bit) for i in range(count)])  116 us
    dot_general x31, matrix products, dot(): return jnp.dot(left, right, preferred_element_type=f32, precision=precision)  41.9 us
    dot_general x13, matrix products, dot_t(): lax.dot_general(left, right, (((1,), (1,)), ((), ())), preferred_element_...  27 us
    dot_general x7, matrix products, t_dot(): lax.dot_general(left, right, (((0,), (0,)), ((), ())), preferred_element_...  26.3 us
    pallas_call x2, Pallas kernels, attention_forward(): pl.pallas_call(att_fwd_kernel, in_specs=[pl.BlockSpec(memory_space=pltpu....  22.8 us
    slice x26, local copies, waits for them, and re-layouts, after(): lax.slice(earlier, (0,) * earlier.ndim, (1,) * earlier.ndim).reshape(())  18.4 us
    unnamed x388, local copies, waits for them, and re-layouts  13.5 us
  transfers between devices with their start and end apart: 58, of which 32 were waited for; matrix products, arithmetic and copies ran while one was open for 34% of the time, Pallas kernels for 9%

profile of v5, /device:TPU:0, one launch (start us, length us, event | category | flops | bytes accessed | tf_op | source)
XLA Modules:
  0.0 613.0 jit_solution(9790658850717509697)
XLA Ops:
  38.9 6.4 %collective-permute-done.3 = bf16[4,64,768]{2,1,0:T(8,128)(2,1)S(1)} collective-permute-done((bf16[4,64,768]{2,1,0:T(8,128)(2,1)S(1)}, bf16[4,64,768]{2,1,0:T(8,128)(2,1)S(1)}, u32[]{:S(2)}, u32[]{:S(2)}) %collective-permute-start.3) | collective-permute-done | bytes 393248 | tf_op jit(solution)/shard_map/ppermute | solution.py:30
  69.9 11.2 %collective-permute-done.12 = bf16[1,640,128]{2,1,0:T(8,128)(2,1)S(1)} collective-permute-done((bf16[1,640,128]{2,1,0:T(8,128)(2,1)S(1)}, bf16[1,640,128]{2,1,0:T(8,128)(2,1)S(1)}, u32[]{:S(2)}, u32[]{:S(2)}) %collective-permute-start.12) | collective-permute-done | bytes 163872 | tf_op jit(solution)/shard_map/ppermute | solution.py:30
  93.9 9.0 %collective-permute-done.8 = bf16[4,64,768]{2,1,0:T(8,128)(2,1)S(1)} collective-permute-done((bf16[4,64,768]{2,1,0:T(8,128)(2,1)S(1)}, bf16[4,64,768]{2,1,0:T(8,128)(2,1)S(1)}, u32[]{:S(2)}, u32[]{:S(2)}) %collective-permute-start.8) | collective-permute-done | bytes 393248 | tf_op jit(solution)/shard_map/ppermute | solution.py:30
  104.4 13.8 %collective-permute-done.14 = bf16[4,640,128]{2,1,0:T(8,128)(2,1)S(1)} collective-permute-done((bf16[4,640,128]{2,1,0:T(8,128)(2,1)S(1)}, bf16[4,640,128]{2,1,0:T(8,128)(2,1)S(1)}, u32[]{:S(2)}, u32[]{:S(2)}) %collective-permute-start.14) | collective-permute-done | bytes 655392 | tf_op jit(solution)/shard_map/ppermute | solution.py:30
  154.5 7.9 %ssd_forward.1 = (f32[640,768]{1,0:T(8,128)}, f32[5,128,768]{2,1,0:T(8,128)}) custom-call(f32[640,768]{1,0:T(8,128)} %copy-done.11, f32[640,128]{1,0:T(8,128)} %get-tuple-element.153.b_ref, f32[640,128]{1,0:T(8,128)} %get-tuple-element.152.c_ref, f32[640,12]{1,0:T(8,128)} %bitcast.396, f32[5,12,128]{2,1,0:T(8,128)} %copy-done.93, ...), custom_call_target="tpu_custom_call" | custom-call | flops 2264924160 | bytes 9830400 | tf_op jit(solution)/shard_map/ssd_forward/pallas_call | solution.py:505
  165.5 17.3 %attention_forward.2 = (f32[640,128]{1,0:T(8,128)}, f32[2,640,1]{2,1,0:T(8,128)}) custom-call(s32[2]{0:T(128)} %pad_add_fusion.4.where_ref, bf16[640,128]{1,0:T(8,128)(2,1)} %get-tuple-element.207.q_ref, bf16[5120,128]{1,0:T(8,128)(2,1)} %copy-done.77, bf16[5120,128]{1,0:T(8,128)(2,1)} %pad_maximum_fusion.6.vv_ref, s32[640,1]{1,0:T(8,128)} %reshape.741.start_ref, ...), custom_call_target="tpu_custom_call" | custom-call | flops 13421772800 | bytes 2621440 | tf_op jit(solution)/shard_map/attention_forward/pallas_call | solution.py:338
  191.0 12.2 %collective-permute-done.11 = bf16[144,768]{1,0:T(8,128)(2,1)S(1)} collective-permute-done((bf16[144,768]{1,0:T(8,128)(2,1)S(1)}, bf16[144,768]{1,0:T(8,128)(2,1)S(1)}, u32[]{:S(2)}, u32[]{:S(2)}) %collective-permute-start.11) | collective-permute-done | bytes 221216 | tf_op jit(solution)/shard_map/ppermute | solution.py:30
  222.7 9.5 %collective-permute-done.16 = bf16[144,768]{1,0:T(8,128)(2,1)S(1)} collective-permute-done((bf16[144,768]{1,0:T(8,128)(2,1)S(1)}, bf16[144,768]{1,0:T(8,128)(2,1)S(1)}, u32[]{:S(2)}, u32[]{:S(2)}) %collective-permute-start.16) | collective-permute-done | bytes 221216 | tf_op jit(solution)/shard_map/ppermute | solution.py:30
  245.2 12.8 %collective-permute-done.18 = bf16[320,1024]{1,0:T(8,128)(2,1)} collective-permute-done((bf16[320,1024]{1,0:T(8,128)(2,1)S(1)}, bf16[320,1024]{1,0:T(8,128)(2,1)}, u32[]{:S(2)}, u32[]{:S(2)}) %collective-permute-start.18) | collective-permute-done | bytes 655392 | tf_op jit(solution)/shard_map/ppermute | solution.py:30
  260.7 9.0 %fusion.260 = f32[320,4096]{1,0:T(8,128)} fusion(bf16[1024,4096]{1,0:T(8,128)(2,1)} %all-gather.6.cloned.1.call-done, f32[320,1024]{1,0:T(8,128)S(1)} %get-tuple-element.135, f32[1024]{0:T(1024)S(1)} %copy-done.139, f32[320]{0:T(512)S(1)} %fusion.208), kind=kOutput, calls=%fused_computation.588 | convolution fusion | flops 2685337600 | bytes 14947584 | tf_op jit(solution)/shard_map/dot_general | solution.py:192
  269.7 6.4 %fusion.147 = (f32[320,2048]{1,0:T(8,128)S(1)}, f32[320,2048]{1,0:T(8,128)S(1)}) fusion(f32[320,4096]{1,0:T(8,128)} %fusion.260, bf16[2048,1024]{1,0:T(8,128)(2,1)} %all-gather.8.cloned.1.call-done, bf16[1,320,1024]{2,1,0:T(8,128)(2,1)} %param.19), kind=kOutput, calls=%fused_computation.325 | convolution fusion | flops 1350041600 | bytes 15335424 | tf_op jit(solution)/shard_map/dot_general | solution.py:182
  300.8 6.8 %collective-permute-done.19 = bf16[320,1024]{1,0:T(8,128)(2,1)S(1)} collective-permute-done((bf16[320,1024]{1,0:T(8,128)(2,1)}, bf16[320,1024]{1,0:T(8,128)(2,1)S(1)}, u32[]{:S(2)}, u32[]{:S(2)}) %collective-permute-start.19) | collective-permute-done | bytes 655392 | tf_op jit(solution)/shard_map/ppermute | solution.py:30
  311.7 8.2 %convolution_convert_fusion.rest_1_.rest_0_ = bf16[512,4096]{1,0:T(8,128)(2,1)} fusion(bf16[320,4096]{1,0:T(8,128)(2,1)} %collective-permute-done.24, bf16[320,4096]{1,0:T(8,128)(2,1)} %add_convert_fusion, bf16[320,512]{1,0:T(8,128)(2,1)S(1)} %collective-permute-done.23, bf16[320,512]{1,0:T(8,128)(2,1)S(1)} %get-tuple-element.187), kind=kOutput, calls=%fused_computation.1 | convolution fusion | flops 2698248192 | bytes 10092544 | tf_op jit(solution)/shard_map/dot_general | solution.py:172
  372.9 12.1 %ssd_backward.1 = (f32[640,768]{1,0:T(8,128)}, f32[640,128]{1,0:T(8,128)}, f32[640,128]{1,0:T(8,128)}) custom-call(f32[640,768]{1,0:T(8,128)} %copy-done.11, f32[640,768]{1,0:T(8,128)} %convert_element_type.826.dy_ref, f32[640,128]{1,0:T(8,128)} %get-tuple-element.153.b_ref, f32[640,128]{1,0:T(8,128)} %get-tuple-element.152.c_ref, f32[640,12]{1,0:T(8,128)} %bitcast.397, ...), custom_call_target="tpu_custom_call" | custom-call | flops 6039797760 | bytes 11796480 | tf_op jit(solution)/shard_map/ssd_backward/pallas_call | solution.py:542
  391.7 6.5 %attention_backward.2 = (f32[640,128]{1,0:T(8,128)}, bf16[5120,128]{1,0:T(8,128)(2,1)}) custom-call(s32[2]{0:T(128)} %pad_add_fusion.4.where_ref, bf16[640,128]{1,0:T(8,128)(2,1)} %get-tuple-element.207.q_ref, bf16[640,128]{1,0:T(8,128)(2,1)} %get-tuple-element.165.do_ref, bf16[5120,128]{1,0:T(8,128)(2,1)} %copy-done.77, ...), custom_call_target="tpu_custom_call" | custom-call | flops 33554432000 | bytes 2621440 | tf_op jit(solution)/shard_map/attention_backward/pallas_call | solution.py:367
  401.5 6.4 %collective-permute-start.45 = (bf16[2,64,1024]{2,1,0:T(8,128)(2,1)S(1)}, bf16[2,64,1024]{2,1,0:T(8,128)(2,1)S(1)}, u32[]{:S(2)}, u32[]{:S(2)}) collective-permute-start(bf16[2,64,1024]{2,1,0:T(8,128)(2,1)S(1)} %select_bitcast_fusion.15), channel_id=1, source_target_pairs={{0,4},{2,6},{4,0},{6,2},{8,12},{10,14},{12,8},{14,10},{1,5},{3,7},... | collective-permute-start | bytes 786440 | tf_op jit(solution)/shard_map/ppermute | solution.py:30
  408.6 17.6 %collective-permute-start.32 = (bf16[144,768]{1,0:T(8,128)(2,1)S(1)}, bf16[144,768]{1,0:T(8,128)(2,1)S(1)}, u32[]{:S(2)}, u32[]{:S(2)}) collective-permute-start(bf16[144,768]{1,0:T(8,128)(2,1)S(1)} %maximum_add_fusion.9.rest_0_), channel_id=1, source_target_pairs={{0,8},{2,10},{4,12},{6,14},{8,0},{10,2},{12,4},{14,6},{1,9},{3,11}... | collective-permute-start | bytes 663560 | tf_op jit(solution)/shard_map/ppermute | solution.py:30
  426.2 6.3 %attention_backward.3 = (f32[640,128]{1,0:T(8,128)}, bf16[5120,128]{1,0:T(8,128)(2,1)}) custom-call(s32[2]{0:T(128)} %pad_add_fusion.4.where_ref, bf16[640,128]{1,0:T(8,128)(2,1)} %get-tuple-element.206.q_ref, bf16[640,128]{1,0:T(8,128)(2,1)} %get-tuple-element.166.do_ref, bf16[5120,128]{1,0:T(8,128)(2,1)} %copy-done.77, ...), custom_call_target="tpu_custom_call" | custom-call | flops 33554432000 | bytes 2621440 | tf_op jit(solution)/shard_map/attention_backward/pallas_call | solution.py:367
  434.8 8.1 %collective-permute-start.28 = (bf16[2,2,640,128]{3,2,0,1:T(8,128)(2,1)S(1)}, bf16[2,2,640,128]{3,2,0,1:T(8,128)(2,1)S(1)}, u32[]{:S(2)}, u32[]{:S(2)}) collective-permute-start(bf16[2,2,640,128]{3,2,0,1:T(8,128)(2,1)S(1)} %select_bitcast_fusion.1), channel_id=1, source_target_pairs={{0,2},{2,0},{4,6},{6,4},{8,10},{10,8},{12,14},{14,12},{1,3},{3,1},... | collective-permute-start | bytes 1966088 | tf_op jit(solution)/shard_map/ppermute | solution.py:30
  443.9 11.6 %collective-permute-start.46 = (bf16[64,1024]{1,0:T(8,128)(2,1)}, bf16[64,1024]{1,0:T(8,128)(2,1)}, u32[]{:S(2)}, u32[]{:S(2)}) collective-permute-start(bf16[64,1024]{1,0:T(8,128)(2,1)} %select_bitcast_fusion.25), channel_id=1, source_target_pairs={{0,8},{2,10},{4,12},{6,14},{8,0},{10,2},{12,4},{14,6},{1,9},{3,11}... | collective-permute-start | bytes 393224 | tf_op jit(solution)/shard_map/ppermute | solution.py:30
  474.7 7.7 %collective-permute-start.29 = (bf16[2,640,128]{2,1,0:T(8,128)(2,1)S(1)}, bf16[2,640,128]{2,1,0:T(8,128)(2,1)S(1)}, u32[]{:S(2)}, u32[]{:S(2)}) collective-permute-start(bf16[2,640,128]{2,1,0:T(8,128)(2,1)S(1)} %select_bitcast_fusion.11), channel_id=1, source_target_pairs={{0,4},{2,6},{4,0},{6,2},{8,12},{10,14},{12,8},{14,10},{1,5},{3,7},... | collective-permute-start | bytes 983048 | tf_op jit(solution)/shard_map/ppermute | solution.py:30
  482.9 9.3 %collective-permute-done.29 = bf16[2,640,128]{2,1,0:T(8,128)(2,1)S(1)} collective-permute-done((bf16[2,640,128]{2,1,0:T(8,128)(2,1)S(1)}, bf16[2,640,128]{2,1,0:T(8,128)(2,1)S(1)}, u32[]{:S(2)}, u32[]{:S(2)}) %collective-permute-start.29) | collective-permute-done | bytes 327712 | tf_op jit(solution)/shard_map/ppermute | solution.py:30
  506.5 8.8 %collective-permute-start.30 = (bf16[640,128]{1,0:T(8,128)(2,1)S(1)}, bf16[640,128]{1,0:T(8,128)(2,1)S(1)}, u32[]{:S(2)}, u32[]{:S(2)}) collective-permute-start(bf16[640,128]{1,0:T(8,128)(2,1)S(1)} %select_bitcast_fusion.20), channel_id=1, source_target_pairs={{0,8},{2,10},{4,12},{6,14},{8,0},{10,2},{12,4},{14,6},{1,9},{3,11}... | collective-permute-start | bytes 491528 | tf_op jit(solution)/shard_map/ppermute | solution.py:30
  557.2 9.1 %collective-permute-done.37 = bf16[2,2,64,1152]{3,2,0,1:T(8,128)(2,1)S(1)} collective-permute-done((bf16[2,2,64,1152]{3,2,0,1:T(8,128)(2,1)S(1)}, bf16[2,2,64,1152]{3,2,0,1:T(8,128)(2,1)S(1)}, u32[]{:S(2)}, u32[]{:S(2)}) %collective-permute-start.37) | collective-permute-done | bytes 589856 | tf_op jit(solution)/shard_map/ppermute | solution.py:30
  (830 shorter events, 343.4 us)
Async XLA Ops:
  7.2 158.3 %all-gather.4.cloned.1.call-start = ((), (), s32[]{:S(2)}) async-start(), calls=%async_computation.2 | async-start | bytes 3899392 | tf_op jit(solution)/shard_map/all_gather | solution.py:670
  58.9 201.8 %all-gather.6.cloned.1.call-start = ((), (), s32[]{:S(2)}) async-start(), calls=%async_computation.3 | async-start | bytes 8912896 | tf_op jit(solution)/shard_map/all_gather | solution.py:756
  84.1 18.8 %collective-permute-start.8 = (bf16[4,64,768]{2,1,0:T(8,128)(2,1)S(1)}, bf16[4,64,768]{2,1,0:T(8,128)(2,1)S(1)}, u32[]{:S(2)}, u32[]{:S(2)}) collective-permute-start(bf16[4,64,768]{2,1,0:T(8,128)(2,1)S(1)} %bitcast.395), channel_id=1, source_target_pairs={{0,2},{2,0},{4,6},{6,4},{8,10},{10,8},{12,14},{14,12},{1,3},{3,1},... | collective-permute-start | bytes 1179656 | tf_op jit(solution)/shard_map/ppermute | solution.py:30
  91.6 26.6 %collective-permute-start.14 = (bf16[4,640,128]{2,1,0:T(8,128)(2,1)S(1)}, bf16[4,640,128]{2,1,0:T(8,128)(2,1)S(1)}, u32[]{:S(2)}, u32[]{:S(2)}) collective-permute-start(bf16[4,640,128]{2,1,0:T(8,128)(2,1)S(1)} %bitcast.393), channel_id=1, source_target_pairs={{0,2},{2,0},{4,6},{6,4},{8,10},{10,8},{12,14},{14,12},{1,3},{3,1},... | collective-permute-start | bytes 1966088 | tf_op jit(solution)/shard_map/ppermute | solution.py:30
  126.3 143.4 %all-gather.8.cloned.1.call-start = ((), (), s32[]{:S(2)}) async-start(), calls=%async_computation.4 | async-start | bytes 4456448 | tf_op jit(solution)/shard_map/all_gather | solution.py:773
  185.4 308.1 %reduce-scatter.3.cloned.1.call-start = ((), (), s32[]{:S(2)}) async-start(), calls=%async_computation.5 | async-start | bytes 4456448 | tf_op jit(solution)/shard_map/reduce_scatter | solution.py:817
  186.0 17.3 %collective-permute-start.11 = (bf16[144,768]{1,0:T(8,128)(2,1)S(1)}, bf16[144,768]{1,0:T(8,128)(2,1)S(1)}, u32[]{:S(2)}, u32[]{:S(2)}) collective-permute-start(bf16[144,768]{1,0:T(8,128)(2,1)S(1)} %copy-done.109), channel_id=1, source_target_pairs={{0,4},{2,6},{4,0},{6,2},{8,12},{10,14},{12,8},{14,10},{1,5},{3,7},... | collective-permute-start | bytes 663560 | tf_op jit(solution)/shard_map/ppermute | solution.py:30
  211.3 20.9 %collective-permute-start.16 = (bf16[144,768]{1,0:T(8,128)(2,1)S(1)}, bf16[144,768]{1,0:T(8,128)(2,1)S(1)}, u32[]{:S(2)}, u32[]{:S(2)}) collective-permute-start(bf16[144,768]{1,0:T(8,128)(2,1)S(1)} %maximum_add_fusion.7.rest_1_), channel_id=1, source_target_pairs={{0,8},{2,10},{4,12},{6,14},{8,0},{10,2},{12,4},{14,6},{1,9},{3,11}... | collective-permute-start | bytes 663560 | tf_op jit(solution)/shard_map/ppermute | solution.py:30
  245.1 50.9 %collective-permute-start.21 = (bf16[320,1024]{1,0:T(8,128)(2,1)}, bf16[320,1024]{1,0:T(8,128)(2,1)}, u32[]{:S(2)}, u32[]{:S(2)}) collective-permute-start(bf16[320,1024]{1,0:T(8,128)(2,1)} %bitcast.77), channel_id=1, source_target_pairs={{0,16},{16,0},{1,17},{17,1},{2,18},{18,2},{3,19},{19,3},{4,20},{20... | collective-permute-start | bytes 1966088 | tf_op jit(solution)/shard_map/ppermute | solution.py:30
  278.0 33.7 %collective-permute-start.24 = (bf16[320,4096]{1,0:T(8,128)(2,1)}, bf16[320,4096]{1,0:T(8,128)(2,1)}, u32[]{:S(2)}, u32[]{:S(2)}) collective-permute-start(bf16[320,4096]{1,0:T(8,128)(2,1)} %add_convert_fusion), channel_id=1, source_target_pairs={{0,16},{16,0},{1,17},{17,1},{2,18},{18,2},{3,19},{19,3},{4,20},{20... | collective-permute-start | bytes 7864328 | tf_op jit(solution)/shard_map/ppermute | solution.py:30
  319.9 217.4 %reduce-scatter.5.cloned.1.call-start = ((), (), s32[]{:S(2)}) async-start(), calls=%async_computation.6 | async-start | bytes 2228224 | tf_op jit(solution)/shard_map/reduce_scatter | solution.py:817
  323.0 192.3 %collective-permute-start.31 = (bf16[640,512]{1,0:T(8,128)(2,1)}, bf16[640,512]{1,0:T(8,128)(2,1)}, u32[]{:S(2)}, u32[]{:S(2)}) collective-permute-start(bf16[640,512]{1,0:T(8,128)(2,1)} %get-tuple-element.162), channel_id=1, source_target_pairs={{0,16},{16,0},{1,17},{17,1},{2,18},{18,2},{3,19},{19,3},{4,20},{20... | collective-permute-start | bytes 1966088 | tf_op jit(solution)/shard_map/ppermute | solution.py:30
  344.7 23.8 %collective-permute-start.25 = (bf16[8,64,1024]{2,1,0:T(8,128)(2,1)}, bf16[8,64,1024]{2,1,0:T(8,128)(2,1)}, u32[]{:S(2)}, u32[]{:S(2)}) collective-permute-start(bf16[8,64,1024]{2,1,0:T(8,128)(2,1)} %select_bitcast_fusion), channel_id=1, source_target_pairs={{0,16},{16,0},{1,17},{17,1},{2,18},{18,2},{3,19},{19,3},{4,20},{20... | collective-permute-start | bytes 3145736 | tf_op jit(solution)/shard_map/ppermute | solution.py:30
  370.5 29.6 %collective-permute-start.44 = (bf16[2,2,64,1024]{3,2,0,1:T(8,128)(2,1)S(1)}, bf16[2,2,64,1024]{3,2,0,1:T(8,128)(2,1)}, u32[]{:S(2)}, u32[]{:S(2)}) collective-permute-start(bf16[2,2,64,1024]{3,2,0,1:T(8,128)(2,1)S(1)} %select_bitcast_fusion.6), channel_id=1, source_target_pairs={{0,2},{2,0},{4,6},{6,4},{8,10},{10,8},{12,14},{14,12},{1,3},{3,1},... | collective-permute-start | bytes 1572872 | tf_op jit(solution)/shard_map/ppermute | solution.py:30
  387.0 21.0 %collective-permute-start.27 = (bf16[144,768]{1,0:T(8,128)(2,1)S(1)}, bf16[144,768]{1,0:T(8,128)(2,1)S(1)}, u32[]{:S(2)}, u32[]{:S(2)}) collective-permute-start(bf16[144,768]{1,0:T(8,128)(2,1)S(1)} %maximum_add_fusion.8.rest_3_), channel_id=1, source_target_pairs={{0,4},{2,6},{4,0},{6,2},{8,12},{10,14},{12,8},{14,10},{1,5},{3,7},... | collective-permute-start | bytes 663560 | tf_op jit(solution)/shard_map/ppermute | solution.py:30
  401.5 41.6 %collective-permute-start.45 = (bf16[2,64,1024]{2,1,0:T(8,128)(2,1)S(1)}, bf16[2,64,1024]{2,1,0:T(8,128)(2,1)S(1)}, u32[]{:S(2)}, u32[]{:S(2)}) collective-permute-start(bf16[2,64,1024]{2,1,0:T(8,128)(2,1)S(1)} %select_bitcast_fusion.15), channel_id=1, source_target_pairs={{0,4},{2,6},{4,0},{6,2},{8,12},{10,14},{12,8},{14,10},{1,5},{3,7},... | collective-permute-start | bytes 786440 | tf_op jit(solution)/shard_map/ppermute | solution.py:30
  408.6 46.9 %collective-permute-start.32 = (bf16[144,768]{1,0:T(8,128)(2,1)S(1)}, bf16[144,768]{1,0:T(8,128)(2,1)S(1)}, u32[]{:S(2)}, u32[]{:S(2)}) collective-permute-start(bf16[144,768]{1,0:T(8,128)(2,1)S(1)} %maximum_add_fusion.9.rest_0_), channel_id=1, source_target_pairs={{0,8},{2,10},{4,12},{6,14},{8,0},{10,2},{12,4},{14,6},{1,9},{3,11}... | collective-permute-start | bytes 663560 | tf_op jit(solution)/shard_map/ppermute | solution.py:30
  434.8 31.4 %collective-permute-start.28 = (bf16[2,2,640,128]{3,2,0,1:T(8,128)(2,1)S(1)}, bf16[2,2,640,128]{3,2,0,1:T(8,128)(2,1)S(1)}, u32[]{:S(2)}, u32[]{:S(2)}) collective-permute-start(bf16[2,2,640,128]{3,2,0,1:T(8,128)(2,1)S(1)} %select_bitcast_fusion.1), channel_id=1, source_target_pairs={{0,2},{2,0},{4,6},{6,4},{8,10},{10,8},{12,14},{14,12},{1,3},{3,1},... | collective-permute-start | bytes 1966088 | tf_op jit(solution)/shard_map/ppermute | solution.py:30
  443.9 55.2 %collective-permute-start.46 = (bf16[64,1024]{1,0:T(8,128)(2,1)}, bf16[64,1024]{1,0:T(8,128)(2,1)}, u32[]{:S(2)}, u32[]{:S(2)}) collective-permute-start(bf16[64,1024]{1,0:T(8,128)(2,1)} %select_bitcast_fusion.25), channel_id=1, source_target_pairs={{0,8},{2,10},{4,12},{6,14},{8,0},{10,2},{12,4},{14,6},{1,9},{3,11}... | collective-permute-start | bytes 393224 | tf_op jit(solution)/shard_map/ppermute | solution.py:30
  474.7 17.4 %collective-permute-start.29 = (bf16[2,640,128]{2,1,0:T(8,128)(2,1)S(1)}, bf16[2,640,128]{2,1,0:T(8,128)(2,1)S(1)}, u32[]{:S(2)}, u32[]{:S(2)}) collective-permute-start(bf16[2,640,128]{2,1,0:T(8,128)(2,1)S(1)} %select_bitcast_fusion.11), channel_id=1, source_target_pairs={{0,4},{2,6},{4,0},{6,2},{8,12},{10,14},{12,8},{14,10},{1,5},{3,7},... | collective-permute-start | bytes 983048 | tf_op jit(solution)/shard_map/ppermute | solution.py:30
  524.3 19.5 %collective-permute-start.35 = (bf16[640,1152]{1,0:T(8,128)(2,1)}, bf16[640,1152]{1,0:T(8,128)(2,1)}, u32[]{:S(2)}, u32[]{:S(2)}) collective-permute-start(bf16[640,1152]{1,0:T(8,128)(2,1)} %pad_maximum_fusion.2), channel_id=1, source_target_pairs={{0,16},{16,0},{1,17},{17,1},{2,18},{18,2},{3,19},{19,3},{4,20},{20... | collective-permute-start | bytes 4423688 | tf_op jit(solution)/shard_map/ppermute | solution.py:30
  548.1 18.2 %collective-permute-start.37 = (bf16[2,2,64,1152]{3,2,0,1:T(8,128)(2,1)S(1)}, bf16[2,2,64,1152]{3,2,0,1:T(8,128)(2,1)S(1)}, u32[]{:S(2)}, u32[]{:S(2)}) collective-permute-start(bf16[2,2,64,1152]{3,2,0,1:T(8,128)(2,1)S(1)} %select_bitcast_fusion.4), channel_id=1, source_target_pairs={{0,4},{2,6},{4,0},{6,2},{8,12},{10,14},{12,8},{14,10},{1,5},{3,7},... | collective-permute-start | bytes 1769480 | tf_op jit(solution)/shard_map/ppermute | solution.py:30
  554.1 18.0 %collective-permute-start.36 = (bf16[320,1024]{1,0:T(8,128)(2,1)S(1)}, bf16[320,1024]{1,0:T(8,128)(2,1)S(1)}, u32[]{:S(2)}, u32[]{:S(2)}) collective-permute-start(bf16[320,1024]{1,0:T(8,128)(2,1)S(1)} %select_convert_fusion), channel_id=1, source_target_pairs={{0,1},{1,0},{2,3},{3,2},{4,5},{5,4},{6,7},{7,6},{8,9},{9,8},{10,11... | collective-permute-start | bytes 1966088 | tf_op jit(solution)/shard_map/ppermute | solution.py:30
  556.8 17.4 %collective-permute-start.42 = (bf16[64,1152]{1,0:T(8,128)(2,1)S(1)}, bf16[64,1152]{1,0:T(8,128)(2,1)S(1)}, u32[]{:S(2)}, u32[]{:S(2)}) collective-permute-start(bf16[64,1152]{1,0:T(8,128)(2,1)S(1)} %select_bitcast_fusion.23), channel_id=1, source_target_pairs={{0,8},{2,10},{4,12},{6,14},{8,0},{10,2},{12,4},{14,6},{1,9},{3,11}... | collective-permute-start | bytes 442376 | tf_op jit(solution)/shard_map/ppermute | solution.py:30
  (226 other events, 2250.4 us)
Sparse Core Ops, SparseCore 0:
  59.1 63.0 all-gather.3
  126.4 78.4 all-gather.5
  207.7 55.0 all-gather.7
  320.1 104.2 reduce-scatter.2
  426.4 81.2 reduce-scatter.4
